TPU v7x, 32 devices: a whole 2x2x4 slice. The times are simulated.
32 devices in a mesh: dp: 16 (over z, y, core), rep: 2 (over x).
Axes of the slice: x: 2, y: 2, z: 4, core: 2. Of those that a mesh axis runs over, the one named last changes fastest.
Arguments:
- picture_vectors: bfloat16 [8192, 1152], P('dp'), may hold values from -1 to 1
- caption_vectors: bfloat16 [8192, 1152], P('dp'), may hold values from -1 to 1
- matched_caption_index: int32 [16, 512], P('dp'), may hold values from 0 to 511, as said below
- score_multiplier: float32 [], replicated, may hold values from 90 to 110
- score_offset: float32 [], replicated, may hold values from -10.5 to -9.5
- objective_cotangent: float32 [], replicated, may hold values from 0.1 to 0.3
Outputs:
- picture_vector_derivative: float32 [8192, 1152], P('dp')
- caption_vector_derivative: float32 [8192, 1152], P('dp')
Inputs may be any that keep to these rules, and one draw needn't show every extreme that they name: Each row matched_caption_index[p] is a permutation of 0 .. 511.
All inputs are finite; a program needn't handle non-finite values.
Results may differ from a plain program's by a relative error of at most 0.0045.
Values may be sent and summed in bfloat16 or wider, within the bound.
No kernel may reach another device: no remote copies, remote signals or barrier semaphores. Data moves between devices by JAX's collectives and lax.ppermute only.
A program may use at most 64 MiB of HBM per device.

v0:
```python
import jax
import jax.numpy as jnp
from jax import lax
from jax.sharding import PartitionSpec as P

STEPS = 8


def shifted(x, axis, by):
    devices = lax.axis_size(axis)
    return lax.ppermute(x, axis, [(i, (i + by) % devices) for i in range(devices)])


def per_device(
    picture_vectors,
    caption_vectors,
    matched_caption_index,
    score_multiplier,
    score_offset,
    objective_cotangent,
):
    rows = picture_vectors.shape[0]
    column = lax.broadcasted_iota(jnp.int32, (rows, rows), 1)
    match = (column == matched_caption_index.reshape(rows, 1)).astype(jnp.float32)
    replicas = lax.axis_size("rep")
    replica = lax.axis_index("rep")
    share = STEPS // replicas
    start_block = caption_vectors
    other = 1
    moved = shifted(caption_vectors, "dp", other * share)
    start_block = jnp.where(replica == other, moved, start_block)
    first_positive = jnp.where(replica == 0, 1.0, 0.0).astype(jnp.float32)
    text_block = start_block
    picture_derivative_piece = jnp.zeros(picture_vectors.shape, jnp.float32)
    caption_derivative_piece = jnp.zeros(text_block.shape, jnp.float32)
    for turn in range(share):
        if turn + 1 < share:
            following = shifted(text_block, "dp", 1)
        positive = first_positive if turn == 0 else 0.0
        block_picture_derivative_piece = picture_derivative_piece
        block_caption_derivative_piece = caption_derivative_piece
        inner_score_table = lax.dot_general(
            picture_vectors,
            text_block,
            (((1,), (1,)), ((), ())),
            preferred_element_type=jnp.float32,
        )
        couple_score_table = score_multiplier * inner_score_table + score_offset
        grads = (
            objective_cotangent * (jax.nn.sigmoid(couple_score_table) - positive * match)
        ).astype(jnp.bfloat16)
        block_picture_derivative_piece = block_picture_derivative_piece + jnp.dot(
            grads, text_block, preferred_element_type=jnp.float32
        )
        block_caption_derivative_piece = block_caption_derivative_piece + lax.dot_general(
            grads, picture_vectors, (((0,), (0,)), ((), ())), preferred_element_type=jnp.float32
        )
        picture_derivative_piece = block_picture_derivative_piece
        caption_derivative_piece = block_caption_derivative_piece
        if turn + 1 < share:
            caption_derivative_piece = shifted(caption_derivative_piece, "dp", 1)
            text_block = following
    picture_derivative_piece, caption_derivative_piece = (
        picture_derivative_piece,
        caption_derivative_piece,
    )
    caption_derivative_piece = shifted(caption_derivative_piece, "dp", -(share - 1))
    returned = caption_derivative_piece
    other = 1
    farther = shifted(caption_derivative_piece.astype(jnp.bfloat16), "dp", -(other * share)).astype(
        caption_derivative_piece.dtype
    )
    returned = jnp.where(replica == other, farther, returned)
    picture_derivative_piece, caption_derivative_piece = lax.psum(
        (picture_derivative_piece, returned), "rep"
    )
    return (
        score_multiplier * picture_derivative_piece,
        score_multiplier * caption_derivative_piece,
    )


def solution(mesh):
    placed = (P("dp", None), P("dp", None), P("dp", None), P(), P(), P())
    return jax.shard_map(
        per_device,
        mesh=mesh,
        in_specs=placed,
        out_specs=(P("dp", None), P("dp", None)),
        check_vma=False,
    )
```

profile of v0, /device:TPU:0, one launch (start us, length us, event | category | flops | bytes accessed | tf_op | source)
XLA Modules:
  0.0 384.5 jit_solution(13161698738183479239)
XLA Ops:
  7.2 0.0 copy-start
  7.2 0.0 all-reduce.3.cloned.1.call-start
  7.2 3.1 collective-permute-start
  12.3 0.0 copy-start.1
  12.3 26.2 %collective-permute-done = bf16[512,1152]{1,0:T(8,128)(2,1)S(1)} collective-permute-done((bf16[512,1152]{1,0:T(8,128)(2,1)}, bf16[512,1152]{1,0:T(8,128)(2,1)S(1)}, u32[]{:S(2)}, u32[]{:S(2)}) %collective-permute-start) | collective-permute-done | bytes 1179680 | tf_op jit(solution)/shard_map/ppermute | solution.py:11
  38.5 1.4 broadcast_select_fusion
  39.9 0.0 copy-done
  39.9 0.0 copy-done.1
  39.9 1.1 fusion.26
  41.1 0.9 fusion.31
  41.9 0.1 collective-permute-start.4
  42.0 1.6 collective-permute-start.1
  43.6 42.0 %collective-permute-done.1 = bf16[512,1152]{1,0:T(8,128)(2,1)S(1)} collective-permute-done((bf16[512,1152]{1,0:T(8,128)(2,1)S(1)}, bf16[512,1152]{1,0:T(8,128)(2,1)S(1)}, u32[]{:S(2)}, u32[]{:S(2)}) %collective-permute-start.1) | collective-permute-done | bytes 1179680 | tf_op jit(solution)/shard_map/ppermute | solution.py:11
  85.6 1.0 fusion.27
  86.6 0.0 collective-permute-done.4
  86.6 0.9 convolution_add_fusion
  87.5 0.1 collective-permute-start.5
  87.6 0.1 collective-permute-start.2
  87.6 43.5 %collective-permute-done.2 = bf16[512,1152]{1,0:T(8,128)(2,1)S(1)} collective-permute-done((bf16[512,1152]{1,0:T(8,128)(2,1)S(1)}, bf16[512,1152]{1,0:T(8,128)(2,1)S(1)}, u32[]{:S(2)}, u32[]{:S(2)}) %collective-permute-start.2) | collective-permute-done | bytes 1179680 | tf_op jit(solution)/shard_map/ppermute | solution.py:11
  131.2 1.0 fusion.28
  132.2 0.9 fusion.32
  133.1 0.0 collective-permute-done.5
  133.1 0.2 add.69
  133.4 0.1 collective-permute-start.6
  133.4 0.1 collective-permute-start.3
  133.5 44.1 %collective-permute-done.3 = bf16[512,1152]{1,0:T(8,128)(2,1)S(1)} collective-permute-done((bf16[512,1152]{1,0:T(8,128)(2,1)S(1)}, bf16[512,1152]{1,0:T(8,128)(2,1)S(1)}, u32[]{:S(2)}, u32[]{:S(2)}) %collective-permute-start.3) | collective-permute-done | bytes 1179680 | tf_op jit(solution)/shard_map/ppermute | solution.py:11
  177.6 1.0 fusion.29
  178.6 0.9 fusion.33
  179.5 0.0 collective-permute-done.6
  179.5 0.2 add.70
  179.7 0.1 collective-permute-start.7
  179.8 45.1 %collective-permute-done.7 = f32[512,1152]{1,0:T(8,128)S(1)} collective-permute-done((f32[512,1152]{1,0:T(8,128)S(1)}, f32[512,1152]{1,0:T(8,128)S(1)}, u32[]{:S(2)}, u32[]{:S(2)}) %collective-permute-start.7) | collective-permute-done | bytes 2359328 | tf_op jit(solution)/shard_map/ppermute | solution.py:11
  224.9 0.1 convert_element_type.23
  225.0 0.5 collective-permute-start.8
  225.5 0.8 fusion.30
  226.4 0.9 convolution_add_fusion.3
  227.3 0.9 convolution_add_fusion.2
  228.1 2.3 convolution_add_fusion.1
  230.4 23.1 %collective-permute-done.8 = bf16[512,1152]{1,0:T(8,128)(2,1)S(1)} collective-permute-done((bf16[512,1152]{1,0:T(8,128)(2,1)S(1)}, bf16[512,1152]{1,0:T(8,128)(2,1)S(1)}, u32[]{:S(2)}, u32[]{:S(2)}) %collective-permute-start.8) | collective-permute-done | bytes 1179680 | tf_op jit(solution)/shard_map/ppermute | solution.py:11
  253.5 1.7 convert_select_fusion
  255.2 0.0 all-reduce.3.cloned.1.call-update
  255.2 117.6 %all-reduce.3.cloned.1.call-done = (f32[512,1152]{1,0:T(8,128)}, f32[512,1152]{1,0:T(8,128)}) async-done(((f32[512,1152]{1,0:T(8,128)}, f32[512,1152]{1,0:T(8,128)}), (f32[512,1152]{1,0:T(8,128)}, f32[512,1152]{1,0:T(8,128)})) %all-reduce.3.cloned.1.call-update) | async-done | bytes 4718608 | tf_op jit(solution)/shard_map/psum | solution.py:74
  372.8 4.9 %broadcast_multiply_fusion = (f32[512,1152]{1,0:T(8,128)}, f32[512,1152]{1,0:T(8,128)}) fusion(f32[512,1152]{1,0:T(8,128)} %get-tuple-element.3, f32[]{:T(128)S(6)} %copy.21, f32[512,1152]{1,0:T(8,128)} %get-tuple-element.2), kind=kLoop, calls=%fused_computation.39 | loop fusion | flops 1179648 | bytes 9437188 | tf_op jit(solution)/shard_map/mul | solution.py:79
Async XLA Ops:
  7.2 32.8 %copy-start = (bf16[512,1152]{1,0:T(8,128)(2,1)S(1)}, bf16[512,1152]{1,0:T(8,128)(2,1)}, u32[]{:S(2)}) copy-start(bf16[512,1152]{1,0:T(8,128)(2,1)} %param.6) | copy-start | bytes 3538948
  7.2 365.6 %all-reduce.3.cloned.1.call-start = ((), (), s32[]{:S(2)}) async-start(), calls=%async_computation | async-start | bytes 9437184 | tf_op jit(solution)/shard_map/psum | solution.py:74
  7.2 31.3 %collective-permute-start = (bf16[512,1152]{1,0:T(8,128)(2,1)}, bf16[512,1152]{1,0:T(8,128)(2,1)S(1)}, u32[]{:S(2)}, u32[]{:S(2)}) collective-permute-start(bf16[512,1152]{1,0:T(8,128)(2,1)} %param.7), channel_id=1, source_target_pairs={{0,8},{2,10},{4,12},{6,14},{8,16},{10,18},{12,20},{14,22},{16,24},... | collective-permute-start | bytes 3538952 | tf_op jit(solution)/shard_map/ppermute | solution.py:11
  12.3 27.7 %copy-start.1 = (s32[1,512]{1,0:T(1,128)S(1)}, s32[1,512]{1,0:T(1,128)}, u32[]{:S(2)}) copy-start(s32[1,512]{1,0:T(1,128)} %param.8) | copy-start | bytes 6148
  41.9 44.7 %collective-permute-start.4 = (f32[512,1152]{1,0:T(8,128)S(1)}, f32[512,1152]{1,0:T(8,128)S(1)}, u32[]{:S(2)}, u32[]{:S(2)}) collective-permute-start(f32[512,1152]{1,0:T(8,128)S(1)} %fusion.31), channel_id=1, source_target_pairs={{0,2},{2,4},{4,6},{6,8},{8,10},{10,12},{12,14},{14,16},{16,18},{18... | collective-permute-start | bytes 7077896 | tf_op jit(solution)/shard_map/ppermute | solution.py:11
  42.0 43.6 %collective-permute-start.1 = (bf16[512,1152]{1,0:T(8,128)(2,1)S(1)}, bf16[512,1152]{1,0:T(8,128)(2,1)S(1)}, u32[]{:S(2)}, u32[]{:S(2)}) collective-permute-start(bf16[512,1152]{1,0:T(8,128)(2,1)S(1)} %broadcast_select_fusion), channel_id=1, source_target_pairs={{0,2},{2,4},{4,6},{6,8},{8,10},{10,12},{12,14},{14,16},{16,18},{18... | collective-permute-start | bytes 3538952 | tf_op jit(solution)/shard_map/ppermute | solution.py:11
  87.5 45.6 %collective-permute-start.5 = (f32[512,1152]{1,0:T(8,128)S(1)}, f32[512,1152]{1,0:T(8,128)S(1)}, u32[]{:S(2)}, u32[]{:S(2)}) collective-permute-start(f32[512,1152]{1,0:T(8,128)S(1)} %convolution_add_fusion), channel_id=1, source_target_pairs={{0,2},{2,4},{4,6},{6,8},{8,10},{10,12},{12,14},{14,16},{16,18},{18... | collective-permute-start | bytes 7077896 | tf_op jit(solution)/shard_map/ppermute | solution.py:11
  87.6 43.6 %collective-permute-start.2 = (bf16[512,1152]{1,0:T(8,128)(2,1)S(1)}, bf16[512,1152]{1,0:T(8,128)(2,1)S(1)}, u32[]{:S(2)}, u32[]{:S(2)}) collective-permute-start(bf16[512,1152]{1,0:T(8,128)(2,1)S(1)} %collective-permute-done.1), channel_id=1, source_target_pairs={{0,2},{2,4},{4,6},{6,8},{8,10},{10,12},{12,14},{14,16},{16,18},{18... | collective-permute-start | bytes 3538952 | tf_op jit(solution)/shard_map/ppermute | solution.py:11
  133.4 46.1 %collective-permute-start.6 = (f32[512,1152]{1,0:T(8,128)S(1)}, f32[512,1152]{1,0:T(8,128)S(1)}, u32[]{:S(2)}, u32[]{:S(2)}) collective-permute-start(f32[512,1152]{1,0:T(8,128)S(1)} %add.69), channel_id=1, source_target_pairs={{0,2},{2,4},{4,6},{6,8},{8,10},{10,12},{12,14},{14,16},{16,18},{18... | collective-permute-start | bytes 7077896 | tf_op jit(solution)/shard_map/ppermute | solution.py:11
  133.4 44.1 %collective-permute-start.3 = (bf16[512,1152]{1,0:T(8,128)(2,1)S(1)}, bf16[512,1152]{1,0:T(8,128)(2,1)S(1)}, u32[]{:S(2)}, u32[]{:S(2)}) collective-permute-start(bf16[512,1152]{1,0:T(8,128)(2,1)S(1)} %collective-permute-done.2), channel_id=1, source_target_pairs={{0,2},{2,4},{4,6},{6,8},{8,10},{10,12},{12,14},{14,16},{16,18},{18... | collective-permute-start | bytes 3538952 | tf_op jit(solution)/shard_map/ppermute | solution.py:11
  179.7 45.2 %collective-permute-start.7 = (f32[512,1152]{1,0:T(8,128)S(1)}, f32[512,1152]{1,0:T(8,128)S(1)}, u32[]{:S(2)}, u32[]{:S(2)}) collective-permute-start(f32[512,1152]{1,0:T(8,128)S(1)} %add.70), channel_id=1, source_target_pairs={{0,26},{2,28},{4,30},{6,0},{8,2},{10,4},{12,6},{14,8},{16,10},{18,... | collective-permute-start | bytes 7077896 | tf_op jit(solution)/shard_map/ppermute | solution.py:11
  225.0 28.5 %collective-permute-start.8 = (bf16[512,1152]{1,0:T(8,128)(2,1)S(1)}, bf16[512,1152]{1,0:T(8,128)(2,1)S(1)}, u32[]{:S(2)}, u32[]{:S(2)}) collective-permute-start(bf16[512,1152]{1,0:T(8,128)(2,1)S(1)} %convert_element_type.23), channel_id=1, source_target_pairs={{0,24},{2,26},{4,28},{6,30},{8,0},{10,2},{12,4},{14,6},{16,8},{18,... | collective-permute-start | bytes 3538952 | tf_op jit(solution)/shard_map/ppermute | solution.py:11
Sparse Core Ops, SparseCore 0:
  255.3 117.4 all-reduce.2
where the time goes:
time: 385 us
  waiting for transfers between devices  342 us (89%)
  between operations  16.2 us (4%)
  matrix products  12.5 us (3%)
  other arithmetic  8.55 us (2%)
  starting transfers between devices  5.58 us (1%)
    ppermute x9, waiting for transfers between devices, shifted(): lax.ppermute(x, axis, [(i, (i + by) % devices) for i in range(devices)])  224 us
    psum x1, waiting for transfers between devices, per_device(): lax.psum((picture_derivative_piece, returned), 'rep')  118 us
  transfers between devices with their start and end apart: 10, of which 7 were waited for; matrix products, arithmetic and copies ran while one was open for 3% of the time, Pallas kernels for 0%

commit v1 on v0

v1 whole, which is shorter than its diff:
```python
import jax
import jax.numpy as jnp
from jax import lax
from jax.experimental import pallas as pl
from jax.experimental.pallas import tpu as pltpu
from jax.sharding import PartitionSpec as P

GROUP = 4
CHUNKS = 2
VMEM_BYTES = 40 * 1024 * 1024

FIRST, CORE, SIDE = 0, 1, 2


def hop(x, pairs):
    return lax.ppermute(x, ("dp", "rep"), pairs)


def pairs_of(devices, target, members):
    pairs = []
    for p in range(devices):
        if p % GROUP in members:
            q = target(p)
            pairs.append((2 * p, 2 * q))
            pairs.append((2 * (devices - 1 - p) + 1, 2 * (devices - 1 - q) + 1))
    return pairs


def grads_of(scale_ref, left, block, match=None):
    product = lax.dot_general(
        left, block, (((1,), (1,)), ((), ())), preferred_element_type=jnp.float32
    )
    value = jax.nn.sigmoid(scale_ref[0] * product + scale_ref[1])
    if match is not None:
        value = value - match
    return (scale_ref[2] * value).astype(jnp.bfloat16)


def add_blocks(scale_ref, left_ref, refs, out_ref, match=None):
    left = left_ref[...]
    blocks = [ref[...] for ref in refs]
    grads = [grads_of(scale_ref, left, block, match) for block in blocks]
    if len(refs) > 1:
        blocks, grads = [jnp.concatenate(blocks, axis=0)], [jnp.concatenate(grads, axis=1)]
    out_ref[...] += jnp.dot(grads[0], blocks[0], preferred_element_type=jnp.float32)


def first_kernel(
    flag_ref, scale_ref, down_ref, along_ref, left_ref, own_ref, one_ref, out_ref
):
    own_rows = pl.program_id(0) == 0
    out_ref[...] = jnp.zeros_like(out_ref)

    @pl.when(own_rows)
    def _():
        shape = (left_ref.shape[0], own_ref.shape[0])
        column = lax.broadcasted_iota(jnp.int32, shape, 1)
        row = lax.broadcasted_iota(jnp.int32, shape, 0)
        straight = (column == down_ref[...]).astype(jnp.float32)
        turned = (row == along_ref[...]).astype(jnp.float32)
        match = jnp.where(flag_ref[FIRST] == 1, straight, turned)
        add_blocks(scale_ref, left_ref, [own_ref], out_ref, match)

    @pl.when(jnp.logical_and(jnp.logical_not(own_rows), flag_ref[CORE] == 0))
    def _():
        add_blocks(scale_ref, left_ref, [own_ref], out_ref)

    add_blocks(scale_ref, left_ref, [one_ref], out_ref)


def second_kernel(flag_ref, scale_ref, left_ref, sum_ref, one_ref, over_ref, out_ref):
    out_ref[...] = sum_ref[...]
    add_blocks(scale_ref, left_ref, [one_ref], out_ref)

    @pl.when(flag_ref[SIDE] == 1)
    def _():
        add_blocks(scale_ref, left_ref, [over_ref], out_ref)


def third_kernel(flag_ref, scale_ref, left_ref, sum_ref, *rest):
    two, over, last, out_ref = rest[:CHUNKS], rest[CHUNKS:-2], rest[-2], rest[-1]
    other_rows = pl.program_id(0) == 1
    out_ref[...] = sum_ref[...]

    @pl.when(jnp.logical_or(other_rows, flag_ref[CORE] == 0))
    def _():
        add_blocks(scale_ref, left_ref, two, out_ref)

    @pl.when(flag_ref[CORE] == 1)
    def _():
        add_blocks(scale_ref, left_ref, over, out_ref)

    @pl.when(flag_ref[SIDE] == 0)
    def _():
        add_blocks(scale_ref, left_ref, [last], out_ref)


def last_kernel(flag_ref, scale_ref, left_ref, sum_ref, last_ref, out_ref, total_ref):
    total_ref[...] = sum_ref[...]

    @pl.when(flag_ref[SIDE] == 0)
    def _():
        add_blocks(scale_ref, left_ref, [last_ref], total_ref)

    out_ref[...] = total_ref[...].astype(out_ref.dtype)


def whole(x):
    return pl.BlockSpec(x.shape, lambda i: (0,) * x.ndim)


def params():
    return pltpu.CompilerParams(
        dimension_semantics=("arbitrary",), vmem_limit_bytes=VMEM_BYTES
    )


def cost(pairs, rows, depth):
    return pl.CostEstimate(
        flops=int(4 * pairs * rows * rows * depth),
        bytes_accessed=int(8 * rows * depth),
        transcendentals=int(pairs * rows * rows),
    )


SMEM = pl.BlockSpec(memory_space=pltpu.SMEM)


def per_device(
    picture_vectors,
    caption_vectors,
    matched_caption_index,
    score_multiplier,
    score_offset,
    objective_cotangent,
):
    rows, depth = picture_vectors.shape
    devices = lax.axis_size("dp")
    first = lax.axis_index("rep") == 0
    place = lax.axis_index("dp")
    place = jnp.where(first, place, devices - 1 - place)
    flags = jnp.stack([first.astype(jnp.int32), place & 1, (place >> 1) & 1])
    scale = jnp.stack([score_multiplier, score_offset, objective_cotangent])

    def up(p):
        return (p + GROUP) % devices

    def across(p):
        return p ^ 2

    def swapped(p):
        return p ^ 1

    to_up = pairs_of(devices, up, (0, 1, 2, 3))
    to_side_1 = pairs_of(devices, across, (0, 1))
    core_1_across = pairs_of(devices, across, (1, 3))
    onward = pairs_of(devices, up, (1, 3)) + pairs_of(devices, across, (0, 2))
    last_step = pairs_of(devices, up, (0,)) + pairs_of(devices, across, (3,))
    core_swap = pairs_of(devices, swapped, (0, 1, 2, 3))
    replica_swap = [(2 * p + r, 2 * p + 1 - r) for p in range(devices) for r in range(2)]

    moving = jnp.where(first, caption_vectors, picture_vectors)
    fixed = jnp.where(first, picture_vectors, caption_vectors)
    size = rows // CHUNKS
    own = [moving[k * size : (k + 1) * size] for k in range(CHUNKS)]

    tile = pl.BlockSpec((rows, depth), lambda i: (i, 0))
    down = matched_caption_index.reshape(rows, 1)
    sums = jax.ShapeDtypeStruct((2 * rows, depth), jnp.float32)

    def kernel(body, name, pairs, operands, specs):
        return pl.pallas_call(
            body,
            grid=(2,),
            out_shape=sums,
            in_specs=[SMEM, SMEM] + specs,
            out_specs=tile,
            compiler_params=params(),
            cost_estimate=cost(pairs, rows, depth),
            name=name,
        )(flags, scale, *operands)

    one = [hop(x, to_up) for x in own]
    other_fixed = hop(fixed, core_swap)
    from_0 = hop(moving, to_side_1)
    both = jnp.concatenate([fixed, other_fixed], axis=0)
    two_a = hop(one[0], onward)
    over_a = hop(one[0], core_1_across)
    total = kernel(
        first_kernel,
        "first_blocks",
        3,
        (down, matched_caption_index, both, moving, one[0]),
        [whole(down), whole(matched_caption_index), tile, whole(moving), whole(one[0])],
    )
    one_b, total = lax.optimization_barrier((one[1], total))
    two_b = hop(one_b, onward)
    over_b = hop(one_b, core_1_across)
    total = kernel(
        second_kernel,
        "second_blocks",
        3,
        (both, total, one_b, from_0),
        [tile, tile, whole(one_b), whole(from_0)],
    )
    last_a = hop(two_a, last_step)
    two_b, total = lax.optimization_barrier((two_b, total))
    last_b = hop(two_b, last_step)
    blocks = [two_a, two_b, over_a, over_b, last_a]
    total = kernel(
        third_kernel,
        "third_blocks",
        4,
        (both, total, *blocks),
        [tile, tile] + [whole(x) for x in blocks],
    )

    def finish(which, dtype, name):
        part = pl.BlockSpec((rows, depth), lambda i: (which, 0))
        return pl.pallas_call(
            last_kernel,
            grid=(1,),
            out_shape=jax.ShapeDtypeStruct((rows, depth), dtype),
            in_specs=[SMEM, SMEM, part, part, whole(last_b)],
            out_specs=tile,
            scratch_shapes=[pltpu.VMEM((rows, depth), jnp.float32)],
            compiler_params=params(),
            cost_estimate=cost(0.5, rows, depth),
            name=name,
        )(flags, scale, both, total, last_b)

    other_total = finish(1, jnp.bfloat16, "last_block_other")
    received = hop(other_total, core_swap)
    own_total = finish(0, jnp.float32, "last_block_own")

    mine = (score_multiplier * (own_total + received.astype(jnp.float32))).astype(jnp.bfloat16)
    theirs = hop(mine, replica_swap)
    return (
        jnp.where(first, mine, theirs).astype(jnp.float32),
        jnp.where(first, theirs, mine).astype(jnp.float32),
    )


def solution(mesh):
    placed = (P("dp", None), P("dp", None), P("dp", None), P(), P(), P())
    return jax.shard_map(
        per_device,
        mesh=mesh,
        in_specs=placed,
        out_specs=(P("dp", None), P("dp", None)),
        check_vma=False,
    )
```

time: 385 us -> 112 us (0.29)
  waiting for transfers between devices: 342 us -> 48.4 us
  Pallas kernels: 0 us -> 24.9 us
  starting transfers between devices: 5.58 us -> 24.5 us
  between operations: 16.2 us -> 2.74 us
  matrix products: 12.5 us -> 0 us
    ppermute x9 -> x12, waiting for transfers between devices: 224 us -> 48.4 us  [hop(): return lax.ppermute(x, ('dp', 'rep'), pairs)]
    psum x1 -> x0, waiting for transfers between devices: 118 us -> none  [per_device(): lax.psum((picture_derivative_piece, returned), 'rep')]
    pallas_call x0 -> x5, Pallas kernels: none -> 24.9 us  [the longest x3 20 us: kernel(): pl.pallas_call(body, grid=(2,), out_shape=sums, in_specs=[SMEM, SMEM] + s...]
    ppermute x9 -> x12, starting transfers between devices: 5.54 us -> 24.5 us  [hop(): return lax.ppermute(x, ('dp', 'rep'), pairs)]
    dot_general x12 -> x0, matrix products: 12.5 us -> none  [the longest x4 4.84 us: per_device(): jnp.dot(grads, text_block, preferred_element_type=jnp.float32)]
    mul x1 -> x0, other arithmetic: 4.86 us -> none  [per_device(): score_multiplier * caption_derivative_piece]
  transfers between devices with their start and end apart: 10 -> 12, of which waited for: 7 -> 7; matrix products, arithmetic and copies ran while one was open for 3% -> 3% of each run, Pallas kernels for 0% -> 20%
where the time goes in v1:
time: 112 us
  waiting for transfers between devices  48.4 us (43%)
  Pallas kernels  24.9 us (22%)
  starting transfers between devices  24.5 us (22%)
  other arithmetic  7.6 us (7%)
  local copies, waits for them, and re-layouts  3.38 us (3%)
  between operations  2.74 us (2%)
    ppermute x12, waiting for transfers between devices, hop(): return lax.ppermute(x, ('dp', 'rep'), pairs)  48.4 us
    ppermute x12, starting transfers between devices, hop(): return lax.ppermute(x, ('dp', 'rep'), pairs)  24.5 us
    pallas_call x3, Pallas kernels, kernel(): pl.pallas_call(body, grid=(2,), out_shape=sums, in_specs=[SMEM, SMEM] + s...  20 us
    pallas_call x2, Pallas kernels, finish(): pl.pallas_call(last_kernel, grid=(1,), out_shape=jax.ShapeDtypeStruct((ro...  4.91 us
    select_n x1, other arithmetic, per_device(): moving = jnp.where(first, caption_vectors, picture_vectors)  2.86 us
    convert_element_type x1, other arithmetic, per_device(): jnp.where(first, theirs, mine).astype(jnp.float32)  2.49 us
  transfers between devices with their start and end apart: 12, of which 7 were waited for; matrix products, arithmetic and copies ran while one was open for 3% of the time, Pallas kernels for 20%

profile of v1, /device:TPU:0, one launch (start us, length us, event | category | flops | bytes accessed | tf_op | source)
XLA Modules:
  0.0 111.5 jit_solution(3911529319881010194)
XLA Ops:
  0.6 2.9 %broadcast_select_fusion = (bf16[512,1152]{1,0:T(8,128)(2,1)S(1)}, bf16[512,1152]{1,0:T(8,128)(2,1)}) fusion(bf16[512,1152]{1,0:T(8,128)(2,1)} %param.7, bf16[512,1152]{1,0:T(8,128)(2,1)} %param.6, pred[]{:T(512)S(6)} %eq.3), kind=kLoop, calls=%fused_computation.4 | loop fusion | flops 1179648 | bytes 4718593 | tf_op jit(solution)/shard_map/jit(_where)/select_n | solution.py:162
  3.5 0.5 collective-permute-start
  3.9 0.0 copy-start.1
  3.9 1.1 fusion
  5.1 2.6 %collective-permute-start.2 = (bf16[256,1152]{1,0:T(8,128)(2,1)}, bf16[256,1152]{1,0:T(8,128)(2,1)}, u32[]{:S(2)}, u32[]{:S(2)}) collective-permute-start(bf16[256,1152]{1,0:T(8,128)(2,1)} %get-tuple-element.14), channel_id=1, source_target_pairs={{0,8},{31,23},{2,10},{29,21},{4,12},{27,19},{6,14},{25,17},{8,16},... | collective-permute-start | bytes 1769480 | tf_op jit(solution)/shard_map/ppermute | solution.py:16
  7.6 3.5 %collective-permute-start.4 = (bf16[512,1152]{1,0:T(8,128)(2,1)S(1)}, bf16[512,1152]{1,0:T(8,128)(2,1)S(1)}, u32[]{:S(2)}, u32[]{:S(2)}) collective-permute-start(bf16[512,1152]{1,0:T(8,128)(2,1)S(1)} %get-tuple-element.12.own_ref), channel_id=1, source_target_pairs={{0,4},{31,27},{2,6},{29,25},{8,12},{23,19},{10,14},{21,17},{16,20}... | collective-permute-start | bytes 3538952 | tf_op jit(solution)/shard_map/ppermute | solution.py:16
  11.1 1.6 %collective-permute-start.1 = (bf16[256,1152]{1,0:T(8,128)(2,1)}, bf16[256,1152]{1,0:T(8,128)(2,1)S(1)}, u32[]{:S(2)}, u32[]{:S(2)}) collective-permute-start(bf16[256,1152]{1,0:T(8,128)(2,1)} %get-tuple-element.15), channel_id=1, source_target_pairs={{0,8},{31,23},{2,10},{29,21},{4,12},{27,19},{6,14},{25,17},{8,16},... | collective-permute-start | bytes 1769480 | tf_op jit(solution)/shard_map/ppermute | solution.py:16
  14.7 0.0 copy-done.1
  14.7 0.1 copy.8.down_ref
  14.9 0.1 pad_add_fusion.flag_ref
  14.9 0.1 pad_maximum_fusion.1.scale_ref
  15.0 9.1 %collective-permute-done.2.one_ref = bf16[256,1152]{1,0:T(8,128)(2,1)} collective-permute-done((bf16[256,1152]{1,0:T(8,128)(2,1)}, bf16[256,1152]{1,0:T(8,128)(2,1)}, u32[]{:S(2)}, u32[]{:S(2)}) %collective-permute-start.2) | collective-permute-done | bytes 589856 | tf_op jit(solution)/shard_map/ppermute | solution.py:16
  24.2 1.7 %collective-permute-start.5 = (bf16[256,1152]{1,0:T(8,128)(2,1)}, bf16[256,1152]{1,0:T(8,128)(2,1)S(1)}, u32[]{:S(2)}, u32[]{:S(2)}) collective-permute-start(bf16[256,1152]{1,0:T(8,128)(2,1)} %collective-permute-done.2.one_ref), channel_id=1, source_target_pairs={{2,10},{29,21},{6,14},{25,17},{10,18},{21,13},{14,22},{17,9},{18,2... | collective-permute-start | bytes 1769480 | tf_op jit(solution)/shard_map/ppermute | solution.py:16
  25.8 0.0 collective-permute-done
  25.8 1.8 %pad_maximum_fusion.left_ref = bf16[1024,1152]{1,0:T(8,128)(2,1)S(1)} fusion(bf16[512,1152]{1,0:T(8,128)(2,1)} %collective-permute-done, bf16[512,1152]{1,0:T(8,128)(2,1)} %get-tuple-element.13), kind=kLoop, calls=%fused_computation | loop fusion | flops 4718592 | bytes 4718592 | tf_op jit(solution)/shard_map/concatenate | solution.py:186
  27.6 7.9 %first_blocks.1.sum_ref = f32[1024,1152]{1,0:T(8,128)S(1)} custom-call(s32[3]{0:T(128)S(1)} %pad_add_fusion.flag_ref, f32[3]{0:T(128)S(1)} %pad_maximum_fusion.1.scale_ref, s32[512,1]{1,0:T(8,128)S(1)} %copy.8.down_ref, s32[1,512]{1,0:T(1,128)S(1)} %copy-done.1, bf16[1024,1152]{1,0:T(8,128)(2,1)S(1)} %pad_maximum_fusion.left_ref, ...), custom_call_target="tpu_custom_call" | custom-call | flops 3623878656 | bytes 4718592 | tf_op jit(solution)/shard_map/first_blocks/pallas_call | solution.py:172
  35.5 1.2 %collective-permute-done.1.one_ref = bf16[256,1152]{1,0:T(8,128)(2,1)S(1)} collective-permute-done((bf16[256,1152]{1,0:T(8,128)(2,1)}, bf16[256,1152]{1,0:T(8,128)(2,1)S(1)}, u32[]{:S(2)}, u32[]{:S(2)}) %collective-permute-start.1) | collective-permute-done | bytes 589856 | tf_op jit(solution)/shard_map/ppermute | solution.py:16
  36.7 1.7 %collective-permute-start.3 = (bf16[256,1152]{1,0:T(8,128)(2,1)S(1)}, bf16[256,1152]{1,0:T(8,128)(2,1)S(1)}, u32[]{:S(2)}, u32[]{:S(2)}) collective-permute-start(bf16[256,1152]{1,0:T(8,128)(2,1)S(1)} %collective-permute-done.1.one_ref), channel_id=1, source_target_pairs={{2,10},{29,21},{6,14},{25,17},{10,18},{21,13},{14,22},{17,9},{18,2... | collective-permute-start | bytes 1769480 | tf_op jit(solution)/shard_map/ppermute | solution.py:16
  38.3 0.7 collective-permute-start.6
  39.0 0.7 collective-permute-start.7
  39.7 6.2 %collective-permute-done.5.rest_0_ = bf16[256,1152]{1,0:T(8,128)(2,1)S(1)} collective-permute-done((bf16[256,1152]{1,0:T(8,128)(2,1)}, bf16[256,1152]{1,0:T(8,128)(2,1)S(1)}, u32[]{:S(2)}, u32[]{:S(2)}) %collective-permute-start.5) | collective-permute-done | bytes 589856 | tf_op jit(solution)/shard_map/ppermute | solution.py:16
  46.0 4.1 %collective-permute-start.8 = (bf16[256,1152]{1,0:T(8,128)(2,1)S(1)}, bf16[256,1152]{1,0:T(8,128)(2,1)S(1)}, u32[]{:S(2)}, u32[]{:S(2)}) collective-permute-start(bf16[256,1152]{1,0:T(8,128)(2,1)S(1)} %collective-permute-done.5.rest_0_), channel_id=1, source_target_pairs={{0,8},{31,23},{8,16},{23,15},{16,24},{15,7},{24,0},{7,31},{6,2},{2... | collective-permute-start | bytes 1769480 | tf_op jit(solution)/shard_map/ppermute | solution.py:16
  50.1 0.0 collective-permute-done.4.over_ref
  50.1 3.7 %second_blocks.1.sum_ref = f32[1024,1152]{1,0:T(8,128)S(1)} custom-call(s32[3]{0:T(128)S(1)} %pad_add_fusion.flag_ref, f32[3]{0:T(128)S(1)} %pad_maximum_fusion.1.scale_ref, bf16[1024,1152]{1,0:T(8,128)(2,1)S(1)} %pad_maximum_fusion.left_ref, f32[1024,1152]{1,0:T(8,128)S(1)} %first_blocks.1.sum_ref, bf16[256,1152]{1,0:T(8,128)(2,1)S(1)} %collective-permute-done.1.one_ref, ...), custom_call_target="tpu_custom_call" | custom-call | flops 3623878656 | bytes 4718592 | tf_op jit(solution)/shard_map/second_blocks/pallas_call | solution.py:172
  53.8 0.0 copy-start
  53.8 2.1 %copy-done = f32[1024,1152]{1,0:T(8,128)} copy-done((f32[1024,1152]{1,0:T(8,128)}, f32[1024,1152]{1,0:T(8,128)S(1)}, u32[]{:S(2)}) %copy-start) | copy-done | bytes 4718616
  55.9 2.6 %collective-permute-done.3.rest_1_ = bf16[256,1152]{1,0:T(8,128)(2,1)S(1)} collective-permute-done((bf16[256,1152]{1,0:T(8,128)(2,1)S(1)}, bf16[256,1152]{1,0:T(8,128)(2,1)S(1)}, u32[]{:S(2)}, u32[]{:S(2)}) %collective-permute-start.3) | collective-permute-done | bytes 589856 | tf_op jit(solution)/shard_map/ppermute | solution.py:16
  58.5 4.1 %collective-permute-start.9 = (bf16[256,1152]{1,0:T(8,128)(2,1)S(1)}, bf16[256,1152]{1,0:T(8,128)(2,1)S(1)}, u32[]{:S(2)}, u32[]{:S(2)}) collective-permute-start(bf16[256,1152]{1,0:T(8,128)(2,1)S(1)} %collective-permute-done.3.rest_1_), channel_id=1, source_target_pairs={{0,8},{31,23},{8,16},{23,15},{16,24},{15,7},{24,0},{7,31},{6,2},{2... | collective-permute-start | bytes 1769480 | tf_op jit(solution)/shard_map/ppermute | solution.py:16
  62.6 0.0 collective-permute-done.6.rest_2_
  62.6 0.0 collective-permute-done.7.rest_3_
  62.6 0.0 collective-permute-done.8.rest_4_
  62.6 8.4 %third_blocks.1.sum_ref = f32[1024,1152]{1,0:T(8,128)S(1)} custom-call(s32[3]{0:T(128)S(1)} %pad_add_fusion.flag_ref, f32[3]{0:T(128)S(1)} %pad_maximum_fusion.1.scale_ref, bf16[1024,1152]{1,0:T(8,128)(2,1)S(1)} %pad_maximum_fusion.left_ref, f32[1024,1152]{1,0:T(8,128)} %copy-done, bf16[256,1152]{1,0:T(8,128)(2,1)S(1)} %collective-permute-done.5.rest_0_, ...), custom_call_target="tpu_custom_call" | custom-call | flops 4831838208 | bytes 4718592 | tf_op jit(solution)/shard_map/third_blocks/pallas_call | solution.py:172
  71.1 1.0 collective-permute-done.9.last_ref
  72.1 2.5 %last_block_other.1 = bf16[512,1152]{1,0:T(8,128)(2,1)S(1)} custom-call(s32[3]{0:T(128)S(1)} %pad_add_fusion.flag_ref, f32[3]{0:T(128)S(1)} %pad_maximum_fusion.1.scale_ref, bf16[1024,1152]{1,0:T(8,128)(2,1)S(1)} %pad_maximum_fusion.left_ref, f32[1024,1152]{1,0:T(8,128)S(1)} %third_blocks.1.sum_ref, bf16[256,1152]{1,0:T(8,128)(2,1)S(1)} %collective-permute-done.9.last_ref), custom_call_target="tpu_custom_call" | custom-call | flops 603979776 | bytes 4718592 | tf_op jit(solution)/shard_map/last_block_other/pallas_call | solution.py:220
  74.6 3.4 %collective-permute-start.10 = (bf16[512,1152]{1,0:T(8,128)(2,1)S(1)}, bf16[512,1152]{1,0:T(8,128)(2,1)S(1)}, u32[]{:S(2)}, u32[]{:S(2)}) collective-permute-start(bf16[512,1152]{1,0:T(8,128)(2,1)S(1)} %last_block_other.1), channel_id=1, source_target_pairs={{0,2},{31,29},{2,0},{29,31},{4,6},{27,25},{6,4},{25,27},{8,10},{23... | collective-permute-start | bytes 3538952 | tf_op jit(solution)/shard_map/ppermute | solution.py:16
  78.0 2.4 %last_block_own.1 = f32[512,1152]{1,0:T(8,128)S(1)} custom-call(s32[3]{0:T(128)S(1)} %pad_add_fusion.flag_ref, f32[3]{0:T(128)S(1)} %pad_maximum_fusion.1.scale_ref, bf16[1024,1152]{1,0:T(8,128)(2,1)S(1)} %pad_maximum_fusion.left_ref, f32[1024,1152]{1,0:T(8,128)S(1)} %third_blocks.1.sum_ref, bf16[256,1152]{1,0:T(8,128)(2,1)S(1)} %collective-permute-done.9.last_ref), custom_call_target="tpu_custom_call" | custom-call | flops 603979776 | bytes 4718592 | tf_op jit(solution)/shard_map/last_block_own/pallas_call | solution.py:220
  80.4 0.1 collective-permute-done.10
  80.4 0.3 multiply_convert_fusion
  80.7 0.1 collective-permute-start.11
  80.8 28.2 %collective-permute-done.11 = bf16[512,1152]{1,0:T(8,128)(2,1)S(1)} collective-permute-done((bf16[512,1152]{1,0:T(8,128)(2,1)S(1)}, bf16[512,1152]{1,0:T(8,128)(2,1)S(1)}, u32[]{:S(2)}, u32[]{:S(2)}) %collective-permute-start.11) | collective-permute-done | bytes 1179680 | tf_op jit(solution)/shard_map/ppermute | solution.py:16
  109.1 2.5 %select_convert_fusion = (f32[512,1152]{1,0:T(8,128)}, f32[512,1152]{1,0:T(8,128)}) fusion(bf16[512,1152]{1,0:T(8,128)(2,1)S(1)} %collective-permute-done.11, bf16[512,1152]{1,0:T(8,128)(2,1)S(1)} %multiply_convert_fusion, pred[]{:T(512)S(6)} %eq.3), kind=kLoop, calls=%fused_computation.2 | loop fusion | flops 2359296 | bytes 7077889 | tf_op jit(solution)/shard_map/convert_element_type | solution.py:240
Async XLA Ops:
  3.5 22.3 %collective-permute-start = (bf16[512,1152]{1,0:T(8,128)(2,1)}, bf16[512,1152]{1,0:T(8,128)(2,1)}, u32[]{:S(2)}, u32[]{:S(2)}) collective-permute-start(bf16[512,1152]{1,0:T(8,128)(2,1)} %get-tuple-element.13), channel_id=1, source_target_pairs={{0,2},{31,29},{2,0},{29,31},{4,6},{27,25},{6,4},{25,27},{8,10},{23... | collective-permute-start | bytes 3538952 | tf_op jit(solution)/shard_map/ppermute | solution.py:16
  3.9 10.8 %copy-start.1 = (s32[1,512]{1,0:T(1,128)S(1)}, s32[1,512]{1,0:T(1,128)}, u32[]{:S(2)}) copy-start(s32[1,512]{1,0:T(1,128)} %along_ref.1) | copy-start | bytes 6148
  5.1 19.1 %collective-permute-start.2 = (bf16[256,1152]{1,0:T(8,128)(2,1)}, bf16[256,1152]{1,0:T(8,128)(2,1)}, u32[]{:S(2)}, u32[]{:S(2)}) collective-permute-start(bf16[256,1152]{1,0:T(8,128)(2,1)} %get-tuple-element.14), channel_id=1, source_target_pairs={{0,8},{31,23},{2,10},{29,21},{4,12},{27,19},{6,14},{25,17},{8,16},... | collective-permute-start | bytes 1769480 | tf_op jit(solution)/shard_map/ppermute | solution.py:16
  7.6 42.4 %collective-permute-start.4 = (bf16[512,1152]{1,0:T(8,128)(2,1)S(1)}, bf16[512,1152]{1,0:T(8,128)(2,1)S(1)}, u32[]{:S(2)}, u32[]{:S(2)}) collective-permute-start(bf16[512,1152]{1,0:T(8,128)(2,1)S(1)} %get-tuple-element.12.own_ref), channel_id=1, source_target_pairs={{0,4},{31,27},{2,6},{29,25},{8,12},{23,19},{10,14},{21,17},{16,20}... | collective-permute-start | bytes 3538952 | tf_op jit(solution)/shard_map/ppermute | solution.py:16
  11.1 25.6 %collective-permute-start.1 = (bf16[256,1152]{1,0:T(8,128)(2,1)}, bf16[256,1152]{1,0:T(8,128)(2,1)S(1)}, u32[]{:S(2)}, u32[]{:S(2)}) collective-permute-start(bf16[256,1152]{1,0:T(8,128)(2,1)} %get-tuple-element.15), channel_id=1, source_target_pairs={{0,8},{31,23},{2,10},{29,21},{4,12},{27,19},{6,14},{25,17},{8,16},... | collective-permute-start | bytes 1769480 | tf_op jit(solution)/shard_map/ppermute | solution.py:16
  24.2 21.8 %collective-permute-start.5 = (bf16[256,1152]{1,0:T(8,128)(2,1)}, bf16[256,1152]{1,0:T(8,128)(2,1)S(1)}, u32[]{:S(2)}, u32[]{:S(2)}) collective-permute-start(bf16[256,1152]{1,0:T(8,128)(2,1)} %collective-permute-done.2.one_ref), channel_id=1, source_target_pairs={{2,10},{29,21},{6,14},{25,17},{10,18},{21,13},{14,22},{17,9},{18,2... | collective-permute-start | bytes 1769480 | tf_op jit(solution)/shard_map/ppermute | solution.py:16
  36.7 21.8 %collective-permute-start.3 = (bf16[256,1152]{1,0:T(8,128)(2,1)S(1)}, bf16[256,1152]{1,0:T(8,128)(2,1)S(1)}, u32[]{:S(2)}, u32[]{:S(2)}) collective-permute-start(bf16[256,1152]{1,0:T(8,128)(2,1)S(1)} %collective-permute-done.1.one_ref), channel_id=1, source_target_pairs={{2,10},{29,21},{6,14},{25,17},{10,18},{21,13},{14,22},{17,9},{18,2... | collective-permute-start | bytes 1769480 | tf_op jit(solution)/shard_map/ppermute | solution.py:16
  38.3 24.3 %collective-permute-start.6 = (bf16[256,1152]{1,0:T(8,128)(2,1)}, bf16[256,1152]{1,0:T(8,128)(2,1)S(1)}, u32[]{:S(2)}, u32[]{:S(2)}) collective-permute-start(bf16[256,1152]{1,0:T(8,128)(2,1)} %collective-permute-done.2.one_ref), channel_id=1, source_target_pairs={{2,6},{29,25},{6,2},{25,29},{10,14},{21,17},{14,10},{17,21},{18,22... | collective-permute-start | bytes 1769480 | tf_op jit(solution)/shard_map/ppermute | solution.py:16
  39.0 23.6 %collective-permute-start.7 = (bf16[256,1152]{1,0:T(8,128)(2,1)S(1)}, bf16[256,1152]{1,0:T(8,128)(2,1)S(1)}, u32[]{:S(2)}, u32[]{:S(2)}) collective-permute-start(bf16[256,1152]{1,0:T(8,128)(2,1)S(1)} %collective-permute-done.1.one_ref), channel_id=1, source_target_pairs={{2,6},{29,25},{6,2},{25,29},{10,14},{21,17},{14,10},{17,21},{18,22... | collective-permute-start | bytes 1769480 | tf_op jit(solution)/shard_map/ppermute | solution.py:16
  46.0 16.7 %collective-permute-start.8 = (bf16[256,1152]{1,0:T(8,128)(2,1)S(1)}, bf16[256,1152]{1,0:T(8,128)(2,1)S(1)}, u32[]{:S(2)}, u32[]{:S(2)}) collective-permute-start(bf16[256,1152]{1,0:T(8,128)(2,1)S(1)} %collective-permute-done.5.rest_0_), channel_id=1, source_target_pairs={{0,8},{31,23},{8,16},{23,15},{16,24},{15,7},{24,0},{7,31},{6,2},{2... | collective-permute-start | bytes 1769480 | tf_op jit(solution)/shard_map/ppermute | solution.py:16
  53.8 2.1 %copy-start = (f32[1024,1152]{1,0:T(8,128)}, f32[1024,1152]{1,0:T(8,128)S(1)}, u32[]{:S(2)}) copy-start(f32[1024,1152]{1,0:T(8,128)S(1)} %second_blocks.1.sum_ref) | copy-start | bytes 14155780
  58.5 13.6 %collective-permute-start.9 = (bf16[256,1152]{1,0:T(8,128)(2,1)S(1)}, bf16[256,1152]{1,0:T(8,128)(2,1)S(1)}, u32[]{:S(2)}, u32[]{:S(2)}) collective-permute-start(bf16[256,1152]{1,0:T(8,128)(2,1)S(1)} %collective-permute-done.3.rest_1_), channel_id=1, source_target_pairs={{0,8},{31,23},{8,16},{23,15},{16,24},{15,7},{24,0},{7,31},{6,2},{2... | collective-permute-start | bytes 1769480 | tf_op jit(solution)/shard_map/ppermute | solution.py:16
  74.6 5.9 %collective-permute-start.10 = (bf16[512,1152]{1,0:T(8,128)(2,1)S(1)}, bf16[512,1152]{1,0:T(8,128)(2,1)S(1)}, u32[]{:S(2)}, u32[]{:S(2)}) collective-permute-start(bf16[512,1152]{1,0:T(8,128)(2,1)S(1)} %last_block_other.1), channel_id=1, source_target_pairs={{0,2},{31,29},{2,0},{29,31},{4,6},{27,25},{6,4},{25,27},{8,10},{23... | collective-permute-start | bytes 3538952 | tf_op jit(solution)/shard_map/ppermute | solution.py:16
  80.7 28.3 %collective-permute-start.11 = (bf16[512,1152]{1,0:T(8,128)(2,1)S(1)}, bf16[512,1152]{1,0:T(8,128)(2,1)S(1)}, u32[]{:S(2)}, u32[]{:S(2)}) collective-permute-start(bf16[512,1152]{1,0:T(8,128)(2,1)S(1)} %multiply_convert_fusion), channel_id=1, source_target_pairs={{0,1},{1,0},{2,3},{3,2},{4,5},{5,4},{6,7},{7,6},{8,9},{9,8},{10,11... | collective-permute-start | bytes 3538952 | tf_op jit(solution)/shard_map/ppermute | solution.py:16

commit v2 on v1

v2 whole, which is shorter than its diff:
```python
import jax
import jax.numpy as jnp
from jax import lax
from jax.experimental import pallas as pl
from jax.experimental.pallas import tpu as pltpu
from jax.sharding import PartitionSpec as P

GROUP = 4
CHUNKS = 2
VMEM_BYTES = 40 * 1024 * 1024

FIRST, CORE, SIDE = 0, 1, 2


def hop(x, pairs):
    return lax.ppermute(x, ("dp", "rep"), pairs)


def pairs_of(devices, target, members):
    pairs = []
    for p in range(devices):
        if p % GROUP in members:
            q = target(p)
            pairs.append((2 * p, 2 * q))
            pairs.append((2 * (devices - 1 - p) + 1, 2 * (devices - 1 - q) + 1))
    return pairs


def grads_of(scale_ref, left, block, match=None):
    product = lax.dot_general(
        left, block, (((1,), (1,)), ((), ())), preferred_element_type=jnp.float32
    )
    value = 1.0 / (scale_ref[2] + jnp.exp2(scale_ref[0] * product + scale_ref[1]))
    if match is not None:
        value = value - scale_ref[3] * match
    return value.astype(jnp.bfloat16)


def add_blocks(scale_ref, left_ref, refs, out_ref, match=None):
    left = left_ref[...]
    blocks = [ref[...] for ref in refs]
    size = blocks[0].shape[0]
    grads = [
        grads_of(
            scale_ref, left, block, None if match is None else match[:, k * size : (k + 1) * size]
        )
        for k, block in enumerate(blocks)
    ]
    if len(refs) > 1:
        blocks, grads = [jnp.concatenate(blocks, axis=0)], [jnp.concatenate(grads, axis=1)]
    out_ref[...] += jnp.dot(grads[0], blocks[0], preferred_element_type=jnp.float32)


def first_kernel(
    flag_ref,
    scale_ref,
    down_ref,
    along_ref,
    left_ref,
    own_a_ref,
    own_b_ref,
    one_ref,
    from_ref,
    out_ref,
):
    own_rows = pl.program_id(0) == 0
    own_refs = [own_a_ref, own_b_ref]
    out_ref[...] = jnp.zeros_like(out_ref)

    @pl.when(own_rows)
    def _():
        shape = (left_ref.shape[0], along_ref.shape[1])
        column = lax.broadcasted_iota(jnp.int32, shape, 1)
        row = lax.broadcasted_iota(jnp.int32, shape, 0)
        straight = (column == down_ref[...]).astype(jnp.float32)
        turned = (row == along_ref[...]).astype(jnp.float32)
        match = jnp.where(flag_ref[FIRST] == 1, straight, turned)
        add_blocks(scale_ref, left_ref, own_refs, out_ref, match)

    @pl.when(jnp.logical_and(jnp.logical_not(own_rows), flag_ref[CORE] == 0))
    def _():
        add_blocks(scale_ref, left_ref, own_refs, out_ref)

    add_blocks(scale_ref, left_ref, [one_ref], out_ref)

    @pl.when(flag_ref[SIDE] == 1)
    def _():
        add_blocks(scale_ref, left_ref, [from_ref], out_ref)


def brought(flag_ref):
    over = jnp.logical_or(flag_ref[CORE] == 1, flag_ref[SIDE] == 1)
    return over, flag_ref[SIDE] == 0


def second_kernel(flag_ref, scale_ref, left_ref, sum_ref, one_ref, over_ref, out_ref):
    has_over, _ = brought(flag_ref)
    out_ref[...] = sum_ref[...]
    add_blocks(scale_ref, left_ref, [one_ref], out_ref)

    @pl.when(has_over)
    def _():
        add_blocks(scale_ref, left_ref, [over_ref], out_ref)


def third_kernel(
    flag_ref, scale_ref, left_ref, sum_ref, two_a, two_b, from_b, last, out_ref
):
    other_rows = pl.program_id(0) == 1
    core, side = flag_ref[CORE], flag_ref[SIDE]
    out_ref[...] = sum_ref[...]

    @pl.when(jnp.logical_or(jnp.logical_and(core == 1, other_rows), core + side == 0))
    def _():
        add_blocks(scale_ref, left_ref, [two_a, two_b], out_ref)

    @pl.when(side == 1)
    def _():
        add_blocks(scale_ref, left_ref, [from_b], out_ref)

    @pl.when(side == 0)
    def _():
        add_blocks(scale_ref, left_ref, [last], out_ref)


def last_kernel(flag_ref, scale_ref, left_ref, sum_ref, over, last, out_ref, total_ref):
    has_over, has_last = brought(flag_ref)
    total_ref[...] = sum_ref[...]

    @pl.when(has_over)
    def _():
        add_blocks(scale_ref, left_ref, [over], total_ref)

    @pl.when(has_last)
    def _():
        add_blocks(scale_ref, left_ref, [last], total_ref)

    out_ref[...] = total_ref[...].astype(out_ref.dtype)


def whole(x):
    return pl.BlockSpec(x.shape, lambda i: (0,) * x.ndim)


def params():
    return pltpu.CompilerParams(
        dimension_semantics=("arbitrary",), vmem_limit_bytes=VMEM_BYTES
    )


def cost(pairs, rows, depth):
    return pl.CostEstimate(
        flops=int(4 * pairs * rows * rows * depth),
        bytes_accessed=int(8 * rows * depth),
        transcendentals=int(pairs * rows * rows),
    )


SMEM = pl.BlockSpec(memory_space=pltpu.SMEM)


def per_device(
    picture_vectors,
    caption_vectors,
    matched_caption_index,
    score_multiplier,
    score_offset,
    objective_cotangent,
):
    rows, depth = picture_vectors.shape
    devices = lax.axis_size("dp")
    first = lax.axis_index("rep") == 0
    place = lax.axis_index("dp")
    place = jnp.where(first, place, devices - 1 - place)
    flags = jnp.stack([first.astype(jnp.int32), place & 1, (place >> 1) & 1])
    log2e = 1.4426950408889634
    scale = jnp.stack(
        [
            -log2e * score_multiplier,
            -log2e * score_offset - jnp.log2(objective_cotangent),
            1.0 / objective_cotangent,
            objective_cotangent,
        ]
    )

    def up(p):
        return (p + GROUP) % devices

    def across(p):
        return p ^ 2

    def swapped(p):
        return p ^ 1

    to_up = pairs_of(devices, up, (0, 1, 2, 3))
    to_side_1 = pairs_of(devices, across, (0, 1))
    but_2_across = pairs_of(devices, across, (0, 1, 3))
    onward = pairs_of(devices, up, (1, 3)) + pairs_of(devices, across, (2,))
    last_step = pairs_of(devices, up, (0,)) + pairs_of(devices, across, (3,))
    core_swap = pairs_of(devices, swapped, (0, 1, 2, 3))
    replica_swap = [(2 * p + r, 2 * p + 1 - r) for p in range(devices) for r in range(2)]

    size = rows // CHUNKS
    parts = [slice(k * size, (k + 1) * size) for k in range(CHUNKS)]
    own = [jnp.where(first, caption_vectors[x], picture_vectors[x]) for x in parts]
    *own, texts, images = lax.optimization_barrier((*own, caption_vectors, picture_vectors))
    fixed = jnp.where(first, images, texts)

    tile = pl.BlockSpec((rows, depth), lambda i: (i, 0))
    down = matched_caption_index.reshape(rows, 1)

    def kernel(body, name, operands, specs, steps=2):
        return pl.pallas_call(
            body,
            grid=(steps,),
            out_shape=jax.ShapeDtypeStruct((steps * rows, depth), jnp.float32),
            in_specs=[SMEM, SMEM] + specs + [whole(x) for x in operands[len(specs) :]],
            out_specs=tile,
            compiler_params=params(),
            cost_estimate=pl.CostEstimate(flops=1, bytes_accessed=1, transcendentals=0),
            name=name,
        )(flags, scale, *operands)

    one_a, one_b = [hop(x, to_up) for x in own]
    from_a = hop(own[0], to_side_1)
    other_fixed = hop(fixed, core_swap)
    both = jnp.concatenate([fixed, other_fixed], axis=0)
    two_a = hop(one_a, onward)
    over_a = hop(one_a, but_2_across)
    total = kernel(
        first_kernel,
        "first_blocks",
        (down, matched_caption_index, both, *own, one_a, from_a),
        [whole(down), whole(matched_caption_index), tile],
    )
    one_b, own_b, total = lax.optimization_barrier((one_b, own[1], total))
    two_b = hop(one_b, onward)
    from_b = hop(own_b, to_side_1)
    total = kernel(
        second_kernel, "second_blocks", (both, total, one_b, over_a), [tile, tile]
    )
    last_a = hop(two_a, last_step)
    two_b, one_b, total = lax.optimization_barrier((two_b, one_b, total))
    last_b = hop(two_b, last_step)
    over_b = hop(one_b, but_2_across)
    total = kernel(
        third_kernel,
        "third_blocks",
        (both, total, two_a, two_b, from_b, last_a),
        [tile, tile],
    )

    def finish(which, dtype, name):
        part = pl.BlockSpec((rows, depth), lambda i: (which, 0))
        return pl.pallas_call(
            last_kernel,
            grid=(1,),
            out_shape=jax.ShapeDtypeStruct((rows, depth), dtype),
            in_specs=[SMEM, SMEM, part, part, whole(over_b), whole(last_b)],
            out_specs=tile,
            scratch_shapes=[pltpu.VMEM((rows, depth), jnp.float32)],
            compiler_params=params(),
            cost_estimate=cost(0.5, rows, depth),
            name=name,
        )(flags, scale, both, total, over_b, last_b)

    other_total = finish(1, jnp.bfloat16, "last_block_other")
    received = hop(other_total, core_swap)
    own_total = finish(0, jnp.float32, "last_block_own")

    mine = (score_multiplier * (own_total + received.astype(jnp.float32))).astype(jnp.bfloat16)
    theirs = hop(mine, replica_swap)
    return (
        jnp.where(first, mine, theirs).astype(jnp.float32),
        jnp.where(first, theirs, mine).astype(jnp.float32),
    )


def solution(mesh):
    placed = (P("dp", None), P("dp", None), P("dp", None), P(), P(), P())
    return jax.shard_map(
        per_device,
        mesh=mesh,
        in_specs=placed,
        out_specs=(P("dp", None), P("dp", None)),
        check_vma=False,
    )
```

time: 112 us -> 111 us (level); the launches traced: 112 us -> 109 us
  starting transfers between devices: 24.5 us -> 31.7 us
  waiting for transfers between devices: 48.4 us -> 43.1 us
  local copies, waits for them, and re-layouts: 3.38 us -> 0.59 us
  Pallas kernels: 24.9 us -> 23.4 us
    ppermute x12 -> x13, starting transfers between devices: 24.5 us -> 31.7 us  [hop(): return lax.ppermute(x, ('dp', 'rep'), pairs)]
    ppermute x12 -> x13, waiting for transfers between devices: 48.4 us -> 43.1 us  [hop(): return lax.ppermute(x, ('dp', 'rep'), pairs)]
    unnamed x4 -> x6, local copies, waits for them, and re-layouts: 2.13 us -> 0.44 us
    pallas_call x3, Pallas kernels: 20 us -> 18.6 us  [kernel(): pl.pallas_call(body, grid=(steps,), out_shape=jax.ShapeDtypeStruct((steps...]
    select_n x1 -> x2, other arithmetic: 2.86 us -> 3.02 us  [the longest x1 1.88 us: per_device(): jnp.where(first, caption_vectors[x], picture_vectors[x])]
  transfers between devices with their start and end apart: 12 -> 13, of which waited for: 7 -> 6; matrix products, arithmetic and copies ran while one was open for 3% -> 2% of each run, Pallas kernels for 20% -> 19%
where the time goes in v2:
time: 111 us; the launch traced here: 109 us
  waiting for transfers between devices  43.1 us (39%)
  starting transfers between devices  31.7 us (29%)
  Pallas kernels  23.4 us (21%)
  other arithmetic  7.77 us (7%)
  between operations  2.87 us (3%)
    ppermute x13, waiting for transfers between devices, hop(): return lax.ppermute(x, ('dp', 'rep'), pairs)  43.1 us
    ppermute x13, starting transfers between devices, hop(): return lax.ppermute(x, ('dp', 'rep'), pairs)  31.7 us
    pallas_call x3, Pallas kernels, kernel(): pl.pallas_call(body, grid=(steps,), out_shape=jax.ShapeDtypeStruct((steps...  18.6 us
    pallas_call x2, Pallas kernels, finish(): pl.pallas_call(last_kernel, grid=(1,), out_shape=jax.ShapeDtypeStruct((ro...  4.74 us
    convert_element_type x1, other arithmetic, per_device(): jnp.where(first, theirs, mine).astype(jnp.float32)  2.49 us
  transfers between devices with their start and end apart: 13, of which 6 were waited for; matrix products, arithmetic and copies ran while one was open for 2% of the time, Pallas kernels for 19%

profile of v2, /device:TPU:0, one launch (start us, length us, event | category | flops | bytes accessed | tf_op | source)
XLA Modules:
  0.0 109.4 jit_solution(1426030914072809978)
XLA Ops:
  0.6 0.0 copy-start.1
  0.6 0.0 copy-start.2
  0.7 1.9 %slice_select_fusion = (bf16[256,1152]{1,0:T(8,128)(2,1)S(1)}, bf16[256,1152]{1,0:T(8,128)(2,1)S(1)}) fusion(bf16[512,1152]{1,0:T(8,128)(2,1)} %param.6, bf16[512,1152]{1,0:T(8,128)(2,1)} %param.7, pred[]{:T(512)S(6)} %eq.3), kind=kLoop, calls=%fused_computation.5 | loop fusion | flops 589824 | bytes 3538945 | tf_op jit(solution)/shard_map/jit(_where)/select_n | solution.py:205
  2.5 0.1 copy-done.1
  2.6 0.4 copy-done.2
  3.0 0.0 copy-start
  3.0 1.1 %broadcast_select_fusion = bf16[512,1152]{1,0:T(8,128)(2,1)} fusion(bf16[512,1152]{1,0:T(8,128)(2,1)S(1)} %copy-done.1, bf16[512,1152]{1,0:T(8,128)(2,1)S(1)} %copy-done.2, pred[]{:T(512)S(6)} %eq.3), kind=kLoop, calls=%fused_computation.4 | loop fusion | flops 589824 | bytes 3538945 | tf_op jit(solution)/shard_map/jit(_where)/select_n | solution.py:207
  4.1 0.5 collective-permute-start
  4.6 2.6 %collective-permute-start.2 = (bf16[256,1152]{1,0:T(8,128)(2,1)S(1)}, bf16[256,1152]{1,0:T(8,128)(2,1)S(1)}, u32[]{:S(2)}, u32[]{:S(2)}) collective-permute-start(bf16[256,1152]{1,0:T(8,128)(2,1)S(1)} %get-tuple-element.15.own_a_ref), channel_id=1, source_target_pairs={{0,8},{31,23},{2,10},{29,21},{4,12},{27,19},{6,14},{25,17},{8,16},... | collective-permute-start | bytes 1769480 | tf_op jit(solution)/shard_map/ppermute | solution.py:16
  7.1 3.4 %collective-permute-start.3 = (bf16[256,1152]{1,0:T(8,128)(2,1)S(1)}, bf16[256,1152]{1,0:T(8,128)(2,1)S(1)}, u32[]{:S(2)}, u32[]{:S(2)}) collective-permute-start(bf16[256,1152]{1,0:T(8,128)(2,1)S(1)} %get-tuple-element.15.own_a_ref), channel_id=1, source_target_pairs={{0,4},{31,27},{2,6},{29,25},{8,12},{23,19},{10,14},{21,17},{16,20}... | collective-permute-start | bytes 1769480 | tf_op jit(solution)/shard_map/ppermute | solution.py:16
  10.6 1.6 %collective-permute-start.1 = (bf16[256,1152]{1,0:T(8,128)(2,1)S(1)}, bf16[256,1152]{1,0:T(8,128)(2,1)S(1)}, u32[]{:S(2)}, u32[]{:S(2)}) collective-permute-start(bf16[256,1152]{1,0:T(8,128)(2,1)S(1)} %get-tuple-element.20.own_b_ref), channel_id=1, source_target_pairs={{0,8},{31,23},{2,10},{29,21},{4,12},{27,19},{6,14},{25,17},{8,16},... | collective-permute-start | bytes 1769480 | tf_op jit(solution)/shard_map/ppermute | solution.py:16
  14.3 0.0 copy-done
  14.3 0.1 copy.8.down_ref
  14.4 0.1 pad_add_fusion.flag_ref
  14.5 0.1 pad_maximum_fusion.1.scale_ref
  14.6 8.8 %collective-permute-done.2.one_ref = bf16[256,1152]{1,0:T(8,128)(2,1)S(1)} collective-permute-done((bf16[256,1152]{1,0:T(8,128)(2,1)S(1)}, bf16[256,1152]{1,0:T(8,128)(2,1)S(1)}, u32[]{:S(2)}, u32[]{:S(2)}) %collective-permute-start.2) | collective-permute-done | bytes 589856 | tf_op jit(solution)/shard_map/ppermute | solution.py:16
  23.4 1.3 %collective-permute-start.6 = (bf16[256,1152]{1,0:T(8,128)(2,1)S(1)}, bf16[256,1152]{1,0:T(8,128)(2,1)S(1)}, u32[]{:S(2)}, u32[]{:S(2)}) collective-permute-start(bf16[256,1152]{1,0:T(8,128)(2,1)S(1)} %collective-permute-done.2.one_ref), channel_id=1, source_target_pairs={{2,10},{29,21},{6,14},{25,17},{10,18},{21,13},{14,22},{17,9},{18,2... | collective-permute-start | bytes 1769480 | tf_op jit(solution)/shard_map/ppermute | solution.py:16
  24.6 4.6 %collective-permute-start.5 = (bf16[256,1152]{1,0:T(8,128)(2,1)S(1)}, bf16[256,1152]{1,0:T(8,128)(2,1)S(1)}, u32[]{:S(2)}, u32[]{:S(2)}) collective-permute-start(bf16[256,1152]{1,0:T(8,128)(2,1)S(1)} %collective-permute-done.2.one_ref), channel_id=1, source_target_pairs={{0,4},{31,27},{2,6},{29,25},{6,2},{25,29},{8,12},{23,19},{10,14},{... | collective-permute-start | bytes 1769480 | tf_op jit(solution)/shard_map/ppermute | solution.py:16
  29.3 0.0 collective-permute-done
  29.3 1.8 %pad_maximum_fusion.left_ref = bf16[1024,1152]{1,0:T(8,128)(2,1)S(1)} fusion(bf16[512,1152]{1,0:T(8,128)(2,1)} %collective-permute-done, bf16[512,1152]{1,0:T(8,128)(2,1)} %broadcast_select_fusion), kind=kLoop, calls=%fused_computation | loop fusion | flops 4718592 | bytes 4718592 | tf_op jit(solution)/shard_map/concatenate | solution.py:227
  31.1 0.0 collective-permute-done.3.from_ref
  31.1 7.6 %first_blocks.1.sum_ref = f32[1024,1152]{1,0:T(8,128)S(1)} custom-call(s32[3]{0:T(128)S(1)} %pad_add_fusion.flag_ref, f32[4]{0:T(128)S(1)} %pad_maximum_fusion.1.scale_ref, s32[512,1]{1,0:T(8,128)S(1)} %copy.8.down_ref, s32[1,512]{1,0:T(1,128)S(1)} %copy-done, bf16[1024,1152]{1,0:T(8,128)(2,1)S(1)} %pad_maximum_fusion.left_ref, ...), custom_call_target="tpu_custom_call" | custom-call | flops 1 | bytes 1 | tf_op jit(solution)/shard_map/first_blocks/pallas_call | solution.py:213
  38.7 0.0 collective-permute-done.1.one_ref
  38.7 1.3 %collective-permute-start.4 = (bf16[256,1152]{1,0:T(8,128)(2,1)S(1)}, bf16[256,1152]{1,0:T(8,128)(2,1)S(1)}, u32[]{:S(2)}, u32[]{:S(2)}) collective-permute-start(bf16[256,1152]{1,0:T(8,128)(2,1)S(1)} %collective-permute-done.1.one_ref), channel_id=1, source_target_pairs={{2,10},{29,21},{6,14},{25,17},{10,18},{21,13},{14,22},{17,9},{18,2... | collective-permute-start | bytes 1769480 | tf_op jit(solution)/shard_map/ppermute | solution.py:16
  40.0 4.6 %collective-permute-start.7 = (bf16[256,1152]{1,0:T(8,128)(2,1)S(1)}, bf16[256,1152]{1,0:T(8,128)(2,1)S(1)}, u32[]{:S(2)}, u32[]{:S(2)}) collective-permute-start(bf16[256,1152]{1,0:T(8,128)(2,1)S(1)} %get-tuple-element.20.own_b_ref), channel_id=1, source_target_pairs={{0,4},{31,27},{2,6},{29,25},{8,12},{23,19},{10,14},{21,17},{16,20}... | collective-permute-start | bytes 1769480 | tf_op jit(solution)/shard_map/ppermute | solution.py:16
  44.6 0.0 collective-permute-done.6.two_a
  44.6 1.9 %collective-permute-start.8 = (bf16[256,1152]{1,0:T(8,128)(2,1)S(1)}, bf16[256,1152]{1,0:T(8,128)(2,1)S(1)}, u32[]{:S(2)}, u32[]{:S(2)}) collective-permute-start(bf16[256,1152]{1,0:T(8,128)(2,1)S(1)} %collective-permute-done.6.two_a), channel_id=1, source_target_pairs={{0,8},{31,23},{8,16},{23,15},{16,24},{15,7},{24,0},{7,31},{6,2},{2... | collective-permute-start | bytes 1769480 | tf_op jit(solution)/shard_map/ppermute | solution.py:16
  46.5 0.0 collective-permute-done.5.over_ref
  46.6 3.7 %second_blocks.1.sum_ref = f32[1024,1152]{1,0:T(8,128)S(1)} custom-call(s32[3]{0:T(128)S(1)} %pad_add_fusion.flag_ref, f32[4]{0:T(128)S(1)} %pad_maximum_fusion.1.scale_ref, bf16[1024,1152]{1,0:T(8,128)(2,1)S(1)} %pad_maximum_fusion.left_ref, f32[1024,1152]{1,0:T(8,128)S(1)} %first_blocks.1.sum_ref, bf16[256,1152]{1,0:T(8,128)(2,1)S(1)} %collective-permute-done.1.one_ref, ...), custom_call_target="tpu_custom_call" | custom-call | flops 1 | bytes 1 | tf_op jit(solution)/shard_map/second_blocks/pallas_call | solution.py:213
  50.2 2.5 %collective-permute-done.4.two_b = bf16[256,1152]{1,0:T(8,128)(2,1)S(1)} collective-permute-done((bf16[256,1152]{1,0:T(8,128)(2,1)S(1)}, bf16[256,1152]{1,0:T(8,128)(2,1)S(1)}, u32[]{:S(2)}, u32[]{:S(2)}) %collective-permute-start.4) | collective-permute-done | bytes 589856 | tf_op jit(solution)/shard_map/ppermute | solution.py:16
  52.8 1.5 %collective-permute-start.9 = (bf16[256,1152]{1,0:T(8,128)(2,1)S(1)}, bf16[256,1152]{1,0:T(8,128)(2,1)S(1)}, u32[]{:S(2)}, u32[]{:S(2)}) collective-permute-start(bf16[256,1152]{1,0:T(8,128)(2,1)S(1)} %collective-permute-done.1.one_ref), channel_id=1, source_target_pairs={{0,4},{31,27},{2,6},{29,25},{6,2},{25,29},{8,12},{23,19},{10,14},{... | collective-permute-start | bytes 1769480 | tf_op jit(solution)/shard_map/ppermute | solution.py:16
  54.3 2.1 %collective-permute-start.10 = (bf16[256,1152]{1,0:T(8,128)(2,1)S(1)}, bf16[256,1152]{1,0:T(8,128)(2,1)S(1)}, u32[]{:S(2)}, u32[]{:S(2)}) collective-permute-start(bf16[256,1152]{1,0:T(8,128)(2,1)S(1)} %collective-permute-done.4.two_b), channel_id=1, source_target_pairs={{0,8},{31,23},{8,16},{23,15},{16,24},{15,7},{24,0},{7,31},{6,2},{2... | collective-permute-start | bytes 1769480 | tf_op jit(solution)/shard_map/ppermute | solution.py:16
  56.4 1.8 %collective-permute-done.8.last = bf16[256,1152]{1,0:T(8,128)(2,1)S(1)} collective-permute-done((bf16[256,1152]{1,0:T(8,128)(2,1)S(1)}, bf16[256,1152]{1,0:T(8,128)(2,1)S(1)}, u32[]{:S(2)}, u32[]{:S(2)}) %collective-permute-start.8) | collective-permute-done | bytes 589856 | tf_op jit(solution)/shard_map/ppermute | solution.py:16
  58.2 0.0 collective-permute-done.7.from_b
  58.2 7.4 %third_blocks.1.sum_ref = f32[1024,1152]{1,0:T(8,128)S(1)} custom-call(s32[3]{0:T(128)S(1)} %pad_add_fusion.flag_ref, f32[4]{0:T(128)S(1)} %pad_maximum_fusion.1.scale_ref, bf16[1024,1152]{1,0:T(8,128)(2,1)S(1)} %pad_maximum_fusion.left_ref, f32[1024,1152]{1,0:T(8,128)S(1)} %second_blocks.1.sum_ref, bf16[256,1152]{1,0:T(8,128)(2,1)S(1)} %collective-permute-done.6.two_a, ...), custom_call_target="tpu_custom_call" | custom-call | flops 1 | bytes 1 | tf_op jit(solution)/shard_map/third_blocks/pallas_call | solution.py:213
  65.6 3.6 %collective-permute-done.9.over = bf16[256,1152]{1,0:T(8,128)(2,1)S(1)} collective-permute-done((bf16[256,1152]{1,0:T(8,128)(2,1)S(1)}, bf16[256,1152]{1,0:T(8,128)(2,1)S(1)}, u32[]{:S(2)}, u32[]{:S(2)}) %collective-permute-start.9) | collective-permute-done | bytes 589856 | tf_op jit(solution)/shard_map/ppermute | solution.py:16
  69.2 0.0 collective-permute-done.10.last
  69.2 2.4 %last_block_other.1 = bf16[512,1152]{1,0:T(8,128)(2,1)S(1)} custom-call(s32[3]{0:T(128)S(1)} %pad_add_fusion.flag_ref, f32[4]{0:T(128)S(1)} %pad_maximum_fusion.1.scale_ref, bf16[1024,1152]{1,0:T(8,128)(2,1)S(1)} %pad_maximum_fusion.left_ref, f32[1024,1152]{1,0:T(8,128)S(1)} %third_blocks.1.sum_ref, bf16[256,1152]{1,0:T(8,128)(2,1)S(1)} %collective-permute-done.9.over, ...), custom_call_target="tpu_custom_call" | custom-call | flops 603979776 | bytes 4718592 | tf_op jit(solution)/shard_map/last_block_other/pallas_call | solution.py:255
  71.6 1.7 %collective-permute-start.11 = (bf16[512,1152]{1,0:T(8,128)(2,1)S(1)}, bf16[512,1152]{1,0:T(8,128)(2,1)S(1)}, u32[]{:S(2)}, u32[]{:S(2)}) collective-permute-start(bf16[512,1152]{1,0:T(8,128)(2,1)S(1)} %last_block_other.1), channel_id=1, source_target_pairs={{0,2},{31,29},{2,0},{29,31},{4,6},{27,25},{6,4},{25,27},{8,10},{23... | collective-permute-start | bytes 3538952 | tf_op jit(solution)/shard_map/ppermute | solution.py:16
  73.2 2.4 %last_block_own.1 = f32[512,1152]{1,0:T(8,128)S(1)} custom-call(s32[3]{0:T(128)S(1)} %pad_add_fusion.flag_ref, f32[4]{0:T(128)S(1)} %pad_maximum_fusion.1.scale_ref, bf16[1024,1152]{1,0:T(8,128)(2,1)S(1)} %pad_maximum_fusion.left_ref, f32[1024,1152]{1,0:T(8,128)S(1)} %third_blocks.1.sum_ref, bf16[256,1152]{1,0:T(8,128)(2,1)S(1)} %collective-permute-done.9.over, ...), custom_call_target="tpu_custom_call" | custom-call | flops 603979776 | bytes 4718592 | tf_op jit(solution)/shard_map/last_block_own/pallas_call | solution.py:255
  75.6 0.1 collective-permute-done.11
  75.7 0.3 multiply_convert_fusion
  76.0 4.6 %collective-permute-start.12 = (bf16[512,1152]{1,0:T(8,128)(2,1)S(1)}, bf16[512,1152]{1,0:T(8,128)(2,1)S(1)}, u32[]{:S(2)}, u32[]{:S(2)}) collective-permute-start(bf16[512,1152]{1,0:T(8,128)(2,1)S(1)} %multiply_convert_fusion), channel_id=1, source_target_pairs={{0,1},{1,0},{2,3},{3,2},{4,5},{5,4},{6,7},{7,6},{8,9},{9,8},{10,11... | collective-permute-start | bytes 3538952 | tf_op jit(solution)/shard_map/ppermute | solution.py:16
  80.6 26.3 %collective-permute-done.12 = bf16[512,1152]{1,0:T(8,128)(2,1)S(1)} collective-permute-done((bf16[512,1152]{1,0:T(8,128)(2,1)S(1)}, bf16[512,1152]{1,0:T(8,128)(2,1)S(1)}, u32[]{:S(2)}, u32[]{:S(2)}) %collective-permute-start.12) | collective-permute-done | bytes 1179680 | tf_op jit(solution)/shard_map/ppermute | solution.py:16
  106.9 2.5 %select_convert_fusion = (f32[512,1152]{1,0:T(8,128)}, f32[512,1152]{1,0:T(8,128)}) fusion(bf16[512,1152]{1,0:T(8,128)(2,1)S(1)} %collective-permute-done.12, bf16[512,1152]{1,0:T(8,128)(2,1)S(1)} %multiply_convert_fusion, pred[]{:T(512)S(6)} %eq.3), kind=kLoop, calls=%fused_computation.2 | loop fusion | flops 2359296 | bytes 7077889 | tf_op jit(solution)/shard_map/convert_element_type | solution.py:275
Async XLA Ops:
  0.6 2.0 %copy-start.1 = (bf16[512,1152]{1,0:T(8,128)(2,1)S(1)}, bf16[512,1152]{1,0:T(8,128)(2,1)}, u32[]{:S(2)}) copy-start(bf16[512,1152]{1,0:T(8,128)(2,1)} %param.6) | copy-start | bytes 3538948
  0.6 2.3 %copy-start.2 = (bf16[512,1152]{1,0:T(8,128)(2,1)S(1)}, bf16[512,1152]{1,0:T(8,128)(2,1)}, u32[]{:S(2)}) copy-start(bf16[512,1152]{1,0:T(8,128)(2,1)} %param.7) | copy-start | bytes 3538948
  3.0 11.3 %copy-start = (s32[1,512]{1,0:T(1,128)S(1)}, s32[1,512]{1,0:T(1,128)}, u32[]{:S(2)}) copy-start(s32[1,512]{1,0:T(1,128)} %along_ref.1) | copy-start | bytes 6148
  4.1 25.1 %collective-permute-start = (bf16[512,1152]{1,0:T(8,128)(2,1)}, bf16[512,1152]{1,0:T(8,128)(2,1)}, u32[]{:S(2)}, u32[]{:S(2)}) collective-permute-start(bf16[512,1152]{1,0:T(8,128)(2,1)} %broadcast_select_fusion), channel_id=1, source_target_pairs={{0,2},{31,29},{2,0},{29,31},{4,6},{27,25},{6,4},{25,27},{8,10},{23... | collective-permute-start | bytes 3538952 | tf_op jit(solution)/shard_map/ppermute | solution.py:16
  4.6 18.8 %collective-permute-start.2 = (bf16[256,1152]{1,0:T(8,128)(2,1)S(1)}, bf16[256,1152]{1,0:T(8,128)(2,1)S(1)}, u32[]{:S(2)}, u32[]{:S(2)}) collective-permute-start(bf16[256,1152]{1,0:T(8,128)(2,1)S(1)} %get-tuple-element.15.own_a_ref), channel_id=1, source_target_pairs={{0,8},{31,23},{2,10},{29,21},{4,12},{27,19},{6,14},{25,17},{8,16},... | collective-permute-start | bytes 1769480 | tf_op jit(solution)/shard_map/ppermute | solution.py:16
  7.1 23.9 %collective-permute-start.3 = (bf16[256,1152]{1,0:T(8,128)(2,1)S(1)}, bf16[256,1152]{1,0:T(8,128)(2,1)S(1)}, u32[]{:S(2)}, u32[]{:S(2)}) collective-permute-start(bf16[256,1152]{1,0:T(8,128)(2,1)S(1)} %get-tuple-element.15.own_a_ref), channel_id=1, source_target_pairs={{0,4},{31,27},{2,6},{29,25},{8,12},{23,19},{10,14},{21,17},{16,20}... | collective-permute-start | bytes 1769480 | tf_op jit(solution)/shard_map/ppermute | solution.py:16
  10.6 28.1 %collective-permute-start.1 = (bf16[256,1152]{1,0:T(8,128)(2,1)S(1)}, bf16[256,1152]{1,0:T(8,128)(2,1)S(1)}, u32[]{:S(2)}, u32[]{:S(2)}) collective-permute-start(bf16[256,1152]{1,0:T(8,128)(2,1)S(1)} %get-tuple-element.20.own_b_ref), channel_id=1, source_target_pairs={{0,8},{31,23},{2,10},{29,21},{4,12},{27,19},{6,14},{25,17},{8,16},... | collective-permute-start | bytes 1769480 | tf_op jit(solution)/shard_map/ppermute | solution.py:16
  23.4 21.3 %collective-permute-start.6 = (bf16[256,1152]{1,0:T(8,128)(2,1)S(1)}, bf16[256,1152]{1,0:T(8,128)(2,1)S(1)}, u32[]{:S(2)}, u32[]{:S(2)}) collective-permute-start(bf16[256,1152]{1,0:T(8,128)(2,1)S(1)} %collective-permute-done.2.one_ref), channel_id=1, source_target_pairs={{2,10},{29,21},{6,14},{25,17},{10,18},{21,13},{14,22},{17,9},{18,2... | collective-permute-start | bytes 1769480 | tf_op jit(solution)/shard_map/ppermute | solution.py:16
  24.6 21.9 %collective-permute-start.5 = (bf16[256,1152]{1,0:T(8,128)(2,1)S(1)}, bf16[256,1152]{1,0:T(8,128)(2,1)S(1)}, u32[]{:S(2)}, u32[]{:S(2)}) collective-permute-start(bf16[256,1152]{1,0:T(8,128)(2,1)S(1)} %collective-permute-done.2.one_ref), channel_id=1, source_target_pairs={{0,4},{31,27},{2,6},{29,25},{6,2},{25,29},{8,12},{23,19},{10,14},{... | collective-permute-start | bytes 1769480 | tf_op jit(solution)/shard_map/ppermute | solution.py:16
  38.7 14.1 %collective-permute-start.4 = (bf16[256,1152]{1,0:T(8,128)(2,1)S(1)}, bf16[256,1152]{1,0:T(8,128)(2,1)S(1)}, u32[]{:S(2)}, u32[]{:S(2)}) collective-permute-start(bf16[256,1152]{1,0:T(8,128)(2,1)S(1)} %collective-permute-done.1.one_ref), channel_id=1, source_target_pairs={{2,10},{29,21},{6,14},{25,17},{10,18},{21,13},{14,22},{17,9},{18,2... | collective-permute-start | bytes 1769480 | tf_op jit(solution)/shard_map/ppermute | solution.py:16
  40.0 18.2 %collective-permute-start.7 = (bf16[256,1152]{1,0:T(8,128)(2,1)S(1)}, bf16[256,1152]{1,0:T(8,128)(2,1)S(1)}, u32[]{:S(2)}, u32[]{:S(2)}) collective-permute-start(bf16[256,1152]{1,0:T(8,128)(2,1)S(1)} %get-tuple-element.20.own_b_ref), channel_id=1, source_target_pairs={{0,4},{31,27},{2,6},{29,25},{8,12},{23,19},{10,14},{21,17},{16,20}... | collective-permute-start | bytes 1769480 | tf_op jit(solution)/shard_map/ppermute | solution.py:16
  44.6 13.6 %collective-permute-start.8 = (bf16[256,1152]{1,0:T(8,128)(2,1)S(1)}, bf16[256,1152]{1,0:T(8,128)(2,1)S(1)}, u32[]{:S(2)}, u32[]{:S(2)}) collective-permute-start(bf16[256,1152]{1,0:T(8,128)(2,1)S(1)} %collective-permute-done.6.two_a), channel_id=1, source_target_pairs={{0,8},{31,23},{8,16},{23,15},{16,24},{15,7},{24,0},{7,31},{6,2},{2... | collective-permute-start | bytes 1769480 | tf_op jit(solution)/shard_map/ppermute | solution.py:16
  52.8 16.4 %collective-permute-start.9 = (bf16[256,1152]{1,0:T(8,128)(2,1)S(1)}, bf16[256,1152]{1,0:T(8,128)(2,1)S(1)}, u32[]{:S(2)}, u32[]{:S(2)}) collective-permute-start(bf16[256,1152]{1,0:T(8,128)(2,1)S(1)} %collective-permute-done.1.one_ref), channel_id=1, source_target_pairs={{0,4},{31,27},{2,6},{29,25},{6,2},{25,29},{8,12},{23,19},{10,14},{... | collective-permute-start | bytes 1769480 | tf_op jit(solution)/shard_map/ppermute | solution.py:16
  54.3 14.9 %collective-permute-start.10 = (bf16[256,1152]{1,0:T(8,128)(2,1)S(1)}, bf16[256,1152]{1,0:T(8,128)(2,1)S(1)}, u32[]{:S(2)}, u32[]{:S(2)}) collective-permute-start(bf16[256,1152]{1,0:T(8,128)(2,1)S(1)} %collective-permute-done.4.two_b), channel_id=1, source_target_pairs={{0,8},{31,23},{8,16},{23,15},{16,24},{15,7},{24,0},{7,31},{6,2},{2... | collective-permute-start | bytes 1769480 | tf_op jit(solution)/shard_map/ppermute | solution.py:16
  71.6 4.1 %collective-permute-start.11 = (bf16[512,1152]{1,0:T(8,128)(2,1)S(1)}, bf16[512,1152]{1,0:T(8,128)(2,1)S(1)}, u32[]{:S(2)}, u32[]{:S(2)}) collective-permute-start(bf16[512,1152]{1,0:T(8,128)(2,1)S(1)} %last_block_other.1), channel_id=1, source_target_pairs={{0,2},{31,29},{2,0},{29,31},{4,6},{27,25},{6,4},{25,27},{8,10},{23... | collective-permute-start | bytes 3538952 | tf_op jit(solution)/shard_map/ppermute | solution.py:16
  76.0 30.9 %collective-permute-start.12 = (bf16[512,1152]{1,0:T(8,128)(2,1)S(1)}, bf16[512,1152]{1,0:T(8,128)(2,1)S(1)}, u32[]{:S(2)}, u32[]{:S(2)}) collective-permute-start(bf16[512,1152]{1,0:T(8,128)(2,1)S(1)} %multiply_convert_fusion), channel_id=1, source_target_pairs={{0,1},{1,0},{2,3},{3,2},{4,5},{5,4},{6,7},{7,6},{8,9},{9,8},{10,11... | collective-permute-start | bytes 3538952 | tf_op jit(solution)/shard_map/ppermute | solution.py:16

commit v3 on v2

v3 whole, which is shorter than its diff:
```python
import jax
import jax.numpy as jnp
from jax import lax
from jax.experimental import pallas as pl
from jax.experimental.pallas import tpu as pltpu
from jax.sharding import PartitionSpec as P

GROUP = 4
VMEM_BYTES = 36 * 1024 * 1024
NO_ROOM = 60 * 1024 * 1024

FIRST, CORE, SIDE = 0, 1, 2


def hop(x, pairs):
    return lax.ppermute(x, ("dp", "rep"), pairs)


def pairs_of(devices, target, members):
    pairs = []
    for p in range(devices):
        if p % GROUP in members:
            q = target(p)
            pairs.append((2 * p, 2 * q))
            pairs.append((2 * (devices - 1 - p) + 1, 2 * (devices - 1 - q) + 1))
    return pairs


def grads_of(scale_ref, left, block, match=None):
    product = lax.dot_general(
        left, block, (((1,), (1,)), ((), ())), preferred_element_type=jnp.float32
    )
    value = 1.0 / (scale_ref[2] + jnp.exp2(scale_ref[0] * product + scale_ref[1]))
    if match is not None:
        value = value - scale_ref[3] * match
    return value.astype(jnp.bfloat16)


def add_block(scale_ref, left_ref, refs, out_ref, match=None):
    block = jnp.concatenate([ref[...] for ref in refs], axis=0) if len(refs) > 1 else refs[0][...]
    grads = grads_of(scale_ref, left_ref[...], block, match)
    out_ref[...] += jnp.dot(grads, block, preferred_element_type=jnp.float32)


def pick_kernel(image_ref, text_ref, own_a_ref, own_b_ref, fixed_ref, sems):
    half = own_a_ref.shape[0]

    def copies(moving_ref, still_ref):
        moves = [
            pltpu.make_async_copy(moving_ref.at[:half], own_a_ref, sems.at[0]),
            pltpu.make_async_copy(moving_ref.at[half:], own_b_ref, sems.at[1]),
            pltpu.make_async_copy(still_ref, fixed_ref, sems.at[2]),
        ]
        for move in moves:
            move.start()
        for move in moves:
            move.wait()

    first = lax.axis_index("rep") == 0

    @pl.when(first)
    def _():
        copies(text_ref, image_ref)

    @pl.when(jnp.logical_not(first))
    def _():
        copies(image_ref, text_ref)


def choose_rows(fixed_ref, other_ref, left_ref):
    @pl.when(pl.program_id(0) == 0)
    def _():
        left_ref[...] = fixed_ref[...]

    @pl.when(pl.program_id(0) == 1)
    def _():
        left_ref[...] = other_ref[...]


def own_kernel(
    flag_ref, scale_ref, down_ref, along_ref, left_ref, own_a_ref, own_b_ref, out_ref
):
    shape = (left_ref.shape[0], along_ref.shape[1])
    column = lax.broadcasted_iota(jnp.int32, shape, 1)
    row = lax.broadcasted_iota(jnp.int32, shape, 0)
    straight = (column == down_ref[...]).astype(jnp.float32)
    turned = (row == along_ref[...]).astype(jnp.float32)
    match = jnp.where(flag_ref[FIRST] == 1, straight, turned)
    out_ref[...] = jnp.zeros_like(out_ref)
    add_block(scale_ref, left_ref, [own_a_ref, own_b_ref], out_ref, match)


def second_kernel(
    flag_ref,
    scale_ref,
    sum_ref,
    fixed_ref,
    other_ref,
    own_a,
    own_b,
    one_a,
    one_b,
    group,
    over,
    out_ref,
    left_ref,
):
    other_rows = pl.program_id(0) == 1
    core, side = flag_ref[CORE], flag_ref[SIDE]
    choose_rows(fixed_ref, other_ref, left_ref)

    @pl.when(other_rows)
    def _():
        out_ref[...] = jnp.zeros_like(out_ref)

    @pl.when(jnp.logical_not(other_rows))
    def _():
        out_ref[...] = sum_ref[...]

    @pl.when(jnp.logical_and(other_rows, core == 0))
    def _():
        add_block(scale_ref, left_ref, [own_a, own_b], out_ref)

    add_block(scale_ref, left_ref, [one_a, one_b], out_ref)

    @pl.when(jnp.logical_or(core == 1, side == 1))
    def _():
        add_block(scale_ref, left_ref, [group, over], out_ref)


def third_kernel(
    flag_ref, scale_ref, sum_ref, fixed_ref, other_ref, two_a, two_b, over, last, out_ref, left_ref
):
    other_rows = pl.program_id(0) == 1
    core, side = flag_ref[CORE], flag_ref[SIDE]
    choose_rows(fixed_ref, other_ref, left_ref)
    out_ref[...] = sum_ref[...]

    @pl.when(jnp.logical_or(jnp.logical_and(core == 1, other_rows), core + side == 0))
    def _():
        add_block(scale_ref, left_ref, [two_a, two_b], out_ref)

    add_block(scale_ref, left_ref, [over, last], out_ref)


def last_kernel(flag_ref, scale_ref, left_ref, sum_ref, group, last, out_ref, total_ref):
    total_ref[...] = sum_ref[...]

    @pl.when(flag_ref[SIDE] == 0)
    def _():
        add_block(scale_ref, left_ref, [last], total_ref)

    @pl.when(flag_ref[SIDE] == 1)
    def _():
        add_block(scale_ref, left_ref, [group], total_ref)

    out_ref[...] = total_ref[...].astype(out_ref.dtype)


def whole(x):
    return pl.BlockSpec(x.shape, lambda i: (0,) * x.ndim)


def params():
    return pltpu.CompilerParams(
        dimension_semantics=("arbitrary",), vmem_limit_bytes=VMEM_BYTES
    )


NO_COST = pl.CostEstimate(flops=1, bytes_accessed=1, transcendentals=0)
SMEM = pl.BlockSpec(memory_space=pltpu.SMEM)
ANY = pl.BlockSpec(memory_space=pl.ANY)


def per_device(
    picture_vectors,
    caption_vectors,
    matched_caption_index,
    score_multiplier,
    score_offset,
    objective_cotangent,
):
    rows, depth = picture_vectors.shape
    devices = lax.axis_size("dp")
    first = lax.axis_index("rep") == 0
    place = lax.axis_index("dp")
    place = jnp.where(first, place, devices - 1 - place)
    flags = jnp.stack([first.astype(jnp.int32), place & 1, (place >> 1) & 1])
    log2e = 1.4426950408889634
    scale = jnp.stack(
        [
            -log2e * score_multiplier,
            -log2e * score_offset - jnp.log2(objective_cotangent),
            1.0 / objective_cotangent,
            objective_cotangent,
        ]
    )

    def up(p):
        return (p + GROUP) % devices

    def across(p):
        return p ^ 2

    def swapped(p):
        return p ^ 1

    to_up = pairs_of(devices, up, (0, 1, 2, 3))
    to_side_1 = pairs_of(devices, across, (0, 1))
    but_2_across = pairs_of(devices, across, (0, 1, 3))
    onward = pairs_of(devices, up, (1, 3)) + pairs_of(devices, across, (2,))
    last_step = pairs_of(devices, up, (0,)) + pairs_of(devices, across, (3,))
    core_swap = pairs_of(devices, swapped, (0, 1, 2, 3))
    replica_swap = [(2 * p + r, 2 * p + 1 - r) for p in range(devices) for r in range(2)]

    kind = picture_vectors.dtype
    half_shape = jax.ShapeDtypeStruct((rows // 2, depth), kind)
    full_shape = jax.ShapeDtypeStruct((rows, depth), kind)
    own_a, own_b, fixed = pl.pallas_call(
        pick_kernel,
        out_shape=[half_shape, half_shape, full_shape],
        in_specs=[ANY, ANY],
        out_specs=[pl.BlockSpec(memory_space=pltpu.VMEM)] * 3,
        scratch_shapes=[pltpu.SemaphoreType.DMA((3,))],
        compiler_params=pltpu.CompilerParams(vmem_limit_bytes=NO_ROOM),
        cost_estimate=NO_COST,
        name="pick",
    )(picture_vectors, caption_vectors)

    tile = pl.BlockSpec((rows, depth), lambda i: (i, 0))
    down = matched_caption_index.reshape(rows, 1)

    def kernel(body, name, operands, specs, steps=2):
        return pl.pallas_call(
            body,
            grid=(steps,),
            out_shape=jax.ShapeDtypeStruct((steps * rows, depth), jnp.float32),
            in_specs=[SMEM, SMEM] + specs + [whole(x) for x in operands[len(specs) :]],
            out_specs=tile,
            scratch_shapes=[pltpu.VMEM((rows, depth), kind)] * (steps - 1),
            compiler_params=params(),
            cost_estimate=NO_COST,
            name=name,
        )(flags, scale, *operands)

    one_a, one_b = hop(own_a, to_up), hop(own_b, to_up)
    group_a = hop(own_a, to_side_1)
    other_fixed = hop(fixed, core_swap)
    one_a, fixed_late = lax.optimization_barrier((one_a, fixed))
    two_a = hop(one_a, onward)
    over_a = hop(one_a, but_2_across)
    total = kernel(
        own_kernel, "own_pairs", (down, matched_caption_index, fixed_late, own_a, own_b), [], steps=1
    )
    one_b, total = lax.optimization_barrier((one_b, total))
    two_b = hop(one_b, onward)
    over_b = hop(one_b, but_2_across)
    two_a, total = lax.optimization_barrier((two_a, total))
    total = kernel(
        second_kernel,
        "second_blocks",
        (total, fixed, other_fixed, own_a, own_b, one_a, one_b, group_a, over_a),
        [],
    )
    last_a = hop(two_a, last_step)
    two_b, own_b, total = lax.optimization_barrier((two_b, own_b, total))
    last_b = hop(two_b, last_step)
    group_b = hop(own_b, to_side_1)
    total = kernel(
        third_kernel,
        "third_blocks",
        (total, fixed, other_fixed, two_a, two_b, over_b, last_a),
        [tile],
    )

    def finish(which, left, dtype, name):
        part = pl.BlockSpec((rows, depth), lambda i: (which, 0))
        return pl.pallas_call(
            last_kernel,
            grid=(1,),
            out_shape=jax.ShapeDtypeStruct((rows, depth), dtype),
            in_specs=[SMEM, SMEM, whole(left), part, whole(group_b), whole(last_b)],
            out_specs=tile,
            scratch_shapes=[pltpu.VMEM((rows, depth), jnp.float32)],
            compiler_params=params(),
            cost_estimate=NO_COST,
            name=name,
        )(flags, scale, left, total, group_b, last_b)

    other_total = finish(1, other_fixed, jnp.bfloat16, "last_block_other")
    received = hop(other_total, core_swap)
    own_total = finish(0, fixed, jnp.float32, "last_block_own")

    mine = (score_multiplier * (own_total + received.astype(jnp.float32))).astype(jnp.bfloat16)
    theirs = hop(mine, replica_swap)
    return (
        jnp.where(first, mine, theirs).astype(jnp.float32),
        jnp.where(first, theirs, mine).astype(jnp.float32),
    )


def solution(mesh):
    placed = (P("dp", None), P("dp", None), P("dp", None), P(), P(), P())
    return jax.shard_map(
        per_device,
        mesh=mesh,
        in_specs=placed,
        out_specs=(P("dp", None), P("dp", None)),
        check_vma=False,
    )
```

time: 111 us -> 106 us (0.955)
  other arithmetic: 7.77 us -> 2.99 us
  starting transfers between devices: 31.7 us -> 27.7 us
  local copies, waits for them, and re-layouts: 0.59 us -> 3.55 us
  Pallas kernels: 23.4 us -> 25.1 us
    ppermute x13, starting transfers between devices: 31.7 us -> 27.7 us  [hop(): return lax.ppermute(x, ('dp', 'rep'), pairs)]
    pallas_call x0 -> x1, Pallas kernels: none -> 3.07 us  [per_device(): pl.pallas_call(pick_kernel, out_shape=[half_shape, half_shape, full_shape...]
    select_n x2 -> x0, other arithmetic: 3.02 us -> none  [the longest x1 1.88 us: per_device(): jnp.where(first, caption_vectors[x], picture_vectors[x])]
    unnamed x6 -> x10, local copies, waits for them, and re-layouts: 0.44 us -> 3.4 us
    concatenate x1 -> x0, other arithmetic: 1.81 us -> none  [per_device(): both = jnp.concatenate([fixed, other_fixed], axis=0)]
    pallas_call x3, Pallas kernels: 18.6 us -> 17.1 us  [kernel(): pl.pallas_call(body, grid=(steps,), out_shape=jax.ShapeDtypeStruct((steps...]
  transfers between devices with their start and end apart: 13 -> 13, of which waited for: 6 -> 7; matrix products, arithmetic and copies ran while one was open for 2% -> 0% of each run, Pallas kernels for 19% -> 19%
where the time goes in v3:
time: 106 us; the launch traced here: 105 us
  waiting for transfers between devices  42.9 us (40%)
  starting transfers between devices  27.7 us (26%)
  Pallas kernels  25.1 us (24%)
  local copies, waits for them, and re-layouts  3.55 us (3%)
  other arithmetic  2.99 us (3%)
  between operations  2.86 us (3%)
    ppermute x13, waiting for transfers between devices, hop(): return lax.ppermute(x, ('dp', 'rep'), pairs)  42.9 us
    ppermute x13, starting transfers between devices, hop(): return lax.ppermute(x, ('dp', 'rep'), pairs)  27.7 us
    pallas_call x3, Pallas kernels, kernel(): pl.pallas_call(body, grid=(steps,), out_shape=jax.ShapeDtypeStruct((steps...  17.1 us
    pallas_call x2, Pallas kernels, finish(): pl.pallas_call(last_kernel, grid=(1,), out_shape=jax.ShapeDtypeStruct((ro...  4.92 us
    unnamed x10, local copies, waits for them, and re-layouts  3.4 us
    pallas_call x1, Pallas kernels, per_device(): pl.pallas_call(pick_kernel, out_shape=[half_shape, half_shape, full_shape...  3.07 us
    convert_element_type x1, other arithmetic, per_device(): jnp.where(first, theirs, mine).astype(jnp.float32)  2.49 us
  transfers between devices with their start and end apart: 13, of which 7 were waited for; matrix products, arithmetic and copies ran while one was open for 0% of the time, Pallas kernels for 19%

profile of v3, /device:TPU:0, one launch (start us, length us, event | category | flops | bytes accessed | tf_op | source)
XLA Modules:
  0.0 105.1 jit_solution(15659400446433262385)
XLA Ops:
  0.6 0.0 copy-start.4
  0.6 3.1 %pick.1 = (bf16[256,1152]{1,0:T(8,128)(2,1)}, bf16[256,1152]{1,0:T(8,128)(2,1)}, bf16[512,1152]{1,0:T(8,128)(2,1)}) custom-call(bf16[512,1152]{1,0:T(8,128)(2,1)} %image_ref.1, bf16[512,1152]{1,0:T(8,128)(2,1)} %text_ref.1), custom_call_target="tpu_custom_call" | custom-call | flops 1 | bytes 1 | tf_op jit(solution)/shard_map/pick/pallas_call | solution.py:219
  3.7 3.1 %collective-permute-start.1 = (bf16[256,1152]{1,0:T(8,128)(2,1)}, bf16[256,1152]{1,0:T(8,128)(2,1)S(1)}, u32[]{:S(2)}, u32[]{:S(2)}) collective-permute-start(bf16[256,1152]{1,0:T(8,128)(2,1)} %get-tuple-element.16.own_a_ref.own_a), channel_id=1, source_target_pairs={{0,8},{31,23},{2,10},{29,21},{4,12},{27,19},{6,14},{25,17},{8,16},... | collective-permute-start | bytes 1769480 | tf_op jit(solution)/shard_map/ppermute | solution.py:16
  6.8 1.6 %collective-permute-start = (bf16[256,1152]{1,0:T(8,128)(2,1)}, bf16[256,1152]{1,0:T(8,128)(2,1)S(1)}, u32[]{:S(2)}, u32[]{:S(2)}) collective-permute-start(bf16[256,1152]{1,0:T(8,128)(2,1)} %get-tuple-element.25.own_b_ref.own_b), channel_id=1, source_target_pairs={{0,8},{31,23},{2,10},{29,21},{4,12},{27,19},{6,14},{25,17},{8,16},... | collective-permute-start | bytes 1769480 | tf_op jit(solution)/shard_map/ppermute | solution.py:16
  8.4 0.0 collective-permute-start.4
  8.4 4.3 %collective-permute-start.5 = (bf16[256,1152]{1,0:T(8,128)(2,1)}, bf16[256,1152]{1,0:T(8,128)(2,1)}, u32[]{:S(2)}, u32[]{:S(2)}) collective-permute-start(bf16[256,1152]{1,0:T(8,128)(2,1)} %get-tuple-element.16.own_a_ref.own_a), channel_id=1, source_target_pairs={{0,4},{31,27},{2,6},{29,25},{8,12},{23,19},{10,14},{21,17},{16,20}... | collective-permute-start | bytes 1769480 | tf_op jit(solution)/shard_map/ppermute | solution.py:16
  14.7 0.1 pad_add_fusion.flag_ref
  14.7 8.5 %collective-permute-done.1.one_a = bf16[256,1152]{1,0:T(8,128)(2,1)S(1)} collective-permute-done((bf16[256,1152]{1,0:T(8,128)(2,1)}, bf16[256,1152]{1,0:T(8,128)(2,1)S(1)}, u32[]{:S(2)}, u32[]{:S(2)}) %collective-permute-start.1) | collective-permute-done | bytes 589856 | tf_op jit(solution)/shard_map/ppermute | solution.py:16
  23.2 1.3 %collective-permute-start.3 = (bf16[256,1152]{1,0:T(8,128)(2,1)S(1)}, bf16[256,1152]{1,0:T(8,128)(2,1)S(1)}, u32[]{:S(2)}, u32[]{:S(2)}) collective-permute-start(bf16[256,1152]{1,0:T(8,128)(2,1)S(1)} %collective-permute-done.1.one_a), channel_id=1, source_target_pairs={{2,10},{29,21},{6,14},{25,17},{10,18},{21,13},{14,22},{17,9},{18,2... | collective-permute-start | bytes 1769480 | tf_op jit(solution)/shard_map/ppermute | solution.py:16
  24.5 0.1 pad_maximum_fusion.scale_ref
  24.6 0.0 copy-done.4
  24.6 0.1 copy.8.down_ref
  24.7 4.6 %collective-permute-start.6 = (bf16[256,1152]{1,0:T(8,128)(2,1)S(1)}, bf16[256,1152]{1,0:T(8,128)(2,1)S(1)}, u32[]{:S(2)}, u32[]{:S(2)}) collective-permute-start(bf16[256,1152]{1,0:T(8,128)(2,1)S(1)} %collective-permute-done.1.one_a), channel_id=1, source_target_pairs={{0,4},{31,27},{2,6},{29,25},{6,2},{25,29},{8,12},{23,19},{10,14},{... | collective-permute-start | bytes 1769480 | tf_op jit(solution)/shard_map/ppermute | solution.py:16
  29.3 0.0 copy-start
  29.3 1.3 %copy-done = bf16[512,1152]{1,0:T(8,128)(2,1)S(1)} copy-done((bf16[512,1152]{1,0:T(8,128)(2,1)S(1)}, bf16[512,1152]{1,0:T(8,128)(2,1)}, u32[]{:S(2)}) %copy-start) | copy-done | bytes 1179672
  30.6 0.0 copy-start.2
  30.6 1.1 %copy-done.2 = bf16[256,1152]{1,0:T(8,128)(2,1)S(1)} copy-done((bf16[256,1152]{1,0:T(8,128)(2,1)S(1)}, bf16[256,1152]{1,0:T(8,128)(2,1)}, u32[]{:S(2)}) %copy-start.2) | copy-done | bytes 589848
  31.7 0.0 copy-start.3
  31.7 1.1 %copy-done.3 = bf16[256,1152]{1,0:T(8,128)(2,1)S(1)} copy-done((bf16[256,1152]{1,0:T(8,128)(2,1)S(1)}, bf16[256,1152]{1,0:T(8,128)(2,1)}, u32[]{:S(2)}) %copy-start.3) | copy-done | bytes 589848
  32.7 2.4 %own_pairs.1.sum_ref = f32[512,1152]{1,0:T(8,128)S(1)} custom-call(s32[3]{0:T(128)S(1)} %pad_add_fusion.flag_ref, f32[4]{0:T(128)S(1)} %pad_maximum_fusion.scale_ref, s32[512,1]{1,0:T(8,128)S(1)} %copy.8.down_ref, s32[1,512]{1,0:T(1,128)S(1)} %copy-done.4, bf16[512,1152]{1,0:T(8,128)(2,1)S(1)} %copy-done, bf16[256,1152]{1,0:T(8,128)(2,1)S(1)} %copy-done.3, ...), custom_call_target="tpu_custom_call" | custom-call | flops 1 | bytes 1 | tf_op jit(solution)/shard_map/own_pairs/pallas_call | solution.py:234
  35.1 0.0 copy-start.1
  35.1 0.7 collective-permute-done.one_b
  35.8 1.3 %collective-permute-start.2 = (bf16[256,1152]{1,0:T(8,128)(2,1)S(1)}, bf16[256,1152]{1,0:T(8,128)(2,1)S(1)}, u32[]{:S(2)}, u32[]{:S(2)}) collective-permute-start(bf16[256,1152]{1,0:T(8,128)(2,1)S(1)} %collective-permute-done.one_b), channel_id=1, source_target_pairs={{2,10},{29,21},{6,14},{25,17},{10,18},{21,13},{14,22},{17,9},{18,2... | collective-permute-start | bytes 1769480 | tf_op jit(solution)/shard_map/ppermute | solution.py:16
  37.1 3.8 %collective-permute-done.3.two_a = bf16[256,1152]{1,0:T(8,128)(2,1)S(1)} collective-permute-done((bf16[256,1152]{1,0:T(8,128)(2,1)S(1)}, bf16[256,1152]{1,0:T(8,128)(2,1)S(1)}, u32[]{:S(2)}, u32[]{:S(2)}) %collective-permute-start.3) | collective-permute-done | bytes 589856 | tf_op jit(solution)/shard_map/ppermute | solution.py:16
  40.9 1.5 %collective-permute-start.7 = (bf16[256,1152]{1,0:T(8,128)(2,1)S(1)}, bf16[256,1152]{1,0:T(8,128)(2,1)S(1)}, u32[]{:S(2)}, u32[]{:S(2)}) collective-permute-start(bf16[256,1152]{1,0:T(8,128)(2,1)S(1)} %collective-permute-done.one_b), channel_id=1, source_target_pairs={{0,4},{31,27},{2,6},{29,25},{6,2},{25,29},{8,12},{23,19},{10,14},{... | collective-permute-start | bytes 1769480 | tf_op jit(solution)/shard_map/ppermute | solution.py:16
  42.4 0.0 collective-permute-done.5.group
  42.4 2.0 %collective-permute-start.8 = (bf16[256,1152]{1,0:T(8,128)(2,1)S(1)}, bf16[256,1152]{1,0:T(8,128)(2,1)S(1)}, u32[]{:S(2)}, u32[]{:S(2)}) collective-permute-start(bf16[256,1152]{1,0:T(8,128)(2,1)S(1)} %collective-permute-done.3.two_a), channel_id=1, source_target_pairs={{0,8},{31,23},{8,16},{23,15},{16,24},{15,7},{24,0},{7,31},{6,2},{2... | collective-permute-start | bytes 1769480 | tf_op jit(solution)/shard_map/ppermute | solution.py:16
  44.4 0.0 collective-permute-done.6.over
  44.4 0.0 collective-permute-done.4.other_ref.left_ref
  44.4 6.8 %second_blocks.1.sum_ref = f32[1024,1152]{1,0:T(8,128)S(1)} custom-call(s32[3]{0:T(128)S(1)} %pad_add_fusion.flag_ref, f32[4]{0:T(128)S(1)} %pad_maximum_fusion.scale_ref, f32[512,1152]{1,0:T(8,128)S(1)} %own_pairs.1.sum_ref, bf16[512,1152]{1,0:T(8,128)(2,1)S(1)} %copy-done, bf16[512,1152]{1,0:T(8,128)(2,1)S(1)} %collective-permute-done.4.other_ref.left_ref, ...), custom_call_target="tpu_custom_call" | custom-call | flops 1 | bytes 1 | tf_op jit(solution)/shard_map/second_blocks/pallas_call | solution.py:234
  51.2 0.0 collective-permute-done.2.two_b
  51.2 3.5 %collective-permute-start.9 = (bf16[256,1152]{1,0:T(8,128)(2,1)S(1)}, bf16[256,1152]{1,0:T(8,128)(2,1)S(1)}, u32[]{:S(2)}, u32[]{:S(2)}) collective-permute-start(bf16[256,1152]{1,0:T(8,128)(2,1)S(1)} %copy-done.2), channel_id=1, source_target_pairs={{0,4},{31,27},{2,6},{29,25},{8,12},{23,19},{10,14},{21,17},{16,20}... | collective-permute-start | bytes 1769480 | tf_op jit(solution)/shard_map/ppermute | solution.py:16
  54.7 2.6 %collective-permute-start.10 = (bf16[256,1152]{1,0:T(8,128)(2,1)S(1)}, bf16[256,1152]{1,0:T(8,128)(2,1)S(1)}, u32[]{:S(2)}, u32[]{:S(2)}) collective-permute-start(bf16[256,1152]{1,0:T(8,128)(2,1)S(1)} %collective-permute-done.2.two_b), channel_id=1, source_target_pairs={{0,8},{31,23},{8,16},{23,15},{16,24},{15,7},{24,0},{7,31},{6,2},{2... | collective-permute-start | bytes 1769480 | tf_op jit(solution)/shard_map/ppermute | solution.py:16
  57.3 0.0 collective-permute-done.7.over
  57.3 0.0 collective-permute-done.8.last
  57.3 0.0 copy-done.1
  57.3 7.9 %third_blocks.1.sum_ref = f32[1024,1152]{1,0:T(8,128)S(1)} custom-call(s32[3]{0:T(128)S(1)} %pad_add_fusion.flag_ref, f32[4]{0:T(128)S(1)} %pad_maximum_fusion.scale_ref, f32[1024,1152]{1,0:T(8,128)S(1)} %second_blocks.1.sum_ref, bf16[512,1152]{1,0:T(8,128)(2,1)S(1)} %copy-done.1, bf16[512,1152]{1,0:T(8,128)(2,1)S(1)} %collective-permute-done.4.other_ref.left_ref, ...), custom_call_target="tpu_custom_call" | custom-call | flops 1 | bytes 1 | tf_op jit(solution)/shard_map/third_blocks/pallas_call | solution.py:234
  65.3 0.9 collective-permute-done.9.group
  66.2 2.1 %collective-permute-done.10.last = bf16[256,1152]{1,0:T(8,128)(2,1)S(1)} collective-permute-done((bf16[256,1152]{1,0:T(8,128)(2,1)S(1)}, bf16[256,1152]{1,0:T(8,128)(2,1)S(1)}, u32[]{:S(2)}, u32[]{:S(2)}) %collective-permute-start.10) | collective-permute-done | bytes 589856 | tf_op jit(solution)/shard_map/ppermute | solution.py:16
  68.3 2.5 %last_block_other.1 = bf16[512,1152]{1,0:T(8,128)(2,1)S(1)} custom-call(s32[3]{0:T(128)S(1)} %pad_add_fusion.flag_ref, f32[4]{0:T(128)S(1)} %pad_maximum_fusion.scale_ref, bf16[512,1152]{1,0:T(8,128)(2,1)S(1)} %collective-permute-done.4.other_ref.left_ref, f32[1024,1152]{1,0:T(8,128)S(1)} %third_blocks.1.sum_ref, ...), custom_call_target="tpu_custom_call" | custom-call | flops 1 | bytes 1 | tf_op jit(solution)/shard_map/last_block_other/pallas_call | solution.py:278
  70.8 0.6 collective-permute-start.11
  71.4 2.4 %last_block_own.1 = f32[512,1152]{1,0:T(8,128)S(1)} custom-call(s32[3]{0:T(128)S(1)} %pad_add_fusion.flag_ref, f32[4]{0:T(128)S(1)} %pad_maximum_fusion.scale_ref, bf16[512,1152]{1,0:T(8,128)(2,1)S(1)} %copy-done.1, f32[1024,1152]{1,0:T(8,128)S(1)} %third_blocks.1.sum_ref, bf16[256,1152]{1,0:T(8,128)(2,1)S(1)} %collective-permute-done.9.group, ...), custom_call_target="tpu_custom_call" | custom-call | flops 1 | bytes 1 | tf_op jit(solution)/shard_map/last_block_own/pallas_call | solution.py:278
  73.8 0.1 collective-permute-done.11
  73.9 0.3 multiply_convert_fusion
  74.3 1.4 %collective-permute-start.12 = (bf16[512,1152]{1,0:T(8,128)(2,1)S(1)}, bf16[512,1152]{1,0:T(8,128)(2,1)S(1)}, u32[]{:S(2)}, u32[]{:S(2)}) collective-permute-start(bf16[512,1152]{1,0:T(8,128)(2,1)S(1)} %multiply_convert_fusion), channel_id=1, source_target_pairs={{0,1},{1,0},{2,3},{3,2},{4,5},{5,4},{6,7},{7,6},{8,9},{9,8},{10,11... | collective-permute-start | bytes 3538952 | tf_op jit(solution)/shard_map/ppermute | solution.py:16
  75.7 26.9 %collective-permute-done.12 = bf16[512,1152]{1,0:T(8,128)(2,1)S(1)} collective-permute-done((bf16[512,1152]{1,0:T(8,128)(2,1)S(1)}, bf16[512,1152]{1,0:T(8,128)(2,1)S(1)}, u32[]{:S(2)}, u32[]{:S(2)}) %collective-permute-start.12) | collective-permute-done | bytes 1179680 | tf_op jit(solution)/shard_map/ppermute | solution.py:16
  102.6 2.5 %select_convert_fusion = (f32[512,1152]{1,0:T(8,128)}, f32[512,1152]{1,0:T(8,128)}) fusion(bf16[512,1152]{1,0:T(8,128)(2,1)S(1)} %collective-permute-done.12, bf16[512,1152]{1,0:T(8,128)(2,1)S(1)} %multiply_convert_fusion, pred[]{:T(512)S(6)} %eq.3), kind=kLoop, calls=%fused_computation.1 | loop fusion | flops 2359296 | bytes 7077889 | tf_op jit(solution)/shard_map/convert_element_type | solution.py:298
Async XLA Ops:
  0.6 23.9 %copy-start.4 = (s32[1,512]{1,0:T(1,128)S(1)}, s32[1,512]{1,0:T(1,128)}, u32[]{:S(2)}) copy-start(s32[1,512]{1,0:T(1,128)} %along_ref.1) | copy-start | bytes 6148
  3.7 19.5 %collective-permute-start.1 = (bf16[256,1152]{1,0:T(8,128)(2,1)}, bf16[256,1152]{1,0:T(8,128)(2,1)S(1)}, u32[]{:S(2)}, u32[]{:S(2)}) collective-permute-start(bf16[256,1152]{1,0:T(8,128)(2,1)} %get-tuple-element.16.own_a_ref.own_a), channel_id=1, source_target_pairs={{0,8},{31,23},{2,10},{29,21},{4,12},{27,19},{6,14},{25,17},{8,16},... | collective-permute-start | bytes 1769480 | tf_op jit(solution)/shard_map/ppermute | solution.py:16
  6.8 29.0 %collective-permute-start = (bf16[256,1152]{1,0:T(8,128)(2,1)}, bf16[256,1152]{1,0:T(8,128)(2,1)S(1)}, u32[]{:S(2)}, u32[]{:S(2)}) collective-permute-start(bf16[256,1152]{1,0:T(8,128)(2,1)} %get-tuple-element.25.own_b_ref.own_b), channel_id=1, source_target_pairs={{0,8},{31,23},{2,10},{29,21},{4,12},{27,19},{6,14},{25,17},{8,16},... | collective-permute-start | bytes 1769480 | tf_op jit(solution)/shard_map/ppermute | solution.py:16
  8.4 36.1 %collective-permute-start.4 = (bf16[512,1152]{1,0:T(8,128)(2,1)}, bf16[512,1152]{1,0:T(8,128)(2,1)S(1)}, u32[]{:S(2)}, u32[]{:S(2)}) collective-permute-start(bf16[512,1152]{1,0:T(8,128)(2,1)} %get-tuple-element.17.left_ref.fixed_ref), channel_id=1, source_target_pairs={{0,2},{31,29},{2,0},{29,31},{4,6},{27,25},{6,4},{25,27},{8,10},{23... | collective-permute-start | bytes 3538952 | tf_op jit(solution)/shard_map/ppermute | solution.py:16
  8.4 34.0 %collective-permute-start.5 = (bf16[256,1152]{1,0:T(8,128)(2,1)}, bf16[256,1152]{1,0:T(8,128)(2,1)}, u32[]{:S(2)}, u32[]{:S(2)}) collective-permute-start(bf16[256,1152]{1,0:T(8,128)(2,1)} %get-tuple-element.16.own_a_ref.own_a), channel_id=1, source_target_pairs={{0,4},{31,27},{2,6},{29,25},{8,12},{23,19},{10,14},{21,17},{16,20}... | collective-permute-start | bytes 1769480 | tf_op jit(solution)/shard_map/ppermute | solution.py:16
  23.2 17.7 %collective-permute-start.3 = (bf16[256,1152]{1,0:T(8,128)(2,1)S(1)}, bf16[256,1152]{1,0:T(8,128)(2,1)S(1)}, u32[]{:S(2)}, u32[]{:S(2)}) collective-permute-start(bf16[256,1152]{1,0:T(8,128)(2,1)S(1)} %collective-permute-done.1.one_a), channel_id=1, source_target_pairs={{2,10},{29,21},{6,14},{25,17},{10,18},{21,13},{14,22},{17,9},{18,2... | collective-permute-start | bytes 1769480 | tf_op jit(solution)/shard_map/ppermute | solution.py:16
  24.7 19.7 %collective-permute-start.6 = (bf16[256,1152]{1,0:T(8,128)(2,1)S(1)}, bf16[256,1152]{1,0:T(8,128)(2,1)S(1)}, u32[]{:S(2)}, u32[]{:S(2)}) collective-permute-start(bf16[256,1152]{1,0:T(8,128)(2,1)S(1)} %collective-permute-done.1.one_a), channel_id=1, source_target_pairs={{0,4},{31,27},{2,6},{29,25},{6,2},{25,29},{8,12},{23,19},{10,14},{... | collective-permute-start | bytes 1769480 | tf_op jit(solution)/shard_map/ppermute | solution.py:16
  29.3 1.3 %copy-start = (bf16[512,1152]{1,0:T(8,128)(2,1)S(1)}, bf16[512,1152]{1,0:T(8,128)(2,1)}, u32[]{:S(2)}) copy-start(bf16[512,1152]{1,0:T(8,128)(2,1)} %get-tuple-element.17.left_ref.fixed_ref) | copy-start | bytes 3538948
  30.6 1.1 %copy-start.2 = (bf16[256,1152]{1,0:T(8,128)(2,1)S(1)}, bf16[256,1152]{1,0:T(8,128)(2,1)}, u32[]{:S(2)}) copy-start(bf16[256,1152]{1,0:T(8,128)(2,1)} %get-tuple-element.25.own_b_ref.own_b) | copy-start | bytes 1769476
  31.7 1.1 %copy-start.3 = (bf16[256,1152]{1,0:T(8,128)(2,1)S(1)}, bf16[256,1152]{1,0:T(8,128)(2,1)}, u32[]{:S(2)}) copy-start(bf16[256,1152]{1,0:T(8,128)(2,1)} %get-tuple-element.16.own_a_ref.own_a) | copy-start | bytes 1769476
  35.1 22.2 %copy-start.1 = (bf16[512,1152]{1,0:T(8,128)(2,1)S(1)}, bf16[512,1152]{1,0:T(8,128)(2,1)}, u32[]{:S(2)}) copy-start(bf16[512,1152]{1,0:T(8,128)(2,1)} %get-tuple-element.17.left_ref.fixed_ref) | copy-start | bytes 3538948
  35.8 15.4 %collective-permute-start.2 = (bf16[256,1152]{1,0:T(8,128)(2,1)S(1)}, bf16[256,1152]{1,0:T(8,128)(2,1)S(1)}, u32[]{:S(2)}, u32[]{:S(2)}) collective-permute-start(bf16[256,1152]{1,0:T(8,128)(2,1)S(1)} %collective-permute-done.one_b), channel_id=1, source_target_pairs={{2,10},{29,21},{6,14},{25,17},{10,18},{21,13},{14,22},{17,9},{18,2... | collective-permute-start | bytes 1769480 | tf_op jit(solution)/shard_map/ppermute | solution.py:16
  40.9 16.4 %collective-permute-start.7 = (bf16[256,1152]{1,0:T(8,128)(2,1)S(1)}, bf16[256,1152]{1,0:T(8,128)(2,1)S(1)}, u32[]{:S(2)}, u32[]{:S(2)}) collective-permute-start(bf16[256,1152]{1,0:T(8,128)(2,1)S(1)} %collective-permute-done.one_b), channel_id=1, source_target_pairs={{0,4},{31,27},{2,6},{29,25},{6,2},{25,29},{8,12},{23,19},{10,14},{... | collective-permute-start | bytes 1769480 | tf_op jit(solution)/shard_map/ppermute | solution.py:16
  42.4 14.9 %collective-permute-start.8 = (bf16[256,1152]{1,0:T(8,128)(2,1)S(1)}, bf16[256,1152]{1,0:T(8,128)(2,1)S(1)}, u32[]{:S(2)}, u32[]{:S(2)}) collective-permute-start(bf16[256,1152]{1,0:T(8,128)(2,1)S(1)} %collective-permute-done.3.two_a), channel_id=1, source_target_pairs={{0,8},{31,23},{8,16},{23,15},{16,24},{15,7},{24,0},{7,31},{6,2},{2... | collective-permute-start | bytes 1769480 | tf_op jit(solution)/shard_map/ppermute | solution.py:16
  51.2 15.0 %collective-permute-start.9 = (bf16[256,1152]{1,0:T(8,128)(2,1)S(1)}, bf16[256,1152]{1,0:T(8,128)(2,1)S(1)}, u32[]{:S(2)}, u32[]{:S(2)}) collective-permute-start(bf16[256,1152]{1,0:T(8,128)(2,1)S(1)} %copy-done.2), channel_id=1, source_target_pairs={{0,4},{31,27},{2,6},{29,25},{8,12},{23,19},{10,14},{21,17},{16,20}... | collective-permute-start | bytes 1769480 | tf_op jit(solution)/shard_map/ppermute | solution.py:16
  54.7 13.6 %collective-permute-start.10 = (bf16[256,1152]{1,0:T(8,128)(2,1)S(1)}, bf16[256,1152]{1,0:T(8,128)(2,1)S(1)}, u32[]{:S(2)}, u32[]{:S(2)}) collective-permute-start(bf16[256,1152]{1,0:T(8,128)(2,1)S(1)} %collective-permute-done.2.two_b), channel_id=1, source_target_pairs={{0,8},{31,23},{8,16},{23,15},{16,24},{15,7},{24,0},{7,31},{6,2},{2... | collective-permute-start | bytes 1769480 | tf_op jit(solution)/shard_map/ppermute | solution.py:16
  70.8 3.1 %collective-permute-start.11 = (bf16[512,1152]{1,0:T(8,128)(2,1)S(1)}, bf16[512,1152]{1,0:T(8,128)(2,1)S(1)}, u32[]{:S(2)}, u32[]{:S(2)}) collective-permute-start(bf16[512,1152]{1,0:T(8,128)(2,1)S(1)} %last_block_other.1), channel_id=1, source_target_pairs={{0,2},{31,29},{2,0},{29,31},{4,6},{27,25},{6,4},{25,27},{8,10},{23... | collective-permute-start | bytes 3538952 | tf_op jit(solution)/shard_map/ppermute | solution.py:16
  74.3 28.3 %collective-permute-start.12 = (bf16[512,1152]{1,0:T(8,128)(2,1)S(1)}, bf16[512,1152]{1,0:T(8,128)(2,1)S(1)}, u32[]{:S(2)}, u32[]{:S(2)}) collective-permute-start(bf16[512,1152]{1,0:T(8,128)(2,1)S(1)} %multiply_convert_fusion), channel_id=1, source_target_pairs={{0,1},{1,0},{2,3},{3,2},{4,5},{5,4},{6,7},{7,6},{8,9},{9,8},{10,11... | collective-permute-start | bytes 3538952 | tf_op jit(solution)/shard_map/ppermute | solution.py:16

commit v4 on v3

v4 whole, which is shorter than its diff:
```python
import functools

import jax
import jax.numpy as jnp
from jax import lax
from jax.experimental import pallas as pl
from jax.experimental.pallas import tpu as pltpu
from jax.sharding import PartitionSpec as P

GROUP = 4
VMEM_BYTES = 36 * 1024 * 1024
NO_ROOM = 60 * 1024 * 1024
PICK_BYTES = NO_ROOM

FIRST, CORE, SIDE = 0, 1, 2


def hop(x, pairs):
    return lax.ppermute(x, ("dp", "rep"), pairs)


def pairs_of(devices, target, members):
    pairs = []
    for p in range(devices):
        if p % GROUP in members:
            q = target(p)
            pairs.append((2 * p, 2 * q))
            pairs.append((2 * (devices - 1 - p) + 1, 2 * (devices - 1 - q) + 1))
    return pairs


def grads_of(scale_ref, left, block, match=None):
    product = lax.dot_general(
        left, block, (((1,), (1,)), ((), ())), preferred_element_type=jnp.float32
    )
    value = 1.0 / (scale_ref[2] + jnp.exp2(scale_ref[0] * product + scale_ref[1]))
    if match is not None:
        value = value - scale_ref[3] * match
    return value.astype(jnp.bfloat16)


def add_block(scale_ref, left_ref, refs, out_ref, match=None, fresh=False):
    block = jnp.concatenate([ref[...] for ref in refs], axis=0) if len(refs) > 1 else refs[0][...]
    grads = grads_of(scale_ref, left_ref[...], block, match)
    part = jnp.dot(grads, block, preferred_element_type=jnp.float32)
    out_ref[...] = part if fresh else out_ref[...] + part


PIECES = 4


def copy_all(pairs, sems):
    moves = []
    for source, target in pairs:
        size = source.shape[0] // PIECES
        for k in range(PIECES):
            part = pl.ds(k * size, size)
            moves.append(
                pltpu.make_async_copy(source.at[part], target.at[part], sems.at[len(moves)])
            )
    for move in moves:
        move.start()
    for move in moves:
        move.wait()


def pick_first_kernel(image_ref, text_ref, own_a_ref, sems):
    part = pl.ds(0, own_a_ref.shape[0])
    first = lax.axis_index("rep") == 0

    @pl.when(first)
    def _():
        copy_all([(text_ref.at[part], own_a_ref)], sems)

    @pl.when(jnp.logical_not(first))
    def _():
        copy_all([(image_ref.at[part], own_a_ref)], sems)


def pick_rest_kernel(image_ref, text_ref, own_a_ref, own_b_ref, fixed_ref, sems):
    part = pl.ds(own_b_ref.shape[0], own_b_ref.shape[0])
    first = lax.axis_index("rep") == 0

    @pl.when(first)
    def _():
        copy_all([(text_ref.at[part], own_b_ref), (image_ref, fixed_ref)], sems)

    @pl.when(jnp.logical_not(first))
    def _():
        copy_all([(image_ref.at[part], own_b_ref), (text_ref, fixed_ref)], sems)


def write_kernel(picture_step, start, count, *refs):
    value_refs = refs[:count]
    picture_ref, caption_ref, wide_ref, sems = refs[-4:]
    to_picture = (lax.axis_index("rep") == 0) == picture_step
    size = value_refs[0].shape[0] // PIECES

    def write(target):
        moves = []
        for value_ref in value_refs:
            for k in range(PIECES):
                place = pl.ds(len(moves) * size, size)
                wide_ref[place] = value_ref[pl.ds(k * size, size)].astype(jnp.float32)
                there = target.at[pl.ds(start + len(moves) * size, size)]
                moves.append(
                    pltpu.make_async_copy(wide_ref.at[place], there, sems.at[len(moves)])
                )
                moves[-1].start()
        for move in moves:
            move.wait()

    @pl.when(to_picture)
    def _():
        write(picture_ref)

    @pl.when(jnp.logical_not(to_picture))
    def _():
        write(caption_ref)


def halves(total_ref):
    rows = total_ref.shape[0] // 2
    return total_ref.at[pl.ds(0, rows)], total_ref.at[pl.ds(rows, rows)]


def own_kernel(flag_ref, scale_ref, down_ref, along_ref, fixed_ref, own_a, own_b, total_ref):
    mine, others = halves(total_ref)
    shape = (fixed_ref.shape[0], along_ref.shape[1])
    column = lax.broadcasted_iota(jnp.int32, shape, 1)
    row = lax.broadcasted_iota(jnp.int32, shape, 0)
    straight = (column == down_ref[...]).astype(jnp.float32)
    turned = (row == along_ref[...]).astype(jnp.float32)
    match = jnp.where(flag_ref[FIRST] == 1, straight, turned)
    add_block(scale_ref, fixed_ref, [own_a, own_b], mine, match, fresh=True)
    others[...] = jnp.zeros_like(others)


def halves_kernel(flag_ref, scale_ref, _, fixed_ref, other_ref, half_ref, group_ref, total_ref):
    mine, others = halves(total_ref)
    add_block(scale_ref, fixed_ref, [half_ref, group_ref], mine)
    add_block(scale_ref, other_ref, [half_ref, group_ref], others)


def first_halves_kernel(
    flag_ref, scale_ref, _, fixed_ref, other_ref, half_ref, group_ref, own_a, own_b, total_ref
):
    halves_kernel(flag_ref, scale_ref, _, fixed_ref, other_ref, half_ref, group_ref, total_ref)

    @pl.when(flag_ref[CORE] == 0)
    def _():
        add_block(scale_ref, other_ref, [own_a, own_b], halves(total_ref)[1])


def two_kernel(flag_ref, scale_ref, _, fixed_ref, other_ref, two_a, two_b, total_ref):
    mine, others = halves(total_ref)
    core, side = flag_ref[CORE], flag_ref[SIDE]

    @pl.when(core + side == 0)
    def _():
        add_block(scale_ref, fixed_ref, [two_a, two_b], mine)

    @pl.when(jnp.logical_or(core == 1, side == 0))
    def _():
        add_block(scale_ref, other_ref, [two_a, two_b], others)


def last_sum(flag_ref, scale_ref, rows_ref, sum_ref, group_ref, last_ref, total_ref):
    total_ref[...] = sum_ref[...]

    @pl.when(flag_ref[SIDE] == 0)
    def _():
        add_block(scale_ref, rows_ref, [last_ref], total_ref)

    @pl.when(flag_ref[SIDE] == 1)
    def _():
        add_block(scale_ref, rows_ref, [group_ref], total_ref)


def last_other_kernel(
    start, flag_ref, scale_ref, sum_ref, other_ref, group_ref, last_ref, out_ref, total_ref
):
    part = pl.ds(start, out_ref.shape[0])
    rows_ref, sums_ref = other_ref.at[part], halves(sum_ref)[1].at[part]
    last_sum(flag_ref, scale_ref, rows_ref, sums_ref, group_ref, last_ref, total_ref)
    out_ref[...] = total_ref[...].astype(out_ref.dtype)


def last_own_kernel(
    start, flag_ref, scale_ref, sum_ref, fixed_ref, group_ref, last_ref, came_ref, out_ref, total_ref
):
    part = pl.ds(start, out_ref.shape[0])
    rows_ref, sums_ref = fixed_ref.at[part], halves(sum_ref)[0].at[part]
    last_sum(flag_ref, scale_ref, rows_ref, sums_ref, group_ref, last_ref, total_ref)
    whole_sum = total_ref[...] + came_ref[...].astype(jnp.float32)
    out_ref[...] = (scale_ref[4] * whole_sum).astype(out_ref.dtype)


def params():
    return pltpu.CompilerParams(vmem_limit_bytes=VMEM_BYTES)


NO_COST = pl.CostEstimate(flops=1, bytes_accessed=1, transcendentals=0)
SMEM = pl.BlockSpec(memory_space=pltpu.SMEM)
ANY = pl.BlockSpec(memory_space=pl.ANY)


def per_device(
    picture_vectors,
    caption_vectors,
    matched_caption_index,
    score_multiplier,
    score_offset,
    objective_cotangent,
):
    rows, depth = picture_vectors.shape
    devices = lax.axis_size("dp")
    first = lax.axis_index("rep") == 0
    place = lax.axis_index("dp")
    place = jnp.where(first, place, devices - 1 - place)
    flags = jnp.stack([first.astype(jnp.int32), place & 1, (place >> 1) & 1])
    log2e = 1.4426950408889634
    scale = jnp.stack(
        [
            -log2e * score_multiplier,
            -log2e * score_offset - jnp.log2(objective_cotangent),
            1.0 / objective_cotangent,
            objective_cotangent,
            score_multiplier,
        ]
    )

    def up(p):
        return (p + GROUP) % devices

    def across(p):
        return p ^ 2

    def swapped(p):
        return p ^ 1

    to_up = pairs_of(devices, up, (0, 1, 2, 3))
    to_side_1 = pairs_of(devices, across, (0, 1))
    but_2_across = pairs_of(devices, across, (0, 1, 3))
    onward = pairs_of(devices, up, (1, 3)) + pairs_of(devices, across, (2,))
    last_step = pairs_of(devices, up, (0,)) + pairs_of(devices, across, (3,))
    core_swap = pairs_of(devices, swapped, (0, 1, 2, 3))
    replica_swap = [(2 * p + r, 2 * p + 1 - r) for p in range(devices) for r in range(2)]

    kind = picture_vectors.dtype
    half = rows // 2
    half_shape = jax.ShapeDtypeStruct((half, depth), kind)
    full_shape = jax.ShapeDtypeStruct((rows, depth), kind)
    vmem = pl.BlockSpec(memory_space=pltpu.VMEM)
    arrays = (picture_vectors, caption_vectors)
    own_a = pl.pallas_call(
        pick_first_kernel,
        out_shape=half_shape,
        in_specs=[ANY, ANY],
        out_specs=vmem,
        scratch_shapes=[pltpu.SemaphoreType.DMA((PIECES,))],
        compiler_params=pltpu.CompilerParams(vmem_limit_bytes=PICK_BYTES),
        cost_estimate=NO_COST,
        name="pick_first",
    )(*arrays)
    own_b, fixed = pl.pallas_call(
        pick_rest_kernel,
        out_shape=[half_shape, full_shape],
        in_specs=[ANY, ANY, ANY],
        out_specs=[vmem, vmem],
        scratch_shapes=[pltpu.SemaphoreType.DMA((2 * PIECES,))],
        compiler_params=pltpu.CompilerParams(vmem_limit_bytes=PICK_BYTES),
        cost_estimate=NO_COST,
        name="pick_rest",
    )(*arrays, own_a)
    down = matched_caption_index.reshape(rows, 1)

    def kernel(body, name, *operands, shape=None, scratch=()):
        total_shape = jax.ShapeDtypeStruct((2 * rows, depth), jnp.float32)
        return pl.pallas_call(
            body,
            out_shape=shape or total_shape,
            in_specs=[SMEM, SMEM] + [vmem] * len(operands),
            out_specs=vmem,
            scratch_shapes=scratch,
            input_output_aliases={} if shape or body is own_kernel else {2: 0},
            compiler_params=params(),
            cost_estimate=NO_COST,
            name=name,
        )(flags, scale, *operands)

    one_a, one_b = hop(own_a, to_up), hop(own_b, to_up)
    group_a = hop(own_a, to_side_1)
    other_fixed = hop(fixed, core_swap)
    one_a, fixed_late = lax.optimization_barrier((one_a, fixed))
    two_a = hop(one_a, onward)
    over_a = hop(one_a, but_2_across)
    total = kernel(
        own_kernel,
        "own_blocks",
        down,
        matched_caption_index,
        fixed_late,
        own_a,
        own_b,
    )
    one_b, total = lax.optimization_barrier((one_b, total))
    two_b = hop(one_b, onward)
    over_b = hop(one_b, but_2_across)
    two_a, total = lax.optimization_barrier((two_a, total))
    last_a = hop(two_a, last_step)
    operands = (total, fixed, other_fixed, one_a, group_a, own_a, own_b)
    total = kernel(first_halves_kernel, "first_halves", *operands)
    total = kernel(halves_kernel, "second_halves", total, fixed, other_fixed, one_b, over_a)
    two_b, own_b, total = lax.optimization_barrier((two_b, own_b, total))
    last_b = hop(two_b, last_step)
    group_b = hop(own_b, to_side_1)
    total = kernel(halves_kernel, "third_halves", total, fixed, other_fixed, over_b, last_a)
    total = kernel(two_kernel, "two_block", total, fixed, other_fixed, two_a, two_b)
    width = [pltpu.VMEM((half, depth), jnp.float32)]

    def last_of(body, start, name, *operands):
        return kernel(
            functools.partial(body, start), name, total, *operands, shape=half_shape, scratch=width
        )

    sent, mine = [], []
    for k, name in enumerate(("last_other_a", "last_other_b")):
        sent.append(last_of(last_other_kernel, k * half, name, other_fixed, group_b, last_b))
    came = [hop(x, core_swap) for x in sent]
    for k, name in enumerate(("last_own_a", "last_own_b")):
        mine.append(last_of(last_own_kernel, k * half, name, fixed, group_b, last_b, came[k]))
    theirs = [hop(x, replica_swap) for x in mine]
    out_shape = jax.ShapeDtypeStruct((rows, depth), jnp.float32)

    def write(picture_step, start, values, outs, name):
        count = len(values)
        return pl.pallas_call(
            functools.partial(write_kernel, picture_step, start, count),
            out_shape=[out_shape, out_shape],
            in_specs=[vmem] * count + [ANY] * len(outs),
            out_specs=[ANY, ANY],
            scratch_shapes=[
                pltpu.VMEM((count * half, depth), jnp.float32),
                pltpu.SemaphoreType.DMA((count * PIECES,)),
            ],
            input_output_aliases={count + k: k for k in range(len(outs))},
            compiler_params=params(),
            cost_estimate=NO_COST,
            name=name,
        )(*values, *outs)

    outs = write(True, 0, mine, (), "write_mine")
    outs = write(False, 0, theirs[:1], outs, "write_theirs_a")
    return tuple(write(False, half, theirs[1:], outs, "write_theirs_b"))


def solution(mesh):
    placed = (P("dp", None), P("dp", None), P("dp", None), P(), P(), P())
    return jax.shard_map(
        per_device,
        mesh=mesh,
        in_specs=placed,
        out_specs=(P("dp", None), P("dp", None)),
        check_vma=False,
    )
```

time: 106 us -> 107 us (level)
  Pallas kernels: 25.1 us -> 35.8 us
  waiting for transfers between devices: 42.9 us -> 37.2 us
  other arithmetic: 2.99 us -> 0.08 us
    pallas_call x6 -> x14, Pallas kernels: 25.1 us -> 35.8 us  [the longest x9 27.4 us: kernel(): pl.pallas_call(body, out_shape=shape or total_shape, in_specs=[SMEM, SMEM...]
    ppermute x13 -> x15, waiting for transfers between devices: 42.9 us -> 37.2 us  [hop(): return lax.ppermute(x, ('dp', 'rep'), pairs)]
    convert_element_type x2 -> x0, other arithmetic: 2.83 us -> none  [the longest x1 2.49 us: per_device(): jnp.where(first, theirs, mine).astype(jnp.float32)]
    unnamed x10 -> x12, local copies, waits for them, and re-layouts: 3.4 us -> 2.35 us
    ppermute x13 -> x15, starting transfers between devices: 27.7 us -> 27.4 us  [hop(): return lax.ppermute(x, ('dp', 'rep'), pairs)]
  transfers between devices with their start and end apart: 13 -> 15, of which waited for: 7 -> 7; matrix products, arithmetic and copies ran while one was open for 0% -> 0% of each run, Pallas kernels for 19% -> 29%
where the time goes in v4:
time: 107 us; the launch traced here: 106 us
  waiting for transfers between devices  37.2 us (35%)
  Pallas kernels  35.8 us (33%)
  starting transfers between devices  27.4 us (26%)
  between operations  3.12 us (3%)
  local copies, waits for them, and re-layouts  2.58 us (2%)
    ppermute x15, waiting for transfers between devices, hop(): return lax.ppermute(x, ('dp', 'rep'), pairs)  37.2 us
    ppermute x15, starting transfers between devices, hop(): return lax.ppermute(x, ('dp', 'rep'), pairs)  27.4 us
    pallas_call x9, Pallas kernels, kernel(): pl.pallas_call(body, out_shape=shape or total_shape, in_specs=[SMEM, SMEM...  27.4 us
    pallas_call x3, Pallas kernels, write(): pl.pallas_call(functools.partial(write_kernel, picture_step, start, count...  3.6 us
    pallas_call x1, Pallas kernels, per_device(): pl.pallas_call(pick_rest_kernel, out_shape=[half_shape, full_shape], in_s...  2.79 us
    unnamed x12, local copies, waits for them, and re-layouts  2.35 us
  transfers between devices with their start and end apart: 15, of which 7 were waited for; matrix products, arithmetic and copies ran while one was open for 0% of the time, Pallas kernels for 29%

profile of v4, /device:TPU:0, one launch (start us, length us, event | category | flops | bytes accessed | tf_op | source)
XLA Modules:
  0.0 106.2 jit_solution(16776372578970922261)
XLA Ops:
  0.6 2.0 %pick_first.1.own_a_ref.own_a = bf16[256,1152]{1,0:T(8,128)(2,1)} custom-call(bf16[512,1152]{1,0:T(8,128)(2,1)} %image_ref.3, bf16[512,1152]{1,0:T(8,128)(2,1)} %text_ref.3), custom_call_target="tpu_custom_call" | custom-call | flops 1 | bytes 1 | tf_op jit(solution)/shard_map/pick_first/pallas_call | solution.py:256
  2.6 0.0 copy-start.2
  2.6 3.1 %collective-permute-start.1 = (bf16[256,1152]{1,0:T(8,128)(2,1)}, bf16[256,1152]{1,0:T(8,128)(2,1)S(1)}, u32[]{:S(2)}, u32[]{:S(2)}) collective-permute-start(bf16[256,1152]{1,0:T(8,128)(2,1)} %pick_first.1.own_a_ref.own_a), channel_id=1, source_target_pairs={{0,8},{31,23},{2,10},{29,21},{4,12},{27,19},{6,14},{25,17},{8,16},... | collective-permute-start | bytes 1769480 | tf_op jit(solution)/shard_map/ppermute | solution.py:19
  5.7 2.8 %pick_rest.1 = (bf16[256,1152]{1,0:T(8,128)(2,1)}, bf16[512,1152]{1,0:T(8,128)(2,1)}) custom-call(bf16[512,1152]{1,0:T(8,128)(2,1)} %image_ref.3, bf16[512,1152]{1,0:T(8,128)(2,1)} %text_ref.3, bf16[256,1152]{1,0:T(8,128)(2,1)} %pick_first.1.own_a_ref.own_a), custom_call_target="tpu_custom_call" | custom-call | flops 1 | bytes 1 | tf_op jit(solution)/shard_map/pick_rest/pallas_call | solution.py:266
  8.5 0.1 collective-permute-start.4
  8.6 1.6 %collective-permute-start = (bf16[256,1152]{1,0:T(8,128)(2,1)}, bf16[256,1152]{1,0:T(8,128)(2,1)}, u32[]{:S(2)}, u32[]{:S(2)}) collective-permute-start(bf16[256,1152]{1,0:T(8,128)(2,1)} %get-tuple-element.27.own_b), channel_id=1, source_target_pairs={{0,8},{31,23},{2,10},{29,21},{4,12},{27,19},{6,14},{25,17},{8,16},... | collective-permute-start | bytes 1769480 | tf_op jit(solution)/shard_map/ppermute | solution.py:19
  10.2 3.4 %collective-permute-start.5 = (bf16[256,1152]{1,0:T(8,128)(2,1)S(1)}, bf16[256,1152]{1,0:T(8,128)(2,1)S(1)}, u32[]{:S(2)}, u32[]{:S(2)}) collective-permute-start(bf16[256,1152]{1,0:T(8,128)(2,1)S(1)} %copy-done.2), channel_id=1, source_target_pairs={{0,4},{31,27},{2,6},{29,25},{8,12},{23,19},{10,14},{21,17},{16,20}... | collective-permute-start | bytes 1769480 | tf_op jit(solution)/shard_map/ppermute | solution.py:19
  15.7 0.1 copy.16.down_ref
  15.9 0.1 pad_add_fusion.flag_ref
  16.0 6.1 %collective-permute-done.1.half_ref = bf16[256,1152]{1,0:T(8,128)(2,1)S(1)} collective-permute-done((bf16[256,1152]{1,0:T(8,128)(2,1)}, bf16[256,1152]{1,0:T(8,128)(2,1)S(1)}, u32[]{:S(2)}, u32[]{:S(2)}) %collective-permute-start.1) | collective-permute-done | bytes 589856 | tf_op jit(solution)/shard_map/ppermute | solution.py:19
  22.1 1.3 %collective-permute-start.3 = (bf16[256,1152]{1,0:T(8,128)(2,1)S(1)}, bf16[256,1152]{1,0:T(8,128)(2,1)}, u32[]{:S(2)}, u32[]{:S(2)}) collective-permute-start(bf16[256,1152]{1,0:T(8,128)(2,1)S(1)} %collective-permute-done.1.half_ref), channel_id=1, source_target_pairs={{2,10},{29,21},{6,14},{25,17},{10,18},{21,13},{14,22},{17,9},{18,2... | collective-permute-start | bytes 1769480 | tf_op jit(solution)/shard_map/ppermute | solution.py:19
  23.4 0.1 stack.43.scale_ref
  23.5 5.4 %collective-permute-start.6 = (bf16[256,1152]{1,0:T(8,128)(2,1)S(1)}, bf16[256,1152]{1,0:T(8,128)(2,1)S(1)}, u32[]{:S(2)}, u32[]{:S(2)}) collective-permute-start(bf16[256,1152]{1,0:T(8,128)(2,1)S(1)} %collective-permute-done.1.half_ref), channel_id=1, source_target_pairs={{0,4},{31,27},{2,6},{29,25},{6,2},{25,29},{8,12},{23,19},{10,14},{... | collective-permute-start | bytes 1769480 | tf_op jit(solution)/shard_map/ppermute | solution.py:19
  28.9 0.0 copy-start
  28.9 1.3 %copy-done = bf16[512,1152]{1,0:T(8,128)(2,1)S(1)} copy-done((bf16[512,1152]{1,0:T(8,128)(2,1)S(1)}, bf16[512,1152]{1,0:T(8,128)(2,1)}, u32[]{:S(2)}) %copy-start) | copy-done | bytes 1179672
  30.2 1.1 %copy-done.3 = bf16[256,1152]{1,0:T(8,128)(2,1)S(1)} copy-done((bf16[256,1152]{1,0:T(8,128)(2,1)S(1)}, bf16[256,1152]{1,0:T(8,128)(2,1)}, u32[]{:S(2)}) %copy-start.3) | copy-done | bytes 589848
  31.2 2.5 %own_blocks.1._ = f32[1024,1152]{1,0:T(8,128)S(1)} custom-call(s32[3]{0:T(128)S(1)} %pad_add_fusion.flag_ref, f32[5]{0:T(128)S(1)} %stack.43.scale_ref, s32[512,1]{1,0:T(8,128)S(1)} %copy.16.down_ref, s32[1,512]{1,0:T(1,128)S(1)} %copy-done.5, bf16[512,1152]{1,0:T(8,128)(2,1)S(1)} %copy-done, bf16[256,1152]{1,0:T(8,128)(2,1)S(1)} %copy-done.2, ...), custom_call_target="tpu_custom_call" | custom-call | flops 1 | bytes 1 | tf_op jit(solution)/shard_map/own_blocks/pallas_call | solution.py:280
  33.7 0.0 copy-start.1
  33.7 1.2 %collective-permute-done.half_ref = bf16[256,1152]{1,0:T(8,128)(2,1)} collective-permute-done((bf16[256,1152]{1,0:T(8,128)(2,1)}, bf16[256,1152]{1,0:T(8,128)(2,1)}, u32[]{:S(2)}, u32[]{:S(2)}) %collective-permute-start) | collective-permute-done | bytes 589856 | tf_op jit(solution)/shard_map/ppermute | solution.py:19
  34.9 1.3 %collective-permute-start.2 = (bf16[256,1152]{1,0:T(8,128)(2,1)}, bf16[256,1152]{1,0:T(8,128)(2,1)S(1)}, u32[]{:S(2)}, u32[]{:S(2)}) collective-permute-start(bf16[256,1152]{1,0:T(8,128)(2,1)} %collective-permute-done.half_ref), channel_id=1, source_target_pairs={{2,10},{29,21},{6,14},{25,17},{10,18},{21,13},{14,22},{17,9},{18,2... | collective-permute-start | bytes 1769480 | tf_op jit(solution)/shard_map/ppermute | solution.py:19
  36.1 3.6 %collective-permute-done.3.two_a = bf16[256,1152]{1,0:T(8,128)(2,1)} collective-permute-done((bf16[256,1152]{1,0:T(8,128)(2,1)S(1)}, bf16[256,1152]{1,0:T(8,128)(2,1)}, u32[]{:S(2)}, u32[]{:S(2)}) %collective-permute-start.3) | collective-permute-done | bytes 589856 | tf_op jit(solution)/shard_map/ppermute | solution.py:19
  39.8 1.4 %collective-permute-start.7 = (bf16[256,1152]{1,0:T(8,128)(2,1)}, bf16[256,1152]{1,0:T(8,128)(2,1)S(1)}, u32[]{:S(2)}, u32[]{:S(2)}) collective-permute-start(bf16[256,1152]{1,0:T(8,128)(2,1)} %collective-permute-done.half_ref), channel_id=1, source_target_pairs={{0,4},{31,27},{2,6},{29,25},{6,2},{25,29},{8,12},{23,19},{10,14},{... | collective-permute-start | bytes 1769480 | tf_op jit(solution)/shard_map/ppermute | solution.py:19
  41.2 2.3 %collective-permute-start.8 = (bf16[256,1152]{1,0:T(8,128)(2,1)}, bf16[256,1152]{1,0:T(8,128)(2,1)S(1)}, u32[]{:S(2)}, u32[]{:S(2)}) collective-permute-start(bf16[256,1152]{1,0:T(8,128)(2,1)} %collective-permute-done.3.two_a), channel_id=1, source_target_pairs={{0,8},{31,23},{8,16},{23,15},{16,24},{15,7},{24,0},{7,31},{6,2},{2... | collective-permute-start | bytes 1769480 | tf_op jit(solution)/shard_map/ppermute | solution.py:19
  43.5 0.0 collective-permute-done.4.other_ref
  43.5 5.5 %first_halves.1._ = f32[1024,1152]{1,0:T(8,128)S(1)} custom-call(s32[3]{0:T(128)S(1)} %pad_add_fusion.flag_ref, f32[5]{0:T(128)S(1)} %stack.43.scale_ref, f32[1024,1152]{1,0:T(8,128)S(1)} %own_blocks.1._, bf16[512,1152]{1,0:T(8,128)(2,1)S(1)} %copy-done, bf16[512,1152]{1,0:T(8,128)(2,1)S(1)} %collective-permute-done.4.other_ref, ...), custom_call_target="tpu_custom_call", output_to_operand_aliasing={{}: (2, {})} | custom-call | flops 1 | bytes 1 | tf_op jit(solution)/shard_map/first_halves/pallas_call | solution.py:280
  49.0 0.0 collective-permute-done.6.group_ref
  49.0 4.3 %second_halves.1._ = f32[1024,1152]{1,0:T(8,128)S(1)} custom-call(s32[3]{0:T(128)S(1)} %pad_add_fusion.flag_ref, f32[5]{0:T(128)S(1)} %stack.43.scale_ref, f32[1024,1152]{1,0:T(8,128)S(1)} %first_halves.1._, bf16[512,1152]{1,0:T(8,128)(2,1)S(1)} %copy-done.1, bf16[512,1152]{1,0:T(8,128)(2,1)S(1)} %collective-permute-done.4.other_ref, ...), custom_call_target="tpu_custom_call", output_to_operand_aliasing={{}: (2, {})} | custom-call | flops 1 | bytes 1 | tf_op jit(solution)/shard_map/second_halves/pallas_call | solution.py:280
  53.3 0.0 collective-permute-done.2.two_b
  53.4 3.5 %collective-permute-start.10 = (bf16[256,1152]{1,0:T(8,128)(2,1)S(1)}, bf16[256,1152]{1,0:T(8,128)(2,1)S(1)}, u32[]{:S(2)}, u32[]{:S(2)}) collective-permute-start(bf16[256,1152]{1,0:T(8,128)(2,1)S(1)} %collective-permute-done.2.two_b), channel_id=1, source_target_pairs={{0,8},{31,23},{8,16},{23,15},{16,24},{15,7},{24,0},{7,31},{6,2},{2... | collective-permute-start | bytes 1769480 | tf_op jit(solution)/shard_map/ppermute | solution.py:19
  56.8 1.3 %collective-permute-start.9 = (bf16[256,1152]{1,0:T(8,128)(2,1)S(1)}, bf16[256,1152]{1,0:T(8,128)(2,1)S(1)}, u32[]{:S(2)}, u32[]{:S(2)}) collective-permute-start(bf16[256,1152]{1,0:T(8,128)(2,1)S(1)} %copy-done.4), channel_id=1, source_target_pairs={{0,4},{31,27},{2,6},{29,25},{8,12},{23,19},{10,14},{21,17},{16,20}... | collective-permute-start | bytes 1769480 | tf_op jit(solution)/shard_map/ppermute | solution.py:19
  58.2 0.0 collective-permute-done.8.group_ref
  58.2 3.8 %third_halves.1._ = f32[1024,1152]{1,0:T(8,128)S(1)} custom-call(s32[3]{0:T(128)S(1)} %pad_add_fusion.flag_ref, f32[5]{0:T(128)S(1)} %stack.43.scale_ref, f32[1024,1152]{1,0:T(8,128)S(1)} %second_halves.1._, bf16[512,1152]{1,0:T(8,128)(2,1)S(1)} %copy-done.1, bf16[512,1152]{1,0:T(8,128)(2,1)S(1)} %collective-permute-done.4.other_ref, ...), custom_call_target="tpu_custom_call", output_to_operand_aliasing={{}: (2, {})} | custom-call | flops 1 | bytes 1 | tf_op jit(solution)/shard_map/third_halves/pallas_call | solution.py:280
  62.0 4.7 %two_block.1.sum_ref = f32[1024,1152]{1,0:T(8,128)S(1)} custom-call(s32[3]{0:T(128)S(1)} %pad_add_fusion.flag_ref, f32[5]{0:T(128)S(1)} %stack.43.scale_ref, f32[1024,1152]{1,0:T(8,128)S(1)} %third_halves.1._, bf16[512,1152]{1,0:T(8,128)(2,1)S(1)} %copy-done.1, ...), custom_call_target="tpu_custom_call", output_to_operand_aliasing={{}: (2, {})} | custom-call | flops 1 | bytes 1 | tf_op jit(solution)/shard_map/two_block/pallas_call | solution.py:280
  66.7 0.2 collective-permute-done.10.last_ref
  66.9 4.2 %collective-permute-done.9.group_ref = bf16[256,1152]{1,0:T(8,128)(2,1)S(1)} collective-permute-done((bf16[256,1152]{1,0:T(8,128)(2,1)S(1)}, bf16[256,1152]{1,0:T(8,128)(2,1)S(1)}, u32[]{:S(2)}, u32[]{:S(2)}) %collective-permute-start.9) | collective-permute-done | bytes 589856 | tf_op jit(solution)/shard_map/ppermute | solution.py:19
  71.1 1.6 %last_other_a.1 = bf16[256,1152]{1,0:T(8,128)(2,1)S(1)} custom-call(s32[3]{0:T(128)S(1)} %pad_add_fusion.flag_ref, f32[5]{0:T(128)S(1)} %stack.43.scale_ref, f32[1024,1152]{1,0:T(8,128)S(1)} %two_block.1.sum_ref, bf16[512,1152]{1,0:T(8,128)(2,1)S(1)} %collective-permute-done.4.other_ref, bf16[256,1152]{1,0:T(8,128)(2,1)S(1)} %collective-permute-done.9.group_ref, ...), custom_call_target="tpu_custom_call" | custom-call | flops 1 | bytes 1 | tf_op jit(solution)/shard_map/last_other_a/pallas_call | solution.py:280
  72.8 0.1 collective-permute-start.13
  72.9 1.6 %last_other_b.1 = bf16[256,1152]{1,0:T(8,128)(2,1)S(1)} custom-call(s32[3]{0:T(128)S(1)} %pad_add_fusion.flag_ref, f32[5]{0:T(128)S(1)} %stack.43.scale_ref, f32[1024,1152]{1,0:T(8,128)S(1)} %two_block.1.sum_ref, bf16[512,1152]{1,0:T(8,128)(2,1)S(1)} %collective-permute-done.4.other_ref, bf16[256,1152]{1,0:T(8,128)(2,1)S(1)} %collective-permute-done.9.group_ref, ...), custom_call_target="tpu_custom_call" | custom-call | flops 1 | bytes 1 | tf_op jit(solution)/shard_map/last_other_b/pallas_call | solution.py:280
  74.5 0.6 collective-permute-start.11
  75.0 1.7 %last_own_a.1.refs_0_ = bf16[256,1152]{1,0:T(8,128)(2,1)S(1)} custom-call(s32[3]{0:T(128)S(1)} %pad_add_fusion.flag_ref, f32[5]{0:T(128)S(1)} %stack.43.scale_ref, f32[1024,1152]{1,0:T(8,128)S(1)} %two_block.1.sum_ref, bf16[512,1152]{1,0:T(8,128)(2,1)S(1)} %copy-done.1, bf16[256,1152]{1,0:T(8,128)(2,1)S(1)} %collective-permute-done.9.group_ref, ...), custom_call_target="tpu_custom_call" | custom-call | flops 1 | bytes 1 | tf_op jit(solution)/shard_map/last_own_a/pallas_call | solution.py:280
  76.8 2.0 %collective-permute-start.14 = (bf16[256,1152]{1,0:T(8,128)(2,1)S(1)}, bf16[256,1152]{1,0:T(8,128)(2,1)S(1)}, u32[]{:S(2)}, u32[]{:S(2)}) collective-permute-start(bf16[256,1152]{1,0:T(8,128)(2,1)S(1)} %last_own_a.1.refs_0_), channel_id=1, source_target_pairs={{0,1},{1,0},{2,3},{3,2},{4,5},{5,4},{6,7},{7,6},{8,9},{9,8},{10,11... | collective-permute-start | bytes 1769480 | tf_op jit(solution)/shard_map/ppermute | solution.py:19
  78.8 1.7 %last_own_b.1.refs_1_ = bf16[256,1152]{1,0:T(8,128)(2,1)S(1)} custom-call(s32[3]{0:T(128)S(1)} %pad_add_fusion.flag_ref, f32[5]{0:T(128)S(1)} %stack.43.scale_ref, f32[1024,1152]{1,0:T(8,128)S(1)} %two_block.1.sum_ref, bf16[512,1152]{1,0:T(8,128)(2,1)S(1)} %copy-done.1, bf16[256,1152]{1,0:T(8,128)(2,1)S(1)} %collective-permute-done.9.group_ref, ...), custom_call_target="tpu_custom_call" | custom-call | flops 1 | bytes 1 | tf_op jit(solution)/shard_map/last_own_b/pallas_call | solution.py:280
  80.5 0.1 collective-permute-start.12
  80.6 1.5 %write_mine.1 = (f32[512,1152]{1,0:T(8,128)}, f32[512,1152]{1,0:T(8,128)}) custom-call(bf16[256,1152]{1,0:T(8,128)(2,1)S(1)} %last_own_a.1.refs_0_, bf16[256,1152]{1,0:T(8,128)(2,1)S(1)} %last_own_b.1.refs_1_), custom_call_target="tpu_custom_call" | custom-call | flops 1 | bytes 1 | tf_op jit(solution)/shard_map/write_mine/pallas_call | solution.py:338
  82.1 10.9 %collective-permute-done.14.refs_0_ = bf16[256,1152]{1,0:T(8,128)(2,1)S(1)} collective-permute-done((bf16[256,1152]{1,0:T(8,128)(2,1)S(1)}, bf16[256,1152]{1,0:T(8,128)(2,1)S(1)}, u32[]{:S(2)}, u32[]{:S(2)}) %collective-permute-start.14) | collective-permute-done | bytes 589856 | tf_op jit(solution)/shard_map/ppermute | solution.py:19
  93.0 1.1 write_theirs_a.1
  94.1 10.9 %collective-permute-done.12.refs_0_ = bf16[256,1152]{1,0:T(8,128)(2,1)S(1)} collective-permute-done((bf16[256,1152]{1,0:T(8,128)(2,1)S(1)}, bf16[256,1152]{1,0:T(8,128)(2,1)S(1)}, u32[]{:S(2)}, u32[]{:S(2)}) %collective-permute-start.12) | collective-permute-done | bytes 589856 | tf_op jit(solution)/shard_map/ppermute | solution.py:19
  105.0 1.1 write_theirs_b.1
  (11 shorter events, 0.0 us)
Async XLA Ops:
  0.6 15.1 %copy-start.5 = (s32[1,512]{1,0:T(1,128)S(1)}, s32[1,512]{1,0:T(1,128)}, u32[]{:S(2)}) copy-start(s32[1,512]{1,0:T(1,128)} %along_ref.1) | copy-start | bytes 6148
  2.6 7.6 %copy-start.2 = (bf16[256,1152]{1,0:T(8,128)(2,1)S(1)}, bf16[256,1152]{1,0:T(8,128)(2,1)}, u32[]{:S(2)}) copy-start(bf16[256,1152]{1,0:T(8,128)(2,1)} %pick_first.1.own_a_ref.own_a) | copy-start | bytes 1769476
  2.6 19.5 %collective-permute-start.1 = (bf16[256,1152]{1,0:T(8,128)(2,1)}, bf16[256,1152]{1,0:T(8,128)(2,1)S(1)}, u32[]{:S(2)}, u32[]{:S(2)}) collective-permute-start(bf16[256,1152]{1,0:T(8,128)(2,1)} %pick_first.1.own_a_ref.own_a), channel_id=1, source_target_pairs={{0,8},{31,23},{2,10},{29,21},{4,12},{27,19},{6,14},{25,17},{8,16},... | collective-permute-start | bytes 1769480 | tf_op jit(solution)/shard_map/ppermute | solution.py:19
  8.5 35.0 %collective-permute-start.4 = (bf16[512,1152]{1,0:T(8,128)(2,1)}, bf16[512,1152]{1,0:T(8,128)(2,1)S(1)}, u32[]{:S(2)}, u32[]{:S(2)}) collective-permute-start(bf16[512,1152]{1,0:T(8,128)(2,1)} %get-tuple-element.19.fixed_ref), channel_id=1, source_target_pairs={{0,2},{31,29},{2,0},{29,31},{4,6},{27,25},{6,4},{25,27},{8,10},{23... | collective-permute-start | bytes 3538952 | tf_op jit(solution)/shard_map/ppermute | solution.py:19
  8.6 26.3 %collective-permute-start = (bf16[256,1152]{1,0:T(8,128)(2,1)}, bf16[256,1152]{1,0:T(8,128)(2,1)}, u32[]{:S(2)}, u32[]{:S(2)}) collective-permute-start(bf16[256,1152]{1,0:T(8,128)(2,1)} %get-tuple-element.27.own_b), channel_id=1, source_target_pairs={{0,8},{31,23},{2,10},{29,21},{4,12},{27,19},{6,14},{25,17},{8,16},... | collective-permute-start | bytes 1769480 | tf_op jit(solution)/shard_map/ppermute | solution.py:19
  10.2 30.9 %collective-permute-start.5 = (bf16[256,1152]{1,0:T(8,128)(2,1)S(1)}, bf16[256,1152]{1,0:T(8,128)(2,1)S(1)}, u32[]{:S(2)}, u32[]{:S(2)}) collective-permute-start(bf16[256,1152]{1,0:T(8,128)(2,1)S(1)} %copy-done.2), channel_id=1, source_target_pairs={{0,4},{31,27},{2,6},{29,25},{8,12},{23,19},{10,14},{21,17},{16,20}... | collective-permute-start | bytes 1769480 | tf_op jit(solution)/shard_map/ppermute | solution.py:19
  22.1 17.7 %collective-permute-start.3 = (bf16[256,1152]{1,0:T(8,128)(2,1)S(1)}, bf16[256,1152]{1,0:T(8,128)(2,1)}, u32[]{:S(2)}, u32[]{:S(2)}) collective-permute-start(bf16[256,1152]{1,0:T(8,128)(2,1)S(1)} %collective-permute-done.1.half_ref), channel_id=1, source_target_pairs={{2,10},{29,21},{6,14},{25,17},{10,18},{21,13},{14,22},{17,9},{18,2... | collective-permute-start | bytes 1769480 | tf_op jit(solution)/shard_map/ppermute | solution.py:19
  23.5 25.5 %collective-permute-start.6 = (bf16[256,1152]{1,0:T(8,128)(2,1)S(1)}, bf16[256,1152]{1,0:T(8,128)(2,1)S(1)}, u32[]{:S(2)}, u32[]{:S(2)}) collective-permute-start(bf16[256,1152]{1,0:T(8,128)(2,1)S(1)} %collective-permute-done.1.half_ref), channel_id=1, source_target_pairs={{0,4},{31,27},{2,6},{29,25},{6,2},{25,29},{8,12},{23,19},{10,14},{... | collective-permute-start | bytes 1769480 | tf_op jit(solution)/shard_map/ppermute | solution.py:19
  28.9 1.3 %copy-start = (bf16[512,1152]{1,0:T(8,128)(2,1)S(1)}, bf16[512,1152]{1,0:T(8,128)(2,1)}, u32[]{:S(2)}) copy-start(bf16[512,1152]{1,0:T(8,128)(2,1)} %get-tuple-element.19.fixed_ref) | copy-start | bytes 3538948
  30.2 1.1 %copy-start.3 = (bf16[256,1152]{1,0:T(8,128)(2,1)S(1)}, bf16[256,1152]{1,0:T(8,128)(2,1)}, u32[]{:S(2)}) copy-start(bf16[256,1152]{1,0:T(8,128)(2,1)} %get-tuple-element.27.own_b) | copy-start | bytes 1769476
  31.2 12.3 %copy-start.4 = (bf16[256,1152]{1,0:T(8,128)(2,1)S(1)}, bf16[256,1152]{1,0:T(8,128)(2,1)}, u32[]{:S(2)}) copy-start(bf16[256,1152]{1,0:T(8,128)(2,1)} %get-tuple-element.27.own_b) | copy-start | bytes 1769476
  33.7 15.3 %copy-start.1 = (bf16[512,1152]{1,0:T(8,128)(2,1)S(1)}, bf16[512,1152]{1,0:T(8,128)(2,1)}, u32[]{:S(2)}) copy-start(bf16[512,1152]{1,0:T(8,128)(2,1)} %get-tuple-element.19.fixed_ref) | copy-start | bytes 3538948
  34.9 18.5 %collective-permute-start.2 = (bf16[256,1152]{1,0:T(8,128)(2,1)}, bf16[256,1152]{1,0:T(8,128)(2,1)S(1)}, u32[]{:S(2)}, u32[]{:S(2)}) collective-permute-start(bf16[256,1152]{1,0:T(8,128)(2,1)} %collective-permute-done.half_ref), channel_id=1, source_target_pairs={{2,10},{29,21},{6,14},{25,17},{10,18},{21,13},{14,22},{17,9},{18,2... | collective-permute-start | bytes 1769480 | tf_op jit(solution)/shard_map/ppermute | solution.py:19
  39.8 18.4 %collective-permute-start.7 = (bf16[256,1152]{1,0:T(8,128)(2,1)}, bf16[256,1152]{1,0:T(8,128)(2,1)S(1)}, u32[]{:S(2)}, u32[]{:S(2)}) collective-permute-start(bf16[256,1152]{1,0:T(8,128)(2,1)} %collective-permute-done.half_ref), channel_id=1, source_target_pairs={{0,4},{31,27},{2,6},{29,25},{6,2},{25,29},{8,12},{23,19},{10,14},{... | collective-permute-start | bytes 1769480 | tf_op jit(solution)/shard_map/ppermute | solution.py:19
  41.2 17.0 %collective-permute-start.8 = (bf16[256,1152]{1,0:T(8,128)(2,1)}, bf16[256,1152]{1,0:T(8,128)(2,1)S(1)}, u32[]{:S(2)}, u32[]{:S(2)}) collective-permute-start(bf16[256,1152]{1,0:T(8,128)(2,1)} %collective-permute-done.3.two_a), channel_id=1, source_target_pairs={{0,8},{31,23},{8,16},{23,15},{16,24},{15,7},{24,0},{7,31},{6,2},{2... | collective-permute-start | bytes 1769480 | tf_op jit(solution)/shard_map/ppermute | solution.py:19
  53.4 13.6 %collective-permute-start.10 = (bf16[256,1152]{1,0:T(8,128)(2,1)S(1)}, bf16[256,1152]{1,0:T(8,128)(2,1)S(1)}, u32[]{:S(2)}, u32[]{:S(2)}) collective-permute-start(bf16[256,1152]{1,0:T(8,128)(2,1)S(1)} %collective-permute-done.2.two_b), channel_id=1, source_target_pairs={{0,8},{31,23},{8,16},{23,15},{16,24},{15,7},{24,0},{7,31},{6,2},{2... | collective-permute-start | bytes 1769480 | tf_op jit(solution)/shard_map/ppermute | solution.py:19
  56.8 14.3 %collective-permute-start.9 = (bf16[256,1152]{1,0:T(8,128)(2,1)S(1)}, bf16[256,1152]{1,0:T(8,128)(2,1)S(1)}, u32[]{:S(2)}, u32[]{:S(2)}) collective-permute-start(bf16[256,1152]{1,0:T(8,128)(2,1)S(1)} %copy-done.4), channel_id=1, source_target_pairs={{0,4},{31,27},{2,6},{29,25},{8,12},{23,19},{10,14},{21,17},{16,20}... | collective-permute-start | bytes 1769480 | tf_op jit(solution)/shard_map/ppermute | solution.py:19
  72.8 2.3 %collective-permute-start.13 = (bf16[256,1152]{1,0:T(8,128)(2,1)S(1)}, bf16[256,1152]{1,0:T(8,128)(2,1)S(1)}, u32[]{:S(2)}, u32[]{:S(2)}) collective-permute-start(bf16[256,1152]{1,0:T(8,128)(2,1)S(1)} %last_other_a.1), channel_id=1, source_target_pairs={{0,2},{31,29},{2,0},{29,31},{4,6},{27,25},{6,4},{25,27},{8,10},{23... | collective-permute-start | bytes 1769480 | tf_op jit(solution)/shard_map/ppermute | solution.py:19
  74.5 4.3 %collective-permute-start.11 = (bf16[256,1152]{1,0:T(8,128)(2,1)S(1)}, bf16[256,1152]{1,0:T(8,128)(2,1)S(1)}, u32[]{:S(2)}, u32[]{:S(2)}) collective-permute-start(bf16[256,1152]{1,0:T(8,128)(2,1)S(1)} %last_other_b.1), channel_id=1, source_target_pairs={{0,2},{31,29},{2,0},{29,31},{4,6},{27,25},{6,4},{25,27},{8,10},{23... | collective-permute-start | bytes 1769480 | tf_op jit(solution)/shard_map/ppermute | solution.py:19
  76.8 16.2 %collective-permute-start.14 = (bf16[256,1152]{1,0:T(8,128)(2,1)S(1)}, bf16[256,1152]{1,0:T(8,128)(2,1)S(1)}, u32[]{:S(2)}, u32[]{:S(2)}) collective-permute-start(bf16[256,1152]{1,0:T(8,128)(2,1)S(1)} %last_own_a.1.refs_0_), channel_id=1, source_target_pairs={{0,1},{1,0},{2,3},{3,2},{4,5},{5,4},{6,7},{7,6},{8,9},{9,8},{10,11... | collective-permute-start | bytes 1769480 | tf_op jit(solution)/shard_map/ppermute | solution.py:19
  80.5 24.4 %collective-permute-start.12 = (bf16[256,1152]{1,0:T(8,128)(2,1)S(1)}, bf16[256,1152]{1,0:T(8,128)(2,1)S(1)}, u32[]{:S(2)}, u32[]{:S(2)}) collective-permute-start(bf16[256,1152]{1,0:T(8,128)(2,1)S(1)} %last_own_b.1.refs_1_), channel_id=1, source_target_pairs={{0,1},{1,0},{2,3},{3,2},{4,5},{5,4},{6,7},{7,6},{8,9},{9,8},{10,11... | collective-permute-start | bytes 1769480 | tf_op jit(solution)/shard_map/ppermute | solution.py:19

commit v5 on v4

v5 whole, which is shorter than its diff:
```python
import functools

import jax
import jax.numpy as jnp
from jax import lax
from jax.experimental import pallas as pl
from jax.experimental.pallas import tpu as pltpu
from jax.sharding import PartitionSpec as P

GROUP = 4
VMEM_BYTES = 36 * 1024 * 1024
NO_ROOM = 60 * 1024 * 1024
PICK_BYTES = NO_ROOM

FIRST, CORE, SIDE = 0, 1, 2


def hop(x, pairs):
    return lax.ppermute(x, ("dp", "rep"), pairs)


def pairs_of(devices, target, members):
    pairs = []
    for p in range(devices):
        if p % GROUP in members:
            q = target(p)
            pairs.append((2 * p, 2 * q))
            pairs.append((2 * (devices - 1 - p) + 1, 2 * (devices - 1 - q) + 1))
    return pairs


def grads_of(scale_ref, left, block, match=None):
    product = lax.dot_general(
        left, block, (((1,), (1,)), ((), ())), preferred_element_type=jnp.float32
    )
    value = 1.0 / (scale_ref[2] + jnp.exp2(scale_ref[0] * product + scale_ref[1]))
    if match is not None:
        value = value - scale_ref[3] * match
    return value.astype(jnp.bfloat16)


def add_block(scale_ref, left_ref, refs, out_ref, match=None, fresh=False):
    block = jnp.concatenate([ref[...] for ref in refs], axis=0) if len(refs) > 1 else refs[0][...]
    grads = grads_of(scale_ref, left_ref[...], block, match)
    part = jnp.dot(grads, block, preferred_element_type=jnp.float32)
    out_ref[...] = part if fresh else out_ref[...] + part


PIECES = 4


def copy_all(pairs, sems):
    moves = []
    for source, target in pairs:
        size = source.shape[0] // PIECES
        for k in range(PIECES):
            part = pl.ds(k * size, size)
            moves.append(
                pltpu.make_async_copy(source.at[part], target.at[part], sems.at[len(moves)])
            )
    for move in moves:
        move.start()
    for move in moves:
        move.wait()


def pick_kernel(image_ref, text_ref, _, own_ref, own_b_ref, fixed_ref, sems):
    part = pl.ds(own_b_ref.shape[0], own_b_ref.shape[0])
    first = lax.axis_index("rep") == 0

    def copies(moving_ref, still_ref):
        pairs = [(moving_ref.at[part], own_b_ref), (moving_ref, own_ref), (still_ref, fixed_ref)]
        copy_all(pairs, sems)

    @pl.when(first)
    def _():
        copies(text_ref, image_ref)

    @pl.when(jnp.logical_not(first))
    def _():
        copies(image_ref, text_ref)


def write_kernel(picture_step, start, count, *refs):
    value_refs = refs[:count]
    picture_ref, caption_ref, wide_ref, sems = refs[-4:]
    to_picture = (lax.axis_index("rep") == 0) == picture_step
    size = value_refs[0].shape[0] // PIECES

    def write(target):
        moves = []
        for value_ref in value_refs:
            for k in range(PIECES):
                place = pl.ds(len(moves) * size, size)
                wide_ref[place] = value_ref[pl.ds(k * size, size)].astype(jnp.float32)
                there = target.at[pl.ds(start + len(moves) * size, size)]
                moves.append(
                    pltpu.make_async_copy(wide_ref.at[place], there, sems.at[len(moves)])
                )
                moves[-1].start()
        for move in moves:
            move.wait()

    @pl.when(to_picture)
    def _():
        write(picture_ref)

    @pl.when(jnp.logical_not(to_picture))
    def _():
        write(caption_ref)


def halves(total_ref):
    rows = total_ref.shape[0] // 2
    return total_ref.at[pl.ds(0, rows)], total_ref.at[pl.ds(rows, rows)]


def own_kernel(flag_ref, scale_ref, down_ref, along_ref, fixed_ref, own_ref, total_ref):
    mine, others = halves(total_ref)
    shape = (fixed_ref.shape[0], along_ref.shape[1])
    column = lax.broadcasted_iota(jnp.int32, shape, 1)
    row = lax.broadcasted_iota(jnp.int32, shape, 0)
    straight = (column == down_ref[...]).astype(jnp.float32)
    turned = (row == along_ref[...]).astype(jnp.float32)
    match = jnp.where(flag_ref[FIRST] == 1, straight, turned)
    add_block(scale_ref, fixed_ref, [own_ref], mine, match, fresh=True)
    others[...] = jnp.zeros_like(others)


def has(flag_ref, kind):
    core, side = flag_ref[CORE], flag_ref[SIDE]
    if kind == "own":
        return False, core == 0
    if kind == "group":
        return side == 1, side == 1
    if kind == "over":
        return core == 1, core == 1
    if kind == "two":
        return core + side == 0, jnp.logical_or(core == 1, side == 0)
    return True, True


def either(x, y):
    if x is True or y is True:
        return True
    return y if x is False else x if y is False else jnp.logical_or(x, y)


def blocks_kernel(jobs, flag_ref, scale_ref, _, fixed_ref, other_ref, *refs):
    total_ref, refs = refs[-1], list(refs[:-1])
    for kinds in jobs:
        now = [refs.pop(0) for _ in kinds]
        needed = (False, False)
        for kind in kinds:
            needed = tuple(either(x, y) for x, y in zip(needed, has(flag_ref, kind)))
        for rows_ref, sums_ref, wanted in zip((fixed_ref, other_ref), halves(total_ref), needed):
            if wanted is True:
                add_block(scale_ref, rows_ref, now, sums_ref)
            elif wanted is not False:
                pl.when(wanted)(
                    functools.partial(add_block, scale_ref, rows_ref, now, sums_ref)
                )


def last_sum(scale_ref, rows_ref, sum_ref, lasts, total_ref):
    block = lasts[0][...]
    for ref in lasts[1:]:
        block = block + ref[...]
    grads = grads_of(scale_ref, rows_ref[...], block)
    part = jnp.dot(grads, block, preferred_element_type=jnp.float32)
    total_ref[...] = sum_ref[...] + part


def last_other_kernel(flag_ref, scale_ref, rows_ref, sum_ref, *refs):
    *lasts, out_ref, total_ref = refs
    last_sum(scale_ref, rows_ref, sum_ref, lasts, total_ref)
    out_ref[...] = total_ref[...].astype(out_ref.dtype)


def last_own_kernel(flag_ref, scale_ref, rows_ref, sum_ref, *refs):
    *lasts, came_ref, out_ref, total_ref = refs
    last_sum(scale_ref, rows_ref, sum_ref, lasts, total_ref)
    whole_sum = total_ref[...] + came_ref[...].astype(jnp.float32)
    out_ref[...] = (scale_ref[4] * whole_sum).astype(out_ref.dtype)


def params():
    return pltpu.CompilerParams(vmem_limit_bytes=VMEM_BYTES)


NO_COST = pl.CostEstimate(flops=1, bytes_accessed=1, transcendentals=0)
SMEM = pl.BlockSpec(memory_space=pltpu.SMEM)
ANY = pl.BlockSpec(memory_space=pl.ANY)


def per_device(
    picture_vectors,
    caption_vectors,
    matched_caption_index,
    score_multiplier,
    score_offset,
    objective_cotangent,
):
    rows, depth = picture_vectors.shape
    devices = lax.axis_size("dp")
    first = lax.axis_index("rep") == 0
    place = lax.axis_index("dp")
    place = jnp.where(first, place, devices - 1 - place)
    flags = jnp.stack([first.astype(jnp.int32), place & 1, (place >> 1) & 1])
    log2e = 1.4426950408889634
    scale = jnp.stack(
        [
            -log2e * score_multiplier,
            -log2e * score_offset - jnp.log2(objective_cotangent),
            1.0 / objective_cotangent,
            objective_cotangent,
            score_multiplier,
        ]
    )

    def up(p):
        return (p + GROUP) % devices

    def across(p):
        return p ^ 2

    def swapped(p):
        return p ^ 1

    to_up = pairs_of(devices, up, (0, 1, 2, 3))
    passes_group = place % GROUP == 2
    to_side_1 = pairs_of(devices, across, (0, 1))
    core_1_across = pairs_of(devices, across, (1, 3))
    onward = pairs_of(devices, up, (1, 3)) + pairs_of(devices, across, (2,))
    last_step = pairs_of(devices, up, (0, 2)) + pairs_of(devices, across, (3,))
    core_swap = pairs_of(devices, swapped, (0, 1, 2, 3))
    replica_swap = [(2 * p + r, 2 * p + 1 - r) for p in range(devices) for r in range(2)]

    kind = picture_vectors.dtype
    half = rows // 2
    half_shape = jax.ShapeDtypeStruct((half, depth), kind)
    full_shape = jax.ShapeDtypeStruct((rows, depth), kind)
    vmem = pl.BlockSpec(memory_space=pltpu.VMEM)
    arrays = (picture_vectors, caption_vectors)
    own_a = jnp.where(first, caption_vectors[:half], picture_vectors[:half])
    own, own_b, fixed = pl.pallas_call(
        pick_kernel,
        out_shape=[full_shape, half_shape, full_shape],
        in_specs=[ANY, ANY, ANY],
        out_specs=[vmem, vmem, vmem],
        scratch_shapes=[pltpu.SemaphoreType.DMA((3 * PIECES,))],
        compiler_params=pltpu.CompilerParams(vmem_limit_bytes=PICK_BYTES),
        cost_estimate=NO_COST,
        name="pick",
    )(*arrays, own_a)
    down = matched_caption_index.reshape(rows, 1)

    def kernel(body, name, *operands, adds=True):
        return pl.pallas_call(
            body,
            out_shape=jax.ShapeDtypeStruct((2 * rows, depth), jnp.float32),
            in_specs=[SMEM, SMEM] + [vmem] * len(operands),
            out_specs=vmem,
            input_output_aliases={2: 0} if adds else {},
            compiler_params=params(),
            cost_estimate=NO_COST,
            name=name,
        )(flags, scale, *operands)

    def after(x, *others):
        return lax.optimization_barrier((x, *others))[0]

    def add_blocks(total, name, *jobs):
        blocks = [x for job in jobs for _, x in job]
        body = functools.partial(blocks_kernel, [[kind for kind, _ in job] for job in jobs])
        return kernel(body, name, total, fixed, other_fixed, *blocks)

    one_a, one_b = hop(own_a, to_up), hop(own_b, to_up)
    group = hop(own, to_side_1)
    other_fixed = hop(fixed, core_swap)
    sum_0 = kernel(
        own_kernel,
        "own_block",
        down,
        matched_caption_index,
        after(fixed, one_a),
        own,
        adds=False,
    )
    two_a = hop(one_a, onward)
    over_a = hop(one_a, core_1_across)
    two_b = hop(one_b, onward)
    over_b = hop(one_b, core_1_across)
    last_a = hop(jnp.where(passes_group, group[:half], after(two_a, one_b)), last_step)
    sum_1 = add_blocks(
        after(sum_0, two_a),
        "blocks_1",
        [("group", group)],
    )
    sum_2 = add_blocks(
        after(sum_1, over_a),
        "blocks_2",
        [("own", own)],
        [("one", one_a), ("one", one_b), ("over", over_a)],
    )
    last_b = hop(jnp.where(passes_group, after(group, two_b)[half:], after(two_b, sum_2)), last_step)
    sum_3 = add_blocks(
        after(sum_2, last_a),
        "blocks_3",
        [("over", over_b), ("last", last_a)],
    )
    sum_4 = add_blocks(
        sum_3,
        "blocks_4",
        [("two", two_a), ("two", two_b)],
    )
    total = sum_4

    def last_of(body, name, place, rows_of, *operands):
        block = (half, depth)
        return pl.pallas_call(
            body,
            grid=(1,),
            out_shape=half_shape,
            in_specs=[
                SMEM,
                SMEM,
                pl.BlockSpec(block, lambda i: (place % 2, 0)),
                pl.BlockSpec(block, lambda i: (place, 0)),
            ]
            + [pl.BlockSpec(block, lambda i: (0, 0))] * len(operands),
            out_specs=pl.BlockSpec(block, lambda i: (0, 0)),
            scratch_shapes=[pltpu.VMEM(block, jnp.float32)],
            compiler_params=params(),
            cost_estimate=NO_COST,
            name=name,
        )(flags, scale, rows_of, total, *operands)

    sent = [
        last_of(last_other_kernel, "last_other_a", 2, other_fixed, last_b),
        last_of(last_other_kernel, "last_other_b", 3, other_fixed, last_b),
    ]
    came = [hop(x, core_swap) for x in sent]
    mine = [
        last_of(last_own_kernel, "last_own_a", 0, fixed, last_b, came[0]),
        last_of(last_own_kernel, "last_own_b", 1, fixed, last_b, came[1]),
    ]
    theirs = [hop(x, replica_swap) for x in mine]
    out_shape = jax.ShapeDtypeStruct((rows, depth), jnp.float32)

    def write(picture_step, start, values, outs, name):
        count = len(values)
        return pl.pallas_call(
            functools.partial(write_kernel, picture_step, start, count),
            out_shape=[out_shape, out_shape],
            in_specs=[vmem] * count + [ANY] * len(outs),
            out_specs=[ANY, ANY],
            scratch_shapes=[
                pltpu.VMEM((count * half, depth), jnp.float32),
                pltpu.SemaphoreType.DMA((count * PIECES,)),
            ],
            input_output_aliases={count + k: k for k in range(len(outs))},
            compiler_params=params(),
            cost_estimate=NO_COST,
            name=name,
        )(*values, *outs)

    outs = write(True, 0, mine, (), "write_mine")
    outs = write(False, 0, theirs[:1], outs, "write_theirs_a")
    return tuple(write(False, half, theirs[1:], outs, "write_theirs_b"))


def solution(mesh):
    placed = (P("dp", None), P("dp", None), P("dp", None), P(), P(), P())
    return jax.shard_map(
        per_device,
        mesh=mesh,
        in_specs=placed,
        out_specs=(P("dp", None), P("dp", None)),
        check_vma=False,
    )
```

time: 107 us -> 103 us (0.963)
  Pallas kernels: 35.8 us -> 31.8 us
  starting transfers between devices: 27.4 us -> 24.3 us
  waiting for transfers between devices: 37.2 us -> 39.3 us
  other arithmetic: 0.08 us -> 1.53 us
    pallas_call x11 -> x10, Pallas kernels: 32.2 us -> 28.2 us  [the longest x5 18.7 us: kernel(): pl.pallas_call(body, out_shape=jax.ShapeDtypeStruct((2 * rows, depth), jn...]
    ppermute x15 -> x14, starting transfers between devices: 27.4 us -> 24.3 us  [hop(): return lax.ppermute(x, ('dp', 'rep'), pairs)]
    ppermute x15 -> x14, waiting for transfers between devices: 37.2 us -> 39.3 us  [hop(): return lax.ppermute(x, ('dp', 'rep'), pairs)]
    select_n x0 -> x3, other arithmetic: none -> 1.45 us  [the longest x1 1.32 us: per_device(): own_a = jnp.where(first, caption_vectors[:half], picture_vectors[:half])]
    unnamed x12 -> x10, local copies, waits for them, and re-layouts: 2.35 us -> 2.55 us
  transfers between devices with their start and end apart: 15 -> 14, of which waited for: 7 -> 5; matrix products, arithmetic and copies ran while one was open for 0% -> 0% of each run, Pallas kernels for 29% -> 28%
where the time goes in v5:
time: 103 us
  waiting for transfers between devices  39.3 us (38%)
  Pallas kernels  31.8 us (31%)
  starting transfers between devices  24.3 us (24%)
  between operations  3.1 us (3%)
  local copies, waits for them, and re-layouts  2.79 us (3%)
  other arithmetic  1.53 us (1%)
    ppermute x14, waiting for transfers between devices, hop(): return lax.ppermute(x, ('dp', 'rep'), pairs)  39.3 us
    ppermute x14, starting transfers between devices, hop(): return lax.ppermute(x, ('dp', 'rep'), pairs)  24.3 us
    pallas_call x5, Pallas kernels, kernel(): pl.pallas_call(body, out_shape=jax.ShapeDtypeStruct((2 * rows, depth), jn...  18.7 us
    pallas_call x4, Pallas kernels, last_of(): pl.pallas_call(body, grid=(1,), out_shape=half_shape, in_specs=[SMEM, SME...  5.91 us
    pallas_call x3, Pallas kernels, write(): pl.pallas_call(functools.partial(write_kernel, picture_step, start, count...  3.6 us
    pallas_call x1, Pallas kernels, per_device(): pl.pallas_call(pick_kernel, out_shape=[full_shape, half_shape, full_shape...  3.57 us
    unnamed x10, local copies, waits for them, and re-layouts  2.55 us
  transfers between devices with their start and end apart: 14, of which 5 were waited for; matrix products, arithmetic and copies ran while one was open for 0% of the time, Pallas kernels for 28%

profile of v5, /device:TPU:0, one launch (start us, length us, event | category | flops | bytes accessed | tf_op | source)
XLA Modules:
  0.0 102.9 jit_solution(1049266696692007314)
XLA Ops:
  0.6 1.3 %slice_select_fusion.2._ = bf16[256,1152]{1,0:T(8,128)(2,1)S(1)} fusion(bf16[512,1152]{1,0:T(8,128)(2,1)} %image_ref.1, bf16[512,1152]{1,0:T(8,128)(2,1)} %text_ref.1, pred[]{:T(512)S(6)} %eq.8), kind=kLoop, calls=%fused_computation.2 | loop fusion | flops 294912 | bytes 1769473 | tf_op jit(solution)/shard_map/jit(_where)/select_n | solution.py:245
  2.0 3.1 %collective-permute-start = (bf16[256,1152]{1,0:T(8,128)(2,1)S(1)}, bf16[256,1152]{1,0:T(8,128)(2,1)}, u32[]{:S(2)}, u32[]{:S(2)}) collective-permute-start(bf16[256,1152]{1,0:T(8,128)(2,1)S(1)} %slice_select_fusion.2._), channel_id=1, source_target_pairs={{0,8},{31,23},{2,10},{29,21},{4,12},{27,19},{6,14},{25,17},{8,16},... | collective-permute-start | bytes 1769480 | tf_op jit(solution)/shard_map/ppermute | solution.py:19
  5.1 3.6 %pick.1 = (bf16[512,1152]{1,0:T(8,128)(2,1)}, bf16[256,1152]{1,0:T(8,128)(2,1)}, bf16[512,1152]{1,0:T(8,128)(2,1)}) custom-call(bf16[512,1152]{1,0:T(8,128)(2,1)} %image_ref.1, bf16[512,1152]{1,0:T(8,128)(2,1)} %text_ref.1, bf16[256,1152]{1,0:T(8,128)(2,1)} %copy-done.4), custom_call_target="tpu_custom_call" | custom-call | flops 1 | bytes 1 | tf_op jit(solution)/shard_map/pick/pallas_call | solution.py:246
  8.6 0.1 collective-permute-start.2
  8.7 3.5 %collective-permute-start.3 = (bf16[512,1152]{1,0:T(8,128)(2,1)}, bf16[512,1152]{1,0:T(8,128)(2,1)S(1)}, u32[]{:S(2)}, u32[]{:S(2)}) collective-permute-start(bf16[512,1152]{1,0:T(8,128)(2,1)} %get-tuple-element.18.own_ref.refs_0_), channel_id=1, source_target_pairs={{0,4},{31,27},{2,6},{29,25},{8,12},{23,19},{10,14},{21,17},{16,20}... | collective-permute-start | bytes 3538952 | tf_op jit(solution)/shard_map/ppermute | solution.py:19
  12.2 1.6 %collective-permute-start.5 = (bf16[256,1152]{1,0:T(8,128)(2,1)}, bf16[256,1152]{1,0:T(8,128)(2,1)}, u32[]{:S(2)}, u32[]{:S(2)}) collective-permute-start(bf16[256,1152]{1,0:T(8,128)(2,1)} %get-tuple-element.21), channel_id=1, source_target_pairs={{0,8},{31,23},{2,10},{29,21},{4,12},{27,19},{6,14},{25,17},{8,16},... | collective-permute-start | bytes 1769480 | tf_op jit(solution)/shard_map/ppermute | solution.py:19
  13.8 7.5 %collective-permute-done.refs_1_ = bf16[256,1152]{1,0:T(8,128)(2,1)} collective-permute-done((bf16[256,1152]{1,0:T(8,128)(2,1)S(1)}, bf16[256,1152]{1,0:T(8,128)(2,1)}, u32[]{:S(2)}, u32[]{:S(2)}) %collective-permute-start) | collective-permute-done | bytes 589856 | tf_op jit(solution)/shard_map/ppermute | solution.py:19
  21.3 1.3 %collective-permute-start.1 = (bf16[256,1152]{1,0:T(8,128)(2,1)}, bf16[256,1152]{1,0:T(8,128)(2,1)S(1)}, u32[]{:S(2)}, u32[]{:S(2)}) collective-permute-start(bf16[256,1152]{1,0:T(8,128)(2,1)} %collective-permute-done.refs_1_), channel_id=1, source_target_pairs={{2,10},{29,21},{6,14},{25,17},{10,18},{21,13},{14,22},{17,9},{18,2... | collective-permute-start | bytes 1769480 | tf_op jit(solution)/shard_map/ppermute | solution.py:19
  22.6 1.5 %collective-permute-start.4 = (bf16[256,1152]{1,0:T(8,128)(2,1)}, bf16[256,1152]{1,0:T(8,128)(2,1)}, u32[]{:S(2)}, u32[]{:S(2)}) collective-permute-start(bf16[256,1152]{1,0:T(8,128)(2,1)} %collective-permute-done.refs_1_), channel_id=1, source_target_pairs={{2,6},{29,25},{6,2},{25,29},{10,14},{21,17},{14,10},{17,21},{18,22... | collective-permute-start | bytes 1769480 | tf_op jit(solution)/shard_map/ppermute | solution.py:19
  26.2 0.1 copy.16.down_ref
  26.3 0.1 stack.43.scale_ref
  26.4 7.6 %collective-permute-done.5.refs_2_ = bf16[256,1152]{1,0:T(8,128)(2,1)} collective-permute-done((bf16[256,1152]{1,0:T(8,128)(2,1)}, bf16[256,1152]{1,0:T(8,128)(2,1)}, u32[]{:S(2)}, u32[]{:S(2)}) %collective-permute-start.5) | collective-permute-done | bytes 589856 | tf_op jit(solution)/shard_map/ppermute | solution.py:19
  34.0 1.3 %collective-permute-start.8 = (bf16[256,1152]{1,0:T(8,128)(2,1)}, bf16[256,1152]{1,0:T(8,128)(2,1)S(1)}, u32[]{:S(2)}, u32[]{:S(2)}) collective-permute-start(bf16[256,1152]{1,0:T(8,128)(2,1)} %collective-permute-done.5.refs_2_), channel_id=1, source_target_pairs={{2,10},{29,21},{6,14},{25,17},{10,18},{21,13},{14,22},{17,9},{18,2... | collective-permute-start | bytes 1769480 | tf_op jit(solution)/shard_map/ppermute | solution.py:19
  35.3 0.1 pad_add_fusion.flag_ref
  35.4 1.3 %copy-done = bf16[512,1152]{1,0:T(8,128)(2,1)S(1)} copy-done((bf16[512,1152]{1,0:T(8,128)(2,1)S(1)}, bf16[512,1152]{1,0:T(8,128)(2,1)}, u32[]{:S(2)}) %copy-start) | copy-done | bytes 1179672
  36.6 1.3 %copy-done.2 = bf16[512,1152]{1,0:T(8,128)(2,1)S(1)} copy-done((bf16[512,1152]{1,0:T(8,128)(2,1)S(1)}, bf16[512,1152]{1,0:T(8,128)(2,1)}, u32[]{:S(2)}) %copy-start.2) | copy-done | bytes 1179672
  37.9 2.5 %own_block.1._ = f32[1024,1152]{1,0:T(8,128)S(1)} custom-call(s32[3]{0:T(128)S(1)} %pad_add_fusion.flag_ref, f32[5]{0:T(128)S(1)} %stack.43.scale_ref, s32[512,1]{1,0:T(8,128)S(1)} %copy.16.down_ref, s32[1,512]{1,0:T(1,128)S(1)} %copy-done.3, bf16[512,1152]{1,0:T(8,128)(2,1)S(1)} %copy-done, bf16[512,1152]{1,0:T(8,128)(2,1)S(1)} %copy-done.2), custom_call_target="tpu_custom_call" | custom-call | flops 1 | bytes 1 | tf_op jit(solution)/shard_map/own_block/pallas_call | solution.py:259
  40.4 0.0 collective-permute-done.1.refs_0_
  40.4 0.7 collective-permute-start.7
  41.1 0.0 collective-permute-done.2.other_ref.rows_ref
  41.1 0.0 collective-permute-done.3.refs_0_
  41.1 0.6 blocks_1.1._
  41.7 0.1 slice_select_fusion
  41.8 1.9 %collective-permute-start.6 = (bf16[256,1152]{1,0:T(8,128)(2,1)S(1)}, bf16[256,1152]{1,0:T(8,128)(2,1)S(1)}, u32[]{:S(2)}, u32[]{:S(2)}) collective-permute-start(bf16[256,1152]{1,0:T(8,128)(2,1)S(1)} %slice_select_fusion), channel_id=1, source_target_pairs={{0,8},{31,23},{4,12},{27,19},{8,16},{23,15},{12,20},{19,11},{16,24... | collective-permute-start | bytes 1769480 | tf_op jit(solution)/shard_map/ppermute | solution.py:19
  43.7 8.0 %blocks_2.1._ = f32[1024,1152]{1,0:T(8,128)S(1)} custom-call(s32[3]{0:T(128)S(1)} %pad_add_fusion.flag_ref, f32[5]{0:T(128)S(1)} %stack.43.scale_ref, f32[1024,1152]{1,0:T(8,128)S(1)} %blocks_1.1._, bf16[512,1152]{1,0:T(8,128)(2,1)S(1)} %copy-done.1, bf16[512,1152]{1,0:T(8,128)(2,1)S(1)} %collective-permute-done.2.other_ref.rows_ref, ...), custom_call_target="tpu_custom_call", output_to_operand_aliasing={{}: (2, {})} | custom-call | flops 1 | bytes 1 | tf_op jit(solution)/shard_map/blocks_2/pallas_call | solution.py:259
  51.7 0.0 collective-permute-done.8.refs_1_
  51.7 0.1 slice_select_fusion.1
  51.8 3.7 %collective-permute-start.9 = (bf16[256,1152]{1,0:T(8,128)(2,1)S(1)}, bf16[256,1152]{1,0:T(8,128)(2,1)S(1)}, u32[]{:S(2)}, u32[]{:S(2)}) collective-permute-start(bf16[256,1152]{1,0:T(8,128)(2,1)S(1)} %slice_select_fusion.1), channel_id=1, source_target_pairs={{0,8},{31,23},{4,12},{27,19},{8,16},{23,15},{12,20},{19,11},{16,24... | collective-permute-start | bytes 1769480 | tf_op jit(solution)/shard_map/ppermute | solution.py:19
  55.5 0.0 collective-permute-done.6.refs_1_
  55.5 0.0 collective-permute-done.7.refs_0_
  55.5 3.8 %blocks_3.1._ = f32[1024,1152]{1,0:T(8,128)S(1)} custom-call(s32[3]{0:T(128)S(1)} %pad_add_fusion.flag_ref, f32[5]{0:T(128)S(1)} %stack.43.scale_ref, f32[1024,1152]{1,0:T(8,128)S(1)} %blocks_2.1._, bf16[512,1152]{1,0:T(8,128)(2,1)S(1)} %copy-done.1, bf16[512,1152]{1,0:T(8,128)(2,1)S(1)} %collective-permute-done.2.other_ref.rows_ref, ...), custom_call_target="tpu_custom_call", output_to_operand_aliasing={{}: (2, {})} | custom-call | flops 1 | bytes 1 | tf_op jit(solution)/shard_map/blocks_3/pallas_call | solution.py:259
  59.3 4.0 %blocks_4.1.sum_ref = f32[1024,1152]{1,0:T(8,128)S(1)} custom-call(s32[3]{0:T(128)S(1)} %pad_add_fusion.flag_ref, f32[5]{0:T(128)S(1)} %stack.43.scale_ref, f32[1024,1152]{1,0:T(8,128)S(1)} %blocks_3.1._, bf16[512,1152]{1,0:T(8,128)(2,1)S(1)} %copy-done.1, ...), custom_call_target="tpu_custom_call", output_to_operand_aliasing={{}: (2, {})} | custom-call | flops 1 | bytes 1 | tf_op jit(solution)/shard_map/blocks_4/pallas_call | solution.py:259
  63.2 2.1 %collective-permute-done.9.refs_0_ = bf16[256,1152]{1,0:T(8,128)(2,1)S(1)} collective-permute-done((bf16[256,1152]{1,0:T(8,128)(2,1)S(1)}, bf16[256,1152]{1,0:T(8,128)(2,1)S(1)}, u32[]{:S(2)}, u32[]{:S(2)}) %collective-permute-start.9) | collective-permute-done | bytes 589856 | tf_op jit(solution)/shard_map/ppermute | solution.py:19
  65.4 1.5 %last_other_a.1 = bf16[256,1152]{1,0:T(8,128)(2,1)S(1)} custom-call(s32[3]{0:T(128)S(1)} %pad_add_fusion.flag_ref, f32[5]{0:T(128)S(1)} %stack.43.scale_ref, bf16[512,1152]{1,0:T(8,128)(2,1)S(1)} %collective-permute-done.2.other_ref.rows_ref, f32[1024,1152]{1,0:T(8,128)S(1)} %blocks_4.1.sum_ref, bf16[256,1152]{1,0:T(8,128)(2,1)S(1)} %collective-permute-done.9.refs_0_), custom_call_target="tpu_custom_call" | custom-call | flops 1 | bytes 1 | tf_op jit(solution)/shard_map/last_other_a/pallas_call | solution.py:321
  66.8 0.1 collective-permute-start.12
  66.9 1.5 %last_other_b.1 = bf16[256,1152]{1,0:T(8,128)(2,1)S(1)} custom-call(s32[3]{0:T(128)S(1)} %pad_add_fusion.flag_ref, f32[5]{0:T(128)S(1)} %stack.43.scale_ref, bf16[512,1152]{1,0:T(8,128)(2,1)S(1)} %collective-permute-done.2.other_ref.rows_ref, f32[1024,1152]{1,0:T(8,128)S(1)} %blocks_4.1.sum_ref, bf16[256,1152]{1,0:T(8,128)(2,1)S(1)} %collective-permute-done.9.refs_0_), custom_call_target="tpu_custom_call" | custom-call | flops 1 | bytes 1 | tf_op jit(solution)/shard_map/last_other_b/pallas_call | solution.py:321
  68.4 0.6 collective-permute-start.10
  69.0 0.0 collective-permute-done.12.refs_1_
  69.0 1.5 %last_own_a.1.refs_0_ = bf16[256,1152]{1,0:T(8,128)(2,1)S(1)} custom-call(s32[3]{0:T(128)S(1)} %pad_add_fusion.flag_ref, f32[5]{0:T(128)S(1)} %stack.43.scale_ref, bf16[512,1152]{1,0:T(8,128)(2,1)S(1)} %copy-done.1, f32[1024,1152]{1,0:T(8,128)S(1)} %blocks_4.1.sum_ref, bf16[256,1152]{1,0:T(8,128)(2,1)S(1)} %collective-permute-done.9.refs_0_, ...), custom_call_target="tpu_custom_call" | custom-call | flops 1 | bytes 1 | tf_op jit(solution)/shard_map/last_own_a/pallas_call | solution.py:321
  70.5 4.7 %collective-permute-start.13 = (bf16[256,1152]{1,0:T(8,128)(2,1)S(1)}, bf16[256,1152]{1,0:T(8,128)(2,1)S(1)}, u32[]{:S(2)}, u32[]{:S(2)}) collective-permute-start(bf16[256,1152]{1,0:T(8,128)(2,1)S(1)} %last_own_a.1.refs_0_), channel_id=1, source_target_pairs={{0,1},{1,0},{2,3},{3,2},{4,5},{5,4},{6,7},{7,6},{8,9},{9,8},{10,11... | collective-permute-start | bytes 1769480 | tf_op jit(solution)/shard_map/ppermute | solution.py:19
  75.1 0.0 collective-permute-done.10.refs_1_
  75.1 1.5 %last_own_b.1.refs_1_ = bf16[256,1152]{1,0:T(8,128)(2,1)S(1)} custom-call(s32[3]{0:T(128)S(1)} %pad_add_fusion.flag_ref, f32[5]{0:T(128)S(1)} %stack.43.scale_ref, bf16[512,1152]{1,0:T(8,128)(2,1)S(1)} %copy-done.1, f32[1024,1152]{1,0:T(8,128)S(1)} %blocks_4.1.sum_ref, bf16[256,1152]{1,0:T(8,128)(2,1)S(1)} %collective-permute-done.9.refs_0_, ...), custom_call_target="tpu_custom_call" | custom-call | flops 1 | bytes 1 | tf_op jit(solution)/shard_map/last_own_b/pallas_call | solution.py:321
  76.6 0.4 collective-permute-start.11
  77.0 1.5 %write_mine.1 = (f32[512,1152]{1,0:T(8,128)}, f32[512,1152]{1,0:T(8,128)}) custom-call(bf16[256,1152]{1,0:T(8,128)(2,1)S(1)} %last_own_a.1.refs_0_, bf16[256,1152]{1,0:T(8,128)(2,1)S(1)} %last_own_b.1.refs_1_), custom_call_target="tpu_custom_call" | custom-call | flops 1 | bytes 1 | tf_op jit(solution)/shard_map/write_mine/pallas_call | solution.py:353
  78.5 10.8 %collective-permute-done.13.refs_0_ = bf16[256,1152]{1,0:T(8,128)(2,1)S(1)} collective-permute-done((bf16[256,1152]{1,0:T(8,128)(2,1)S(1)}, bf16[256,1152]{1,0:T(8,128)(2,1)S(1)}, u32[]{:S(2)}, u32[]{:S(2)}) %collective-permute-start.13) | collective-permute-done | bytes 589856 | tf_op jit(solution)/shard_map/ppermute | solution.py:19
  89.3 1.1 %write_theirs_a.1 = (f32[512,1152]{1,0:T(8,128)}, f32[512,1152]{1,0:T(8,128)}) custom-call(bf16[256,1152]{1,0:T(8,128)(2,1)S(1)} %collective-permute-done.13.refs_0_, f32[512,1152]{1,0:T(8,128)} %get-tuple-element.26.refs_1_, f32[512,1152]{1,0:T(8,128)} %get-tuple-element.27.refs_2_), custom_call_target="tpu_custom_call", output_to_operand_aliasing={{0}: (1, {}), {1}: (2, {})} | custom-call | flops 1 | bytes 1 | tf_op jit(solution)/shard_map/write_theirs_a/pallas_call | solution.py:353
  90.4 11.3 %collective-permute-done.11.refs_0_ = bf16[256,1152]{1,0:T(8,128)(2,1)S(1)} collective-permute-done((bf16[256,1152]{1,0:T(8,128)(2,1)S(1)}, bf16[256,1152]{1,0:T(8,128)(2,1)S(1)}, u32[]{:S(2)}, u32[]{:S(2)}) %collective-permute-start.11) | collective-permute-done | bytes 589856 | tf_op jit(solution)/shard_map/ppermute | solution.py:19
  101.7 1.1 %write_theirs_b.1 = (f32[512,1152]{1,0:T(8,128)}, f32[512,1152]{1,0:T(8,128)}) custom-call(bf16[256,1152]{1,0:T(8,128)(2,1)S(1)} %collective-permute-done.11.refs_0_, f32[512,1152]{1,0:T(8,128)} %get-tuple-element.28.refs_1_, f32[512,1152]{1,0:T(8,128)} %get-tuple-element.29.refs_2_), custom_call_target="tpu_custom_call", output_to_operand_aliasing={{0}: (1, {}), {1}: (2, {})} | custom-call | flops 1 | bytes 1 | tf_op jit(solution)/shard_map/write_theirs_b/pallas_call | solution.py:353
  (9 shorter events, 0.0 us)
Async XLA Ops:
  0.6 25.5 %copy-start.3 = (s32[1,512]{1,0:T(1,128)S(1)}, s32[1,512]{1,0:T(1,128)}, u32[]{:S(2)}) copy-start(s32[1,512]{1,0:T(1,128)} %along_ref.1) | copy-start | bytes 6148
  2.0 3.1 %copy-start.4 = (bf16[256,1152]{1,0:T(8,128)(2,1)}, bf16[256,1152]{1,0:T(8,128)(2,1)S(1)}, u32[]{:S(2)}) copy-start(bf16[256,1152]{1,0:T(8,128)(2,1)S(1)} %slice_select_fusion.2._) | copy-start | bytes 1769476
  2.0 19.4 %collective-permute-start = (bf16[256,1152]{1,0:T(8,128)(2,1)S(1)}, bf16[256,1152]{1,0:T(8,128)(2,1)}, u32[]{:S(2)}, u32[]{:S(2)}) collective-permute-start(bf16[256,1152]{1,0:T(8,128)(2,1)S(1)} %slice_select_fusion.2._), channel_id=1, source_target_pairs={{0,8},{31,23},{2,10},{29,21},{4,12},{27,19},{6,14},{25,17},{8,16},... | collective-permute-start | bytes 1769480 | tf_op jit(solution)/shard_map/ppermute | solution.py:19
  8.6 32.5 %collective-permute-start.2 = (bf16[512,1152]{1,0:T(8,128)(2,1)}, bf16[512,1152]{1,0:T(8,128)(2,1)S(1)}, u32[]{:S(2)}, u32[]{:S(2)}) collective-permute-start(bf16[512,1152]{1,0:T(8,128)(2,1)} %get-tuple-element.17.fixed_ref.rows_ref), channel_id=1, source_target_pairs={{0,2},{31,29},{2,0},{29,31},{4,6},{27,25},{6,4},{25,27},{8,10},{23... | collective-permute-start | bytes 3538952 | tf_op jit(solution)/shard_map/ppermute | solution.py:19
  8.7 32.4 %collective-permute-start.3 = (bf16[512,1152]{1,0:T(8,128)(2,1)}, bf16[512,1152]{1,0:T(8,128)(2,1)S(1)}, u32[]{:S(2)}, u32[]{:S(2)}) collective-permute-start(bf16[512,1152]{1,0:T(8,128)(2,1)} %get-tuple-element.18.own_ref.refs_0_), channel_id=1, source_target_pairs={{0,4},{31,27},{2,6},{29,25},{8,12},{23,19},{10,14},{21,17},{16,20}... | collective-permute-start | bytes 3538952 | tf_op jit(solution)/shard_map/ppermute | solution.py:19
  12.2 21.8 %collective-permute-start.5 = (bf16[256,1152]{1,0:T(8,128)(2,1)}, bf16[256,1152]{1,0:T(8,128)(2,1)}, u32[]{:S(2)}, u32[]{:S(2)}) collective-permute-start(bf16[256,1152]{1,0:T(8,128)(2,1)} %get-tuple-element.21), channel_id=1, source_target_pairs={{0,8},{31,23},{2,10},{29,21},{4,12},{27,19},{6,14},{25,17},{8,16},... | collective-permute-start | bytes 1769480 | tf_op jit(solution)/shard_map/ppermute | solution.py:19
  21.3 19.0 %collective-permute-start.1 = (bf16[256,1152]{1,0:T(8,128)(2,1)}, bf16[256,1152]{1,0:T(8,128)(2,1)S(1)}, u32[]{:S(2)}, u32[]{:S(2)}) collective-permute-start(bf16[256,1152]{1,0:T(8,128)(2,1)} %collective-permute-done.refs_1_), channel_id=1, source_target_pairs={{2,10},{29,21},{6,14},{25,17},{10,18},{21,13},{14,22},{17,9},{18,2... | collective-permute-start | bytes 1769480 | tf_op jit(solution)/shard_map/ppermute | solution.py:19
  22.6 19.1 %collective-permute-start.4 = (bf16[256,1152]{1,0:T(8,128)(2,1)}, bf16[256,1152]{1,0:T(8,128)(2,1)}, u32[]{:S(2)}, u32[]{:S(2)}) collective-permute-start(bf16[256,1152]{1,0:T(8,128)(2,1)} %collective-permute-done.refs_1_), channel_id=1, source_target_pairs={{2,6},{29,25},{6,2},{25,29},{10,14},{21,17},{14,10},{17,21},{18,22... | collective-permute-start | bytes 1769480 | tf_op jit(solution)/shard_map/ppermute | solution.py:19
  34.0 17.7 %collective-permute-start.8 = (bf16[256,1152]{1,0:T(8,128)(2,1)}, bf16[256,1152]{1,0:T(8,128)(2,1)S(1)}, u32[]{:S(2)}, u32[]{:S(2)}) collective-permute-start(bf16[256,1152]{1,0:T(8,128)(2,1)} %collective-permute-done.5.refs_2_), channel_id=1, source_target_pairs={{2,10},{29,21},{6,14},{25,17},{10,18},{21,13},{14,22},{17,9},{18,2... | collective-permute-start | bytes 1769480 | tf_op jit(solution)/shard_map/ppermute | solution.py:19
  35.3 1.3 %copy-start = (bf16[512,1152]{1,0:T(8,128)(2,1)S(1)}, bf16[512,1152]{1,0:T(8,128)(2,1)}, u32[]{:S(2)}) copy-start(bf16[512,1152]{1,0:T(8,128)(2,1)} %get-tuple-element.17.fixed_ref.rows_ref) | copy-start | bytes 3538948
  36.6 1.3 %copy-start.2 = (bf16[512,1152]{1,0:T(8,128)(2,1)S(1)}, bf16[512,1152]{1,0:T(8,128)(2,1)}, u32[]{:S(2)}) copy-start(bf16[512,1152]{1,0:T(8,128)(2,1)} %get-tuple-element.18.own_ref.refs_0_) | copy-start | bytes 3538948
  37.9 3.2 %copy-start.1 = (bf16[512,1152]{1,0:T(8,128)(2,1)S(1)}, bf16[512,1152]{1,0:T(8,128)(2,1)}, u32[]{:S(2)}) copy-start(bf16[512,1152]{1,0:T(8,128)(2,1)} %get-tuple-element.17.fixed_ref.rows_ref) | copy-start | bytes 3538948
  40.4 15.1 %collective-permute-start.7 = (bf16[256,1152]{1,0:T(8,128)(2,1)}, bf16[256,1152]{1,0:T(8,128)(2,1)S(1)}, u32[]{:S(2)}, u32[]{:S(2)}) collective-permute-start(bf16[256,1152]{1,0:T(8,128)(2,1)} %collective-permute-done.5.refs_2_), channel_id=1, source_target_pairs={{2,6},{29,25},{6,2},{25,29},{10,14},{21,17},{14,10},{17,21},{18,22... | collective-permute-start | bytes 1769480 | tf_op jit(solution)/shard_map/ppermute | solution.py:19
  41.8 13.7 %collective-permute-start.6 = (bf16[256,1152]{1,0:T(8,128)(2,1)S(1)}, bf16[256,1152]{1,0:T(8,128)(2,1)S(1)}, u32[]{:S(2)}, u32[]{:S(2)}) collective-permute-start(bf16[256,1152]{1,0:T(8,128)(2,1)S(1)} %slice_select_fusion), channel_id=1, source_target_pairs={{0,8},{31,23},{4,12},{27,19},{8,16},{23,15},{12,20},{19,11},{16,24... | collective-permute-start | bytes 1769480 | tf_op jit(solution)/shard_map/ppermute | solution.py:19
  51.8 13.6 %collective-permute-start.9 = (bf16[256,1152]{1,0:T(8,128)(2,1)S(1)}, bf16[256,1152]{1,0:T(8,128)(2,1)S(1)}, u32[]{:S(2)}, u32[]{:S(2)}) collective-permute-start(bf16[256,1152]{1,0:T(8,128)(2,1)S(1)} %slice_select_fusion.1), channel_id=1, source_target_pairs={{0,8},{31,23},{4,12},{27,19},{8,16},{23,15},{12,20},{19,11},{16,24... | collective-permute-start | bytes 1769480 | tf_op jit(solution)/shard_map/ppermute | solution.py:19
  66.8 2.1 %collective-permute-start.12 = (bf16[256,1152]{1,0:T(8,128)(2,1)S(1)}, bf16[256,1152]{1,0:T(8,128)(2,1)S(1)}, u32[]{:S(2)}, u32[]{:S(2)}) collective-permute-start(bf16[256,1152]{1,0:T(8,128)(2,1)S(1)} %last_other_a.1), channel_id=1, source_target_pairs={{0,2},{31,29},{2,0},{29,31},{4,6},{27,25},{6,4},{25,27},{8,10},{23... | collective-permute-start | bytes 1769480 | tf_op jit(solution)/shard_map/ppermute | solution.py:19
  68.4 6.7 %collective-permute-start.10 = (bf16[256,1152]{1,0:T(8,128)(2,1)S(1)}, bf16[256,1152]{1,0:T(8,128)(2,1)S(1)}, u32[]{:S(2)}, u32[]{:S(2)}) collective-permute-start(bf16[256,1152]{1,0:T(8,128)(2,1)S(1)} %last_other_b.1), channel_id=1, source_target_pairs={{0,2},{31,29},{2,0},{29,31},{4,6},{27,25},{6,4},{25,27},{8,10},{23... | collective-permute-start | bytes 1769480 | tf_op jit(solution)/shard_map/ppermute | solution.py:19
  70.5 18.8 %collective-permute-start.13 = (bf16[256,1152]{1,0:T(8,128)(2,1)S(1)}, bf16[256,1152]{1,0:T(8,128)(2,1)S(1)}, u32[]{:S(2)}, u32[]{:S(2)}) collective-permute-start(bf16[256,1152]{1,0:T(8,128)(2,1)S(1)} %last_own_a.1.refs_0_), channel_id=1, source_target_pairs={{0,1},{1,0},{2,3},{3,2},{4,5},{5,4},{6,7},{7,6},{8,9},{9,8},{10,11... | collective-permute-start | bytes 1769480 | tf_op jit(solution)/shard_map/ppermute | solution.py:19
  76.6 25.1 %collective-permute-start.11 = (bf16[256,1152]{1,0:T(8,128)(2,1)S(1)}, bf16[256,1152]{1,0:T(8,128)(2,1)S(1)}, u32[]{:S(2)}, u32[]{:S(2)}) collective-permute-start(bf16[256,1152]{1,0:T(8,128)(2,1)S(1)} %last_own_b.1.refs_1_), channel_id=1, source_target_pairs={{0,1},{1,0},{2,3},{3,2},{4,5},{5,4},{6,7},{7,6},{8,9},{9,8},{10,11... | collective-permute-start | bytes 1769480 | tf_op jit(solution)/shard_map/ppermute | solution.py:19

commit v6 on v5

--- a/solution.py
+++ b/solution.py
@@ -10,7 +10,7 @@
 GROUP = 4
 VMEM_BYTES = 36 * 1024 * 1024
 NO_ROOM = 60 * 1024 * 1024
-PICK_BYTES = NO_ROOM
+PICK_BYTES = 8 * 1024 * 1024
 
 FIRST, CORE, SIDE = 0, 1, 2
 
@@ -300,13 +300,13 @@
     sum_2 = add_blocks(
         after(sum_1, over_a),
         "blocks_2",
-        [("own", own)],
         [("one", one_a), ("one", one_b), ("over", over_a)],
     )
     last_b = hop(jnp.where(passes_group, after(group, two_b)[half:], after(two_b, sum_2)), last_step)
     sum_3 = add_blocks(
         after(sum_2, last_a),
         "blocks_3",
+        [("own", own)],
         [("over", over_b), ("last", last_a)],
     )
     sum_4 = add_blocks(

time: 103 us -> 104 us (level)
  waiting for transfers between devices: 39.3 us -> 36.2 us
  other arithmetic: 1.53 us -> 3.94 us
    ppermute x14, waiting for transfers between devices: 39.3 us -> 36.2 us  [hop(): return lax.ppermute(x, ('dp', 'rep'), pairs)]
    pallas_call x5, Pallas kernels: 18.7 us -> 20.2 us  [kernel(): pl.pallas_call(body, out_shape=jax.ShapeDtypeStruct((2 * rows, depth), jn...]
    pallas_call x1, Pallas kernels: 3.57 us -> 2.15 us  [per_device(): pl.pallas_call(pick_kernel, out_shape=[full_shape, half_shape, full_shape...]
    select_n x1, other arithmetic: 0.07 us -> 1.32 us  [per_device(): jnp.where(passes_group, group[:half], after(two_a, one_b))]
    select_n x1, other arithmetic: 0.07 us -> 1.14 us  [per_device(): jnp.where(passes_group, after(group, two_b)[half:], after(two_b, sum_2))]
    unnamed x10 -> x8, local copies, waits for them, and re-layouts: 2.55 us -> 2.23 us
  transfers between devices with their start and end apart: 14 -> 14, of which waited for: 5 -> 6; matrix products, arithmetic and copies ran while one was open for 0% -> 3% of each run, Pallas kernels for 28% -> 28%
where the time goes in v6:
time: 104 us; the launch traced here: 103 us
  waiting for transfers between devices  36.2 us (35%)
  Pallas kernels  31.9 us (31%)
  starting transfers between devices  24.8 us (24%)
  other arithmetic  3.94 us (4%)
  local copies, waits for them, and re-layouts  3.17 us (3%)
  between operations  3.04 us (3%)
    ppermute x14, waiting for transfers between devices, hop(): return lax.ppermute(x, ('dp', 'rep'), pairs)  36.2 us
    ppermute x14, starting transfers between devices, hop(): return lax.ppermute(x, ('dp', 'rep'), pairs)  24.8 us
    pallas_call x5, Pallas kernels, kernel(): pl.pallas_call(body, out_shape=jax.ShapeDtypeStruct((2 * rows, depth), jn...  20.2 us
    pallas_call x4, Pallas kernels, last_of(): pl.pallas_call(body, grid=(1,), out_shape=half_shape, in_specs=[SMEM, SME...  5.93 us
    pallas_call x3, Pallas kernels, write(): pl.pallas_call(functools.partial(write_kernel, picture_step, start, count...  3.6 us
    unnamed x8, local copies, waits for them, and re-layouts  2.23 us
    pallas_call x1, Pallas kernels, per_device(): pl.pallas_call(pick_kernel, out_shape=[full_shape, half_shape, full_shape...  2.15 us
  transfers between devices with their start and end apart: 14, of which 6 were waited for; matrix products, arithmetic and copies ran while one was open for 3% of the time, Pallas kernels for 28%

profile of v6, /device:TPU:0, one launch (start us, length us, event | category | flops | bytes accessed | tf_op | source)
XLA Modules:
  0.0 103.0 jit_solution(353942352789572272)
XLA Ops:
  0.7 1.4 %slice_select_fusion.2._ = bf16[256,1152]{1,0:T(8,128)(2,1)S(1)} fusion(bf16[512,1152]{1,0:T(8,128)(2,1)} %image_ref.1, bf16[512,1152]{1,0:T(8,128)(2,1)} %text_ref.1, pred[]{:T(512)S(6)} %eq.8), kind=kLoop, calls=%fused_computation.2 | loop fusion | flops 294912 | bytes 1769473 | tf_op jit(solution)/shard_map/jit(_where)/select_n | solution.py:245
  2.1 3.1 %collective-permute-start = (bf16[256,1152]{1,0:T(8,128)(2,1)S(1)}, bf16[256,1152]{1,0:T(8,128)(2,1)}, u32[]{:S(2)}, u32[]{:S(2)}) collective-permute-start(bf16[256,1152]{1,0:T(8,128)(2,1)S(1)} %slice_select_fusion.2._), channel_id=1, source_target_pairs={{0,8},{31,23},{2,10},{29,21},{4,12},{27,19},{6,14},{25,17},{8,16},... | collective-permute-start | bytes 1769480 | tf_op jit(solution)/shard_map/ppermute | solution.py:19
  5.1 1.3 %copy-done.1 = bf16[512,1152]{1,0:T(8,128)(2,1)S(1)} copy-done((bf16[512,1152]{1,0:T(8,128)(2,1)S(1)}, bf16[512,1152]{1,0:T(8,128)(2,1)}, u32[]{:S(2)}) %copy-start.1) | copy-done | bytes 1179672
  6.4 2.1 %pick.1 = (bf16[512,1152]{1,0:T(8,128)(2,1)S(1)}, bf16[256,1152]{1,0:T(8,128)(2,1)}, bf16[512,1152]{1,0:T(8,128)(2,1)S(1)}) custom-call(bf16[512,1152]{1,0:T(8,128)(2,1)S(1)} %copy-done, bf16[512,1152]{1,0:T(8,128)(2,1)S(1)} %copy-done.1, bf16[256,1152]{1,0:T(8,128)(2,1)S(1)} %slice_select_fusion.2._), custom_call_target="tpu_custom_call" | custom-call | flops 1 | bytes 1 | tf_op jit(solution)/shard_map/pick/pallas_call | solution.py:246
  8.6 0.1 collective-permute-start.2
  8.7 4.5 %collective-permute-start.3 = (bf16[512,1152]{1,0:T(8,128)(2,1)S(1)}, bf16[512,1152]{1,0:T(8,128)(2,1)}, u32[]{:S(2)}, u32[]{:S(2)}) collective-permute-start(bf16[512,1152]{1,0:T(8,128)(2,1)S(1)} %get-tuple-element.18.own_ref.refs_0_), channel_id=1, source_target_pairs={{0,4},{31,27},{2,6},{29,25},{8,12},{23,19},{10,14},{21,17},{16,20}... | collective-permute-start | bytes 3538952 | tf_op jit(solution)/shard_map/ppermute | solution.py:19
  13.1 1.6 %collective-permute-start.5 = (bf16[256,1152]{1,0:T(8,128)(2,1)}, bf16[256,1152]{1,0:T(8,128)(2,1)}, u32[]{:S(2)}, u32[]{:S(2)}) collective-permute-start(bf16[256,1152]{1,0:T(8,128)(2,1)} %get-tuple-element.21), channel_id=1, source_target_pairs={{0,8},{31,23},{2,10},{29,21},{4,12},{27,19},{6,14},{25,17},{8,16},... | collective-permute-start | bytes 1769480 | tf_op jit(solution)/shard_map/ppermute | solution.py:19
  14.7 6.7 %collective-permute-done.refs_0_ = bf16[256,1152]{1,0:T(8,128)(2,1)} collective-permute-done((bf16[256,1152]{1,0:T(8,128)(2,1)S(1)}, bf16[256,1152]{1,0:T(8,128)(2,1)}, u32[]{:S(2)}, u32[]{:S(2)}) %collective-permute-start) | collective-permute-done | bytes 589856 | tf_op jit(solution)/shard_map/ppermute | solution.py:19
  21.4 1.3 %collective-permute-start.1 = (bf16[256,1152]{1,0:T(8,128)(2,1)}, bf16[256,1152]{1,0:T(8,128)(2,1)}, u32[]{:S(2)}, u32[]{:S(2)}) collective-permute-start(bf16[256,1152]{1,0:T(8,128)(2,1)} %collective-permute-done.refs_0_), channel_id=1, source_target_pairs={{2,10},{29,21},{6,14},{25,17},{10,18},{21,13},{14,22},{17,9},{18,2... | collective-permute-start | bytes 1769480 | tf_op jit(solution)/shard_map/ppermute | solution.py:19
  22.7 1.5 %collective-permute-start.4 = (bf16[256,1152]{1,0:T(8,128)(2,1)}, bf16[256,1152]{1,0:T(8,128)(2,1)}, u32[]{:S(2)}, u32[]{:S(2)}) collective-permute-start(bf16[256,1152]{1,0:T(8,128)(2,1)} %collective-permute-done.refs_0_), channel_id=1, source_target_pairs={{2,6},{29,25},{6,2},{25,29},{10,14},{21,17},{14,10},{17,21},{18,22... | collective-permute-start | bytes 1769480 | tf_op jit(solution)/shard_map/ppermute | solution.py:19
  26.3 0.9 copy.16.down_ref
  27.1 0.1 stack.43.scale_ref
  27.2 6.9 %collective-permute-done.5.refs_1_ = bf16[256,1152]{1,0:T(8,128)(2,1)} collective-permute-done((bf16[256,1152]{1,0:T(8,128)(2,1)}, bf16[256,1152]{1,0:T(8,128)(2,1)}, u32[]{:S(2)}, u32[]{:S(2)}) %collective-permute-start.5) | collective-permute-done | bytes 589856 | tf_op jit(solution)/shard_map/ppermute | solution.py:19
  34.1 1.3 %collective-permute-start.8 = (bf16[256,1152]{1,0:T(8,128)(2,1)}, bf16[256,1152]{1,0:T(8,128)(2,1)S(1)}, u32[]{:S(2)}, u32[]{:S(2)}) collective-permute-start(bf16[256,1152]{1,0:T(8,128)(2,1)} %collective-permute-done.5.refs_1_), channel_id=1, source_target_pairs={{2,10},{29,21},{6,14},{25,17},{10,18},{21,13},{14,22},{17,9},{18,2... | collective-permute-start | bytes 1769480 | tf_op jit(solution)/shard_map/ppermute | solution.py:19
  35.4 0.1 pad_add_fusion.flag_ref
  35.4 0.9 copy-done.2
  36.4 2.5 %own_block.1._ = f32[1024,1152]{1,0:T(8,128)S(1)} custom-call(s32[3]{0:T(128)S(1)} %pad_add_fusion.flag_ref, f32[5]{0:T(128)S(1)} %stack.43.scale_ref, s32[512,1]{1,0:T(8,128)S(1)} %copy-done.2, s32[1,512]{1,0:T(1,128)S(1)} %copy-done.3, bf16[512,1152]{1,0:T(8,128)(2,1)S(1)} %get-tuple-element.17.fixed_ref.rows_ref, ...), custom_call_target="tpu_custom_call" | custom-call | flops 1 | bytes 1 | tf_op jit(solution)/shard_map/own_block/pallas_call | solution.py:259
  38.9 0.4 collective-permute-done.1.refs_0_
  39.2 0.7 collective-permute-start.7
  39.9 0.0 collective-permute-done.3.refs_0_
  40.0 1.3 %blocks_1.1._ = f32[1024,1152]{1,0:T(8,128)S(1)} custom-call(s32[3]{0:T(128)S(1)} %pad_add_fusion.flag_ref, f32[5]{0:T(128)S(1)} %stack.43.scale_ref, f32[1024,1152]{1,0:T(8,128)S(1)} %own_block.1._, bf16[512,1152]{1,0:T(8,128)(2,1)S(1)} %get-tuple-element.17.fixed_ref.rows_ref, ...), custom_call_target="tpu_custom_call", output_to_operand_aliasing={{}: (2, {})} | custom-call | flops 1 | bytes 1 | tf_op jit(solution)/shard_map/blocks_1/pallas_call | solution.py:259
  41.3 0.0 collective-permute-done.4.refs_2_
  41.3 1.3 %slice_select_fusion = bf16[256,1152]{1,0:T(8,128)(2,1)S(1)} fusion(bf16[256,1152]{1,0:T(8,128)(2,1)} %collective-permute-done.1.refs_0_, bf16[512,1152]{1,0:T(8,128)(2,1)} %collective-permute-done.3.refs_0_, pred[]{:T(512)S(6)} %eq.9), kind=kLoop, calls=%fused_computation | loop fusion | flops 294912 | bytes 1769473 | tf_op jit(solution)/shard_map/jit(_where)/select_n | solution.py:294
  42.6 2.5 %collective-permute-start.6 = (bf16[256,1152]{1,0:T(8,128)(2,1)S(1)}, bf16[256,1152]{1,0:T(8,128)(2,1)S(1)}, u32[]{:S(2)}, u32[]{:S(2)}) collective-permute-start(bf16[256,1152]{1,0:T(8,128)(2,1)S(1)} %slice_select_fusion), channel_id=1, source_target_pairs={{0,8},{31,23},{4,12},{27,19},{8,16},{23,15},{12,20},{19,11},{16,24... | collective-permute-start | bytes 1769480 | tf_op jit(solution)/shard_map/ppermute | solution.py:19
  45.1 6.2 %blocks_2.1._ = f32[1024,1152]{1,0:T(8,128)S(1)} custom-call(s32[3]{0:T(128)S(1)} %pad_add_fusion.flag_ref, f32[5]{0:T(128)S(1)} %stack.43.scale_ref, f32[1024,1152]{1,0:T(8,128)S(1)} %blocks_1.1._, bf16[512,1152]{1,0:T(8,128)(2,1)S(1)} %get-tuple-element.17.fixed_ref.rows_ref, ...), custom_call_target="tpu_custom_call", output_to_operand_aliasing={{}: (2, {})} | custom-call | flops 1 | bytes 1 | tf_op jit(solution)/shard_map/blocks_2/pallas_call | solution.py:259
  51.3 0.0 collective-permute-done.8.refs_1_
  51.3 1.1 %slice_select_fusion.1 = bf16[256,1152]{1,0:T(8,128)(2,1)S(1)} fusion(bf16[256,1152]{1,0:T(8,128)(2,1)S(1)} %collective-permute-done.8.refs_1_, bf16[512,1152]{1,0:T(8,128)(2,1)} %collective-permute-done.3.refs_0_, pred[]{:T(512)S(6)} %eq.9), kind=kLoop, calls=%fused_computation.1 | loop fusion | flops 294912 | bytes 1769473 | tf_op jit(solution)/shard_map/jit(_where)/select_n | solution.py:305
  52.5 3.5 %collective-permute-start.9 = (bf16[256,1152]{1,0:T(8,128)(2,1)S(1)}, bf16[256,1152]{1,0:T(8,128)(2,1)S(1)}, u32[]{:S(2)}, u32[]{:S(2)}) collective-permute-start(bf16[256,1152]{1,0:T(8,128)(2,1)S(1)} %slice_select_fusion.1), channel_id=1, source_target_pairs={{0,8},{31,23},{4,12},{27,19},{8,16},{23,15},{12,20},{19,11},{16,24... | collective-permute-start | bytes 1769480 | tf_op jit(solution)/shard_map/ppermute | solution.py:19
  56.0 0.2 collective-permute-done.6.refs_2_
  56.2 0.0 collective-permute-done.7.refs_1_
  56.2 5.7 %blocks_3.1._ = f32[1024,1152]{1,0:T(8,128)S(1)} custom-call(s32[3]{0:T(128)S(1)} %pad_add_fusion.flag_ref, f32[5]{0:T(128)S(1)} %stack.43.scale_ref, f32[1024,1152]{1,0:T(8,128)S(1)} %blocks_2.1._, bf16[512,1152]{1,0:T(8,128)(2,1)S(1)} %get-tuple-element.17.fixed_ref.rows_ref, ...), custom_call_target="tpu_custom_call", output_to_operand_aliasing={{}: (2, {})} | custom-call | flops 1 | bytes 1 | tf_op jit(solution)/shard_map/blocks_3/pallas_call | solution.py:259
  61.9 4.5 %blocks_4.1.sum_ref = f32[1024,1152]{1,0:T(8,128)S(1)} custom-call(s32[3]{0:T(128)S(1)} %pad_add_fusion.flag_ref, f32[5]{0:T(128)S(1)} %stack.43.scale_ref, f32[1024,1152]{1,0:T(8,128)S(1)} %blocks_3.1._, bf16[512,1152]{1,0:T(8,128)(2,1)S(1)} %get-tuple-element.17.fixed_ref.rows_ref, ...), custom_call_target="tpu_custom_call", output_to_operand_aliasing={{}: (2, {})} | custom-call | flops 1 | bytes 1 | tf_op jit(solution)/shard_map/blocks_4/pallas_call | solution.py:259
  66.4 0.0 collective-permute-done.9.refs_0_
  66.4 1.5 %last_other_a.1 = bf16[256,1152]{1,0:T(8,128)(2,1)S(1)} custom-call(s32[3]{0:T(128)S(1)} %pad_add_fusion.flag_ref, f32[5]{0:T(128)S(1)} %stack.43.scale_ref, bf16[512,1152]{1,0:T(8,128)(2,1)S(1)} %collective-permute-done.2.other_ref.rows_ref, f32[1024,1152]{1,0:T(8,128)S(1)} %blocks_4.1.sum_ref, bf16[256,1152]{1,0:T(8,128)(2,1)S(1)} %collective-permute-done.9.refs_0_), custom_call_target="tpu_custom_call" | custom-call | flops 1 | bytes 1 | tf_op jit(solution)/shard_map/last_other_a/pallas_call | solution.py:321
  67.9 0.1 collective-permute-start.12
  67.9 1.5 %last_other_b.1 = bf16[256,1152]{1,0:T(8,128)(2,1)S(1)} custom-call(s32[3]{0:T(128)S(1)} %pad_add_fusion.flag_ref, f32[5]{0:T(128)S(1)} %stack.43.scale_ref, bf16[512,1152]{1,0:T(8,128)(2,1)S(1)} %collective-permute-done.2.other_ref.rows_ref, f32[1024,1152]{1,0:T(8,128)S(1)} %blocks_4.1.sum_ref, bf16[256,1152]{1,0:T(8,128)(2,1)S(1)} %collective-permute-done.9.refs_0_), custom_call_target="tpu_custom_call" | custom-call | flops 1 | bytes 1 | tf_op jit(solution)/shard_map/last_other_b/pallas_call | solution.py:321
  69.4 0.6 collective-permute-start.10
  70.0 0.0 collective-permute-done.12.refs_1_
  70.0 1.5 %last_own_a.1.refs_0_ = bf16[256,1152]{1,0:T(8,128)(2,1)S(1)} custom-call(s32[3]{0:T(128)S(1)} %pad_add_fusion.flag_ref, f32[5]{0:T(128)S(1)} %stack.43.scale_ref, bf16[512,1152]{1,0:T(8,128)(2,1)S(1)} %get-tuple-element.17.fixed_ref.rows_ref, f32[1024,1152]{1,0:T(8,128)S(1)} %blocks_4.1.sum_ref, bf16[256,1152]{1,0:T(8,128)(2,1)S(1)} %collective-permute-done.9.refs_0_, ...), custom_call_target="tpu_custom_call" | custom-call | flops 1 | bytes 1 | tf_op jit(solution)/shard_map/last_own_a/pallas_call | solution.py:321
  71.5 4.1 %collective-permute-start.13 = (bf16[256,1152]{1,0:T(8,128)(2,1)S(1)}, bf16[256,1152]{1,0:T(8,128)(2,1)S(1)}, u32[]{:S(2)}, u32[]{:S(2)}) collective-permute-start(bf16[256,1152]{1,0:T(8,128)(2,1)S(1)} %last_own_a.1.refs_0_), channel_id=1, source_target_pairs={{0,1},{1,0},{2,3},{3,2},{4,5},{5,4},{6,7},{7,6},{8,9},{9,8},{10,11... | collective-permute-start | bytes 1769480 | tf_op jit(solution)/shard_map/ppermute | solution.py:19
  75.6 0.0 collective-permute-done.10.refs_1_
  75.6 1.5 %last_own_b.1.refs_1_ = bf16[256,1152]{1,0:T(8,128)(2,1)S(1)} custom-call(s32[3]{0:T(128)S(1)} %pad_add_fusion.flag_ref, f32[5]{0:T(128)S(1)} %stack.43.scale_ref, bf16[512,1152]{1,0:T(8,128)(2,1)S(1)} %get-tuple-element.17.fixed_ref.rows_ref, f32[1024,1152]{1,0:T(8,128)S(1)} %blocks_4.1.sum_ref, bf16[256,1152]{1,0:T(8,128)(2,1)S(1)} %collective-permute-done.9.refs_0_, ...), custom_call_target="tpu_custom_call" | custom-call | flops 1 | bytes 1 | tf_op jit(solution)/shard_map/last_own_b/pallas_call | solution.py:321
  77.1 0.2 collective-permute-start.11
  77.2 1.5 %write_mine.1 = (f32[512,1152]{1,0:T(8,128)}, f32[512,1152]{1,0:T(8,128)}) custom-call(bf16[256,1152]{1,0:T(8,128)(2,1)S(1)} %last_own_a.1.refs_0_, bf16[256,1152]{1,0:T(8,128)(2,1)S(1)} %last_own_b.1.refs_1_), custom_call_target="tpu_custom_call" | custom-call | flops 1 | bytes 1 | tf_op jit(solution)/shard_map/write_mine/pallas_call | solution.py:353
  78.7 11.0 %collective-permute-done.13.refs_0_ = bf16[256,1152]{1,0:T(8,128)(2,1)S(1)} collective-permute-done((bf16[256,1152]{1,0:T(8,128)(2,1)S(1)}, bf16[256,1152]{1,0:T(8,128)(2,1)S(1)}, u32[]{:S(2)}, u32[]{:S(2)}) %collective-permute-start.13) | collective-permute-done | bytes 589856 | tf_op jit(solution)/shard_map/ppermute | solution.py:19
  89.7 1.1 %write_theirs_a.1 = (f32[512,1152]{1,0:T(8,128)}, f32[512,1152]{1,0:T(8,128)}) custom-call(bf16[256,1152]{1,0:T(8,128)(2,1)S(1)} %collective-permute-done.13.refs_0_, f32[512,1152]{1,0:T(8,128)} %get-tuple-element.26.refs_1_, f32[512,1152]{1,0:T(8,128)} %get-tuple-element.27.refs_2_), custom_call_target="tpu_custom_call", output_to_operand_aliasing={{0}: (1, {}), {1}: (2, {})} | custom-call | flops 1 | bytes 1 | tf_op jit(solution)/shard_map/write_theirs_a/pallas_call | solution.py:353
  90.8 11.0 %collective-permute-done.11.refs_0_ = bf16[256,1152]{1,0:T(8,128)(2,1)S(1)} collective-permute-done((bf16[256,1152]{1,0:T(8,128)(2,1)S(1)}, bf16[256,1152]{1,0:T(8,128)(2,1)S(1)}, u32[]{:S(2)}, u32[]{:S(2)}) %collective-permute-start.11) | collective-permute-done | bytes 589856 | tf_op jit(solution)/shard_map/ppermute | solution.py:19
  101.8 1.1 %write_theirs_b.1 = (f32[512,1152]{1,0:T(8,128)}, f32[512,1152]{1,0:T(8,128)}) custom-call(bf16[256,1152]{1,0:T(8,128)(2,1)S(1)} %collective-permute-done.11.refs_0_, f32[512,1152]{1,0:T(8,128)} %get-tuple-element.28.refs_1_, f32[512,1152]{1,0:T(8,128)} %get-tuple-element.29.refs_2_), custom_call_target="tpu_custom_call", output_to_operand_aliasing={{0}: (1, {}), {1}: (2, {})} | custom-call | flops 1 | bytes 1 | tf_op jit(solution)/shard_map/write_theirs_b/pallas_call | solution.py:353
  (7 shorter events, 0.0 us)
Async XLA Ops:
  0.6 4.5 %copy-start = (bf16[512,1152]{1,0:T(8,128)(2,1)S(1)}, bf16[512,1152]{1,0:T(8,128)(2,1)}, u32[]{:S(2)}) copy-start(bf16[512,1152]{1,0:T(8,128)(2,1)} %image_ref.1) | copy-start | bytes 3538948
  0.6 25.6 %copy-start.3 = (s32[1,512]{1,0:T(1,128)S(1)}, s32[1,512]{1,0:T(1,128)}, u32[]{:S(2)}) copy-start(s32[1,512]{1,0:T(1,128)} %along_ref.1) | copy-start | bytes 6148
  2.1 19.4 %collective-permute-start = (bf16[256,1152]{1,0:T(8,128)(2,1)S(1)}, bf16[256,1152]{1,0:T(8,128)(2,1)}, u32[]{:S(2)}, u32[]{:S(2)}) collective-permute-start(bf16[256,1152]{1,0:T(8,128)(2,1)S(1)} %slice_select_fusion.2._), channel_id=1, source_target_pairs={{0,8},{31,23},{2,10},{29,21},{4,12},{27,19},{6,14},{25,17},{8,16},... | collective-permute-start | bytes 1769480 | tf_op jit(solution)/shard_map/ppermute | solution.py:19
  5.1 1.3 %copy-start.1 = (bf16[512,1152]{1,0:T(8,128)(2,1)S(1)}, bf16[512,1152]{1,0:T(8,128)(2,1)}, u32[]{:S(2)}) copy-start(bf16[512,1152]{1,0:T(8,128)(2,1)} %text_ref.1) | copy-start | bytes 3538948
  8.6 31.4 %collective-permute-start.2 = (bf16[512,1152]{1,0:T(8,128)(2,1)S(1)}, bf16[512,1152]{1,0:T(8,128)(2,1)S(1)}, u32[]{:S(2)}, u32[]{:S(2)}) collective-permute-start(bf16[512,1152]{1,0:T(8,128)(2,1)S(1)} %get-tuple-element.17.fixed_ref.rows_ref), channel_id=1, source_target_pairs={{0,2},{31,29},{2,0},{29,31},{4,6},{27,25},{6,4},{25,27},{8,10},{23... | collective-permute-start | bytes 3538952 | tf_op jit(solution)/shard_map/ppermute | solution.py:19
  8.7 31.3 %collective-permute-start.3 = (bf16[512,1152]{1,0:T(8,128)(2,1)S(1)}, bf16[512,1152]{1,0:T(8,128)(2,1)}, u32[]{:S(2)}, u32[]{:S(2)}) collective-permute-start(bf16[512,1152]{1,0:T(8,128)(2,1)S(1)} %get-tuple-element.18.own_ref.refs_0_), channel_id=1, source_target_pairs={{0,4},{31,27},{2,6},{29,25},{8,12},{23,19},{10,14},{21,17},{16,20}... | collective-permute-start | bytes 3538952 | tf_op jit(solution)/shard_map/ppermute | solution.py:19
  13.1 20.9 %collective-permute-start.5 = (bf16[256,1152]{1,0:T(8,128)(2,1)}, bf16[256,1152]{1,0:T(8,128)(2,1)}, u32[]{:S(2)}, u32[]{:S(2)}) collective-permute-start(bf16[256,1152]{1,0:T(8,128)(2,1)} %get-tuple-element.21), channel_id=1, source_target_pairs={{0,8},{31,23},{2,10},{29,21},{4,12},{27,19},{6,14},{25,17},{8,16},... | collective-permute-start | bytes 1769480 | tf_op jit(solution)/shard_map/ppermute | solution.py:19
  21.4 17.8 %collective-permute-start.1 = (bf16[256,1152]{1,0:T(8,128)(2,1)}, bf16[256,1152]{1,0:T(8,128)(2,1)}, u32[]{:S(2)}, u32[]{:S(2)}) collective-permute-start(bf16[256,1152]{1,0:T(8,128)(2,1)} %collective-permute-done.refs_0_), channel_id=1, source_target_pairs={{2,10},{29,21},{6,14},{25,17},{10,18},{21,13},{14,22},{17,9},{18,2... | collective-permute-start | bytes 1769480 | tf_op jit(solution)/shard_map/ppermute | solution.py:19
  22.7 18.5 %collective-permute-start.4 = (bf16[256,1152]{1,0:T(8,128)(2,1)}, bf16[256,1152]{1,0:T(8,128)(2,1)}, u32[]{:S(2)}, u32[]{:S(2)}) collective-permute-start(bf16[256,1152]{1,0:T(8,128)(2,1)} %collective-permute-done.refs_0_), channel_id=1, source_target_pairs={{2,6},{29,25},{6,2},{25,29},{10,14},{21,17},{14,10},{17,21},{18,22... | collective-permute-start | bytes 1769480 | tf_op jit(solution)/shard_map/ppermute | solution.py:19
  34.1 17.2 %collective-permute-start.8 = (bf16[256,1152]{1,0:T(8,128)(2,1)}, bf16[256,1152]{1,0:T(8,128)(2,1)S(1)}, u32[]{:S(2)}, u32[]{:S(2)}) collective-permute-start(bf16[256,1152]{1,0:T(8,128)(2,1)} %collective-permute-done.5.refs_1_), channel_id=1, source_target_pairs={{2,10},{29,21},{6,14},{25,17},{10,18},{21,13},{14,22},{17,9},{18,2... | collective-permute-start | bytes 1769480 | tf_op jit(solution)/shard_map/ppermute | solution.py:19
  35.4 1.0 copy-start.2
  39.2 16.9 %collective-permute-start.7 = (bf16[256,1152]{1,0:T(8,128)(2,1)}, bf16[256,1152]{1,0:T(8,128)(2,1)S(1)}, u32[]{:S(2)}, u32[]{:S(2)}) collective-permute-start(bf16[256,1152]{1,0:T(8,128)(2,1)} %collective-permute-done.5.refs_1_), channel_id=1, source_target_pairs={{2,6},{29,25},{6,2},{25,29},{10,14},{21,17},{14,10},{17,21},{18,22... | collective-permute-start | bytes 1769480 | tf_op jit(solution)/shard_map/ppermute | solution.py:19
  42.6 13.6 %collective-permute-start.6 = (bf16[256,1152]{1,0:T(8,128)(2,1)S(1)}, bf16[256,1152]{1,0:T(8,128)(2,1)S(1)}, u32[]{:S(2)}, u32[]{:S(2)}) collective-permute-start(bf16[256,1152]{1,0:T(8,128)(2,1)S(1)} %slice_select_fusion), channel_id=1, source_target_pairs={{0,8},{31,23},{4,12},{27,19},{8,16},{23,15},{12,20},{19,11},{16,24... | collective-permute-start | bytes 1769480 | tf_op jit(solution)/shard_map/ppermute | solution.py:19
  52.5 13.9 %collective-permute-start.9 = (bf16[256,1152]{1,0:T(8,128)(2,1)S(1)}, bf16[256,1152]{1,0:T(8,128)(2,1)S(1)}, u32[]{:S(2)}, u32[]{:S(2)}) collective-permute-start(bf16[256,1152]{1,0:T(8,128)(2,1)S(1)} %slice_select_fusion.1), channel_id=1, source_target_pairs={{0,8},{31,23},{4,12},{27,19},{8,16},{23,15},{12,20},{19,11},{16,24... | collective-permute-start | bytes 1769480 | tf_op jit(solution)/shard_map/ppermute | solution.py:19
  67.9 2.1 %collective-permute-start.12 = (bf16[256,1152]{1,0:T(8,128)(2,1)S(1)}, bf16[256,1152]{1,0:T(8,128)(2,1)S(1)}, u32[]{:S(2)}, u32[]{:S(2)}) collective-permute-start(bf16[256,1152]{1,0:T(8,128)(2,1)S(1)} %last_other_a.1), channel_id=1, source_target_pairs={{0,2},{31,29},{2,0},{29,31},{4,6},{27,25},{6,4},{25,27},{8,10},{23... | collective-permute-start | bytes 1769480 | tf_op jit(solution)/shard_map/ppermute | solution.py:19
  69.4 6.2 %collective-permute-start.10 = (bf16[256,1152]{1,0:T(8,128)(2,1)S(1)}, bf16[256,1152]{1,0:T(8,128)(2,1)S(1)}, u32[]{:S(2)}, u32[]{:S(2)}) collective-permute-start(bf16[256,1152]{1,0:T(8,128)(2,1)S(1)} %last_other_b.1), channel_id=1, source_target_pairs={{0,2},{31,29},{2,0},{29,31},{4,6},{27,25},{6,4},{25,27},{8,10},{23... | collective-permute-start | bytes 1769480 | tf_op jit(solution)/shard_map/ppermute | solution.py:19
  71.5 18.2 %collective-permute-start.13 = (bf16[256,1152]{1,0:T(8,128)(2,1)S(1)}, bf16[256,1152]{1,0:T(8,128)(2,1)S(1)}, u32[]{:S(2)}, u32[]{:S(2)}) collective-permute-start(bf16[256,1152]{1,0:T(8,128)(2,1)S(1)} %last_own_a.1.refs_0_), channel_id=1, source_target_pairs={{0,1},{1,0},{2,3},{3,2},{4,5},{5,4},{6,7},{7,6},{8,9},{9,8},{10,11... | collective-permute-start | bytes 1769480 | tf_op jit(solution)/shard_map/ppermute | solution.py:19
  77.1 24.7 %collective-permute-start.11 = (bf16[256,1152]{1,0:T(8,128)(2,1)S(1)}, bf16[256,1152]{1,0:T(8,128)(2,1)S(1)}, u32[]{:S(2)}, u32[]{:S(2)}) collective-permute-start(bf16[256,1152]{1,0:T(8,128)(2,1)S(1)} %last_own_b.1.refs_1_), channel_id=1, source_target_pairs={{0,1},{1,0},{2,3},{3,2},{4,5},{5,4},{6,7},{7,6},{8,9},{9,8},{10,11... | collective-permute-start | bytes 1769480 | tf_op jit(solution)/shard_map/ppermute | solution.py:19
